TPU v7x, 32 devices: a whole 2x2x4 slice. The times are simulated.
32 devices in a mesh: px: 8 (over y, x, core), py: 4 (over z).
Axes of the slice: x: 2, y: 2, z: 4, core: 2. Of those that a mesh axis runs over, the one named last changes fastest.
Arguments:
- currents_in: bfloat16 [16, 8, 2, 32, 512], P('px', 'py'), may hold values from -6 to 6
- rad_pattern: bfloat16 [2, 512, 512], replicated, may hold values from -0.1875 to 0.1875
- far_map: bfloat16 [512, 2048], replicated, may hold values from -0.25 to 0.25
- reflect: float32 [16, 8, 512], P('px', 'py'), may hold values from 0.2 to 0.7
- centres: float32 [3, 16, 8], P(None, 'px', 'py'), may hold values from -30 to 30
- spectral_dirs: float32 [3, 512], replicated, may hold values from -3 to 3
- receiver_dirs: float32 [3, 2048], replicated, may hold values from -3 to 3
- partners: int32 [16, 8, 12], P('px', 'py'), may hold values from 0 to 127, as said below
- partner_count: int32 [16, 8], P('px', 'py'), may hold values from 1 to 12, as said below
- pair_weight: bfloat16 [16, 8, 12], P('px', 'py'), may hold values from 0.29882812 to 1
Outputs:
- currents: bfloat16 [16, 8, 2, 32, 512], P('px', 'py')
- isar_image: float32 [32, 2048], P('py', 'px')
Inputs may be any that keep to these rules, and one draw needn't show every extreme that they name: `partners`: the first partner_count entries of a patch's list are distinct patches other than itself, at most 1 patch rows away along the hull and, counting columns around the girth (column indices wrap modulo 8), at most 2 columns away; later entries are valid patch ids that are ignored. `partner_count`: some patch lists 12 partners.
All inputs are finite; a program needn't handle non-finite values.
Results may differ from a plain program's by a relative error of at most 0.019.
Values may be sent and summed in bfloat16 or wider, within the bound.
No kernel may reach another device: no remote copies, remote signals or barrier semaphores. Data moves between devices by JAX's collectives and lax.ppermute only.
A program may use at most 64 MiB of HBM per device.

v0:
```python
import functools
import math

import jax
import jax.numpy as jnp
import numpy as np
from jax import lax
from jax.experimental import pallas as pl
from jax.experimental.pallas import tpu as pltpu
from jax.sharding import PartitionSpec as P

SLOTS = 12
ROW_REACH = 1
COL_REACH = 2
OFFSETS = [
    (a, b)
    for a in range(-ROW_REACH, ROW_REACH + 1)
    for b in range(-COL_REACH, COL_REACH + 1)
]
F32 = jnp.float32
BF16 = jnp.bfloat16
HIGH = lax.Precision.HIGHEST
VMEM_LIMIT = 48 * 1024 * 1024


def padded(block, sides, width, periodic):
    for axis, dim in sides:
        count = lax.axis_size(axis)
        forward = [(i, i + 1) for i in range(count - 1)]
        if periodic:
            forward.append((count - 1, 0))
        backward = [(target, source) for source, target in forward]
        low = lax.ppermute(
            lax.slice_in_dim(block, block.shape[dim] - width, None, axis=dim), axis, forward
        )
        high = lax.ppermute(lax.slice_in_dim(block, 0, width, axis=dim), axis, backward)
        block = jnp.concatenate([low, block, high], axis=dim)
    return block


def combined(rad_pattern):
    upper = jnp.concatenate([rad_pattern[0], rad_pattern[1]], axis=1)
    lower = jnp.concatenate([-rad_pattern[1], rad_pattern[0]], axis=1)
    return jnp.concatenate([upper, lower], axis=0)


def radiate(currents, rad_big):
    row_count, col_count, _, illum_count, unit_count = currents.shape
    stacked = jnp.concatenate([currents[:, :, 0], currents[:, :, 1]], axis=-1)
    flat_rows = stacked.reshape(row_count * col_count * illum_count, 2 * unit_count)
    spectra = jnp.dot(flat_rows, rad_big, preferred_element_type=F32)
    return spectra.reshape(row_count, col_count, illum_count, -1)


def receive(arriving, rad_big):
    row_count, col_count, illum_count, double = arriving.shape
    flat_rows = arriving.reshape(-1, double)
    answer = lax.dot_general(
        flat_rows, rad_big, (((1,), (1,)), ((), ())), preferred_element_type=F32
    )
    return answer.reshape(row_count, col_count, illum_count, -1)


def partner_sum(halo_flat, slot_index, weights):
    height = halo_flat.shape[0]
    onehot = slot_index[:, :, None] == jnp.arange(height, dtype=jnp.int32)[None, None, :]
    coef = jnp.sum(jnp.where(onehot, weights[:, :, None].astype(F32), 0.0), axis=1).astype(BF16)
    return jnp.dot(coef, halo_flat, preferred_element_type=F32)


def bounce(current_now, currents_in, rad_big, reflect, cosine, sine_part, plan):
    row_count, col_count, _, illum_count, unit_count = current_now.shape
    spectra = radiate(current_now, rad_big)
    half_width = spectra.shape[-1] // 2
    spec_re = spectra[..., :half_width]
    spec_im = spectra[..., half_width:]
    out_re = spec_re * cosine + spec_im * sine_part
    out_im = spec_im * cosine - spec_re * sine_part
    outgoing = jnp.stack([out_re, out_im], axis=2).astype(BF16)
    girth_block = padded(outgoing, (("py", 1),), COL_REACH, True)
    slot_index, weights = plan
    rim_block = padded(girth_block, (("px", 0),), ROW_REACH, False)
    halo_flat = rim_block.reshape(-1, 2 * illum_count * half_width)
    collected = partner_sum(halo_flat, slot_index, weights)
    collected = collected.reshape(row_count, col_count, 2, illum_count, half_width)
    col_re = collected[:, :, 0]
    col_im = collected[:, :, 1]
    arr_re = col_re * cosine - col_im * sine_part
    arr_im = col_re * sine_part + col_im * cosine
    arriving = jnp.concatenate([arr_re, -arr_im], axis=-1).astype(BF16)
    answer = receive(arriving, rad_big)
    received = jnp.stack([answer[..., :unit_count], -answer[..., unit_count:]], axis=2)
    updated = currents_in.astype(F32) + reflect[:, :, None, None, :] * received
    return updated.astype(BF16)


def patch_sharded(
    currents_in,
    rad_pattern,
    far_map,
    reflect,
    centres,
    spectral_dirs,
    receiver_dirs,
    partners,
    partner_count,
    pair_weight,
):
    row_count, col_count = partner_count.shape
    high = HIGH
    rad_big = combined(rad_pattern)
    phi = jnp.einsum("dm,dab->abm", spectral_dirs, centres, precision=high)
    cosine = jnp.cos(phi)[:, :, None, :]
    sine_part = jnp.sin(phi)[:, :, None, :]
    total_cols = col_count * lax.axis_size("py")
    total_rows = row_count * lax.axis_size("px")
    base_row = lax.axis_index("px") * row_count
    base_col = lax.axis_index("py") * col_count
    across = col_count + 2 * COL_REACH
    local_col = jnp.arange(col_count, dtype=jnp.int32)[None, :, None]
    live = jnp.arange(SLOTS, dtype=jnp.int32)[None, None, :] < partner_count[:, :, None]
    masked_weight = jnp.where(live, pair_weight, jnp.zeros_like(pair_weight))
    part_row = partners // total_cols
    part_col = partners % total_cols
    near_row = part_row - base_row
    near_col = (part_col - base_col - local_col + COL_REACH) % total_cols + local_col
    slot_index = ((near_row + ROW_REACH) * across + near_col).reshape(row_count * col_count, SLOTS)
    weights = masked_weight.reshape(row_count * col_count, SLOTS)
    plan = (slot_index, weights)
    current_now = currents_in
    for bounce_id in range(2):
        current_now = bounce(current_now, currents_in, rad_big, reflect, cosine, sine_part, plan)
    spectra = radiate(current_now, rad_big).astype(BF16)
    illum_count = spectra.shape[2]
    dir_count = far_map.shape[0]
    rcv_count = far_map.shape[1]
    beams = jnp.dot(spectra.reshape(-1, dir_count), far_map, preferred_element_type=F32)
    beams = beams.reshape(row_count, col_count, illum_count, 2, rcv_count)
    view = jnp.einsum("dr,dab->abr", receiver_dirs, centres, precision=high)
    cos_view = jnp.cos(view)[:, :, None, :]
    sin_view = jnp.sin(view)[:, :, None, :]
    beam_re = beams[:, :, :, 0]
    beam_im = beams[:, :, :, 1]
    far_re = jnp.sum(beam_re * cos_view - beam_im * sin_view, axis=(0, 1))
    far_im = jnp.sum(beam_re * sin_view + beam_im * cos_view, axis=(0, 1))
    factor = 1.0 / math.sqrt(total_rows * total_cols)
    far_part = jnp.stack([far_re, far_im]) * factor
    owned_far = lax.psum(
        lax.psum_scatter(far_part.astype(BF16), "py", scatter_dimension=1, tiled=True), "px"
    ).astype(F32)
    bin_width = rcv_count // lax.axis_size("px")
    rcv_ids = jnp.arange(rcv_count, dtype=jnp.int32)[:, None]
    bin_ids = lax.axis_index("px") * bin_width + jnp.arange(bin_width, dtype=jnp.int32)[None, :]
    turn_angle = (rcv_ids * bin_ids % rcv_count).astype(F32) * (2.0 * math.pi / rcv_count)
    norm_factor = 1.0 / math.sqrt(rcv_count)
    cos_table = jnp.cos(turn_angle) * norm_factor
    sin_table = jnp.sin(turn_angle) * norm_factor
    image_re = jnp.dot(owned_far[0], cos_table, precision=high) + jnp.dot(
        owned_far[1], sin_table, precision=high
    )
    image_im = jnp.dot(owned_far[1], cos_table, precision=high) - jnp.dot(
        owned_far[0], sin_table, precision=high
    )
    isar_image = 0.125 * (image_re * image_re + image_im * image_im)
    return (current_now, isar_image)


def turn_polynomials():
    grid = np.linspace(0.0, 0.25, 4001)
    safe = np.where(grid > 0, np.sqrt(grid), 1.0)
    sine_over = np.where(grid > 0, np.sin(2 * np.pi * safe) / safe, 2 * np.pi)
    cosine = np.cos(2 * np.pi * np.sqrt(grid))
    make = np.polynomial.chebyshev.Chebyshev.fit
    power = np.polynomial.Polynomial
    sine_fit = make(grid, sine_over, 6).convert(kind=power).coef
    cosine_fit = make(grid, cosine, 7).convert(kind=power).coef
    return [float(c) for c in sine_fit], [float(c) for c in cosine_fit]


SINE_FIT, COSINE_FIT = turn_polynomials()


def horner(coefs, x):
    value = jnp.full_like(x, coefs[-1])
    for c in coefs[-2::-1]:
        value = value * x + c
    return value


def cos_sin(turns):
    frac = turns - jnp.floor(turns + 0.5)
    square = frac * frac
    return horner(COSINE_FIT, square), frac * horner(SINE_FIT, square)


def dot(left, right):
    return jnp.dot(left, right, preferred_element_type=F32)


def dot_t(left, right):
    return lax.dot_general(left, right, (((1,), (1,)), ((), ())), preferred_element_type=F32)


def one_hot_rows(sources):
    table = np.zeros((len(sources), len(sources)), np.float32)
    table[np.arange(len(sources)), sources] = 1.0
    return table


def pack_kernel(
    rows, total_cols, base, cur, order, reflect, weight, partners, count, centres, out
):
    local_rows, local_cols, unit_count = reflect.shape
    local = local_rows * local_cols
    half = unit_count // 2
    width = unit_count + half
    out[:, :unit_count] = dot(order[...], cur[...]).astype(BF16)
    refl = reflect[...].reshape(local, unit_count)
    refl = jnp.concatenate([refl[:, :half], refl[:, half:]], axis=0)
    lane = lax.broadcasted_iota(jnp.int32, (local, 128), 1)
    row = lax.broadcasted_iota(jnp.int32, (local, 128), 0)
    patch_row = base[0] + row // local_cols
    patch_col = base[1] + row % local_cols
    target = jnp.full((local, 128), -1, jnp.int32)
    for o, (a, b) in enumerate(OFFSETS):
        col = patch_col + b
        col = jnp.where(col < 0, col + total_cols, col)
        col = jnp.where(col >= total_cols, col - total_cols, col)
        target = jnp.where(lane == o, (patch_row + a) * total_cols + col, target)
    small = jnp.zeros((local, 128), F32)
    for r in range(local_rows):
        for c in range(local_cols):
            here = row == r * local_cols + c
            for s in range(SLOTS):
                w = jnp.where(s < count[r, c], weight[r, c, s], 0.0)
                small = small + jnp.where(here & (target == partners[r, c, s]), w, 0.0)
    spot = jnp.zeros((local, 128), F32)
    first = len(OFFSETS)
    for d in range(3):
        in_place = (lane >= first + 3 * d) & (lane < first + 3 * d + 3)
        for r in range(local_rows):
            for c in range(local_cols):
                here = row == r * local_cols + c
                spot = jnp.where(in_place & here, centres[d, r, c], spot)
    top = spot.astype(BF16).astype(F32)
    rest = spot - top
    middle = rest.astype(BF16).astype(F32)
    bottom = rest - middle
    term = lane - first
    term = term - jnp.where(term >= 6, 6, jnp.where(term >= 3, 3, 0))
    parts = jnp.where(term == 0, top, jnp.where(term == 1, middle, bottom))
    small = jnp.where((lane >= first) & (lane < first + 9), parts, small)
    small = jnp.concatenate([small, jnp.zeros_like(small)], axis=0)
    tail = jnp.concatenate([refl, small], axis=1)
    tail = jnp.concatenate([tail, tail], axis=0).astype(BF16)
    step = tail.shape[0]
    for s in range(rows // step):
        out[step * s : step * (s + 1), unit_count:] = tail


def main_kernel(
    scale,
    splits,
    got,
    order,
    back,
    offset_of,
    spectral_dirs,
    receiver_dirs,
    short_cos,
    short_sin,
    twist_cos,
    twist_sin,
    long_table,
    rad_hbm,
    far_hbm,
    out,
    rad,
    far_map,
    rad_sem,
    far_sem,
):
    rad_copy = pltpu.make_async_copy(rad_hbm, rad, rad_sem)
    far_copy = pltpu.make_async_copy(far_hbm, far_map, far_sem)
    rad_copy.start()
    far_copy.start()
    unit_count = rad.shape[1]
    half = unit_count // 2
    patches = got.shape[0] // 2
    sorted_rows = dot(order[...], got[...])
    start = sorted_rows[:, :unit_count]
    reflect = jnp.concatenate(
        [
            sorted_rows[:patches, unit_count : unit_count + half],
            sorted_rows[patches:, unit_count : unit_count + half],
        ],
        axis=1,
    )
    small = sorted_rows[:patches, unit_count + half :]
    first = len(OFFSETS)
    centre = []
    for d in range(3):
        at = first + 3 * d
        value = small[:, at : at + 1] + small[:, at + 1 : at + 2] + small[:, at + 2 : at + 3]
        centre.append(value * (0.5 / math.pi))

    def turns(dirs):
        return centre[0] * dirs[0:1] + centre[1] * dirs[1:2] + centre[2] * dirs[2:3]

    coef = jnp.zeros((patches, patches), F32)
    offsets = offset_of[...]
    for o in range(len(OFFSETS)):
        coef = coef + jnp.where(offsets == o, small[:, o : o + 1], 0.0)
    coef = coef.astype(BF16)
    cosine, sine = cos_sin(turns(spectral_dirs[...]))
    rad_copy.wait()

    def spectrum(current):
        first_part = dot(current, rad[0])
        second_part = dot(current, rad[1])
        return (
            first_part[:patches] - second_part[patches:],
            second_part[:patches] + first_part[patches:],
        )

    current = start.astype(BF16)
    for _ in range(2):
        spec_re, spec_im = spectrum(current)
        outgoing = jnp.concatenate(
            [spec_re * cosine + spec_im * sine, spec_im * cosine - spec_re * sine], axis=1
        ).astype(BF16)
        collected = dot(coef, outgoing)
        width = collected.shape[1] // 2
        col_re = collected[:, :width]
        col_im = collected[:, width:]
        arriving = jnp.concatenate(
            [col_re * cosine - col_im * sine, col_re * sine + col_im * cosine], axis=0
        ).astype(BF16)
        first_part = dot_t(arriving, rad[0])
        second_part = dot_t(arriving, rad[1])
        recv_re = first_part[:patches] - second_part[patches:]
        recv_im = second_part[:patches] + first_part[patches:]
        current = jnp.concatenate(
            [start[:patches] + reflect * recv_re, start[patches:] + reflect * recv_im], axis=0
        ).astype(BF16)
    out[:, :unit_count] = dot(back[...], current).astype(BF16)

    spec_re, spec_im = spectrum(current)
    final = jnp.concatenate([spec_re, spec_im], axis=0).astype(BF16)
    far_copy.wait()
    tile = far_map.shape[1] // splits
    far_re, far_im = [], []
    for t in range(splits):
        beams = dot(final, far_map[:, tile * t : tile * (t + 1)])
        cos_view, sin_view = cos_sin(turns(receiver_dirs[:, tile * t : tile * (t + 1)]))
        beam_re = beams[:patches]
        beam_im = beams[patches:]
        far_re.append(jnp.sum(beam_re * cos_view - beam_im * sin_view, axis=0, keepdims=True))
        far_im.append(jnp.sum(beam_re * sin_view + beam_im * cos_view, axis=0, keepdims=True))
    mid_re = jnp.zeros((splits, tile), F32)
    mid_im = jnp.zeros((splits, tile), F32)
    for t in range(splits):
        c = short_cos[:, t : t + 1]
        s = short_sin[:, t : t + 1]
        mid_re = mid_re + (c * far_re[t] + s * far_im[t])
        mid_im = mid_im + (c * far_im[t] - s * far_re[t])
    tw_re = mid_re * twist_cos[...] + mid_im * twist_sin[...]
    tw_im = mid_im * twist_cos[...] - mid_re * twist_sin[...]
    both = jnp.concatenate([tw_re, tw_im], axis=0)
    answer = jnp.dot(both, long_table[...], precision=HIGH, preferred_element_type=F32)
    image_re = answer[:splits, :tile] + answer[splits:, tile:]
    image_im = answer[splits:, :tile] - answer[:splits, tile:]
    image = (scale * (image_re * image_re + image_im * image_im)).astype(BF16)
    pieces = tile // 128
    rows_each = out.shape[0] // pieces
    for p in range(pieces):
        piece = image[:, 128 * p : 128 * (p + 1)].astype(F32)
        piece = jnp.concatenate([piece, piece], axis=0).astype(BF16)
        for s in range(rows_each // piece.shape[0]):
            at = p * rows_each + s * piece.shape[0]
            out[at : at + piece.shape[0], unit_count:] = piece


def unpack_kernel(per_row, place, got, order, currents, image):
    unit_count = currents.shape[1]
    currents[...] = dot(order[...], got[:, :unit_count]).astype(BF16)
    splits = 8
    owned, bins = image.shape
    height = owned * splits
    at = pl.multiple_of(place[1] * height, height)
    block = got[pl.ds(at, height), unit_count:]
    each = bins // splits
    lane = lax.broadcasted_iota(jnp.int32, (128, bins), 0)
    column = lax.broadcasted_iota(jnp.int32, (128, bins), 1)
    pick = jnp.where(lane == place[0] * each + column // splits, 1.0, 0.0).astype(BF16)
    spread = dot(block, pick)
    row = lax.broadcasted_iota(jnp.int32, (height, bins), 0)
    column = lax.broadcasted_iota(jnp.int32, (height, bins), 1)
    spread = jnp.where(row % splits == column % splits, spread, 0.0)
    image[...] = jnp.sum(spread.reshape(owned, splits, bins), axis=1)


def params():
    return pltpu.CompilerParams(vmem_limit_bytes=VMEM_LIMIT)


def whole(memory_space):
    return pl.BlockSpec(memory_space=memory_space)


def illumination_sharded(
    currents_in,
    rad_pattern,
    far_map,
    reflect,
    centres,
    spectral_dirs,
    receiver_dirs,
    partners,
    partner_count,
    pair_weight,
):
    local_rows, local_cols, _, illum_count, unit_count = currents_in.shape
    n_px, n_py = lax.axis_size("px"), lax.axis_size("py")
    devices = n_px * n_py
    local = local_rows * local_cols
    rows = 2 * local * illum_count
    total_cols = local_cols * n_py
    total_rows = local_rows * n_px
    patches = total_rows * total_cols
    rcv_count = far_map.shape[1]
    block = 2 * local

    ids = np.arange(rows).reshape(local, 2, illum_count)
    to_send = np.ascontiguousarray(ids.transpose(2, 1, 0)).reshape(-1)
    send_table = one_hot_rows(to_send)
    ids = np.arange(rows).reshape(devices, 2, local)
    to_sort = np.ascontiguousarray(ids.transpose(1, 0, 2)).reshape(-1)
    sort_table = one_hot_rows(to_sort)

    patch = np.arange(patches)
    device, within = patch // local, patch % local
    patch_row = device // n_py * local_rows + within // local_cols
    patch_col = device % n_py * local_cols + within % local_cols
    offset_of = np.full((patches, patches), -1, np.int32)
    for o, (a, b) in enumerate(OFFSETS):
        match = (patch_row[None, :] - patch_row[:, None] == a) & (
            (patch_col[None, :] - patch_col[:, None] - b) % total_cols == 0
        )
        offset_of[match] = o

    splits = n_px
    tile = rcv_count // splits
    short = 2 * np.pi / splits * (np.arange(splits)[:, None] * np.arange(splits)[None, :] % splits)
    twist = 2 * np.pi / rcv_count * (np.arange(splits)[:, None] * np.arange(tile)[None, :])
    long = 2 * np.pi / tile * (np.arange(tile)[:, None] * np.arange(tile)[None, :] % tile)
    long_table = np.concatenate([np.cos(long), np.sin(long)], axis=1)

    vmem, smem, anywhere = pltpu.VMEM, pltpu.SMEM, pl.ANY
    base = jnp.stack([lax.axis_index("px") * local_rows, lax.axis_index("py") * local_cols])
    sent_width = unit_count + unit_count // 2 + 128
    packed = pl.pallas_call(
        functools.partial(pack_kernel, rows, total_cols),
        out_shape=jax.ShapeDtypeStruct((rows, sent_width), BF16),
        in_specs=[whole(m) for m in (smem, vmem, vmem, vmem, smem, smem, smem, smem)],
        out_specs=whole(vmem),
        compiler_params=params(),
        name="pack",
    )(
        base.astype(jnp.int32),
        currents_in.reshape(rows, unit_count),
        jnp.asarray(send_table, BF16),
        reflect,
        pair_weight.astype(F32),
        partners,
        partner_count,
        centres,
    )
    axes = ("px", "py")
    got = lax.all_to_all(packed.reshape(devices, block, sent_width), axes, 0, 0, tiled=True)

    scale = 0.125 / (patches * rcv_count)
    back_width = unit_count + 128
    answer = pl.pallas_call(
        functools.partial(main_kernel, scale, splits),
        out_shape=jax.ShapeDtypeStruct((rows, back_width), BF16),
        in_specs=[whole(vmem)] * 11 + [whole(anywhere)] * 2,
        out_specs=whole(vmem),
        scratch_shapes=[
            pltpu.VMEM(rad_pattern.shape, BF16),
            pltpu.VMEM(far_map.shape, BF16),
            pltpu.SemaphoreType.DMA,
            pltpu.SemaphoreType.DMA,
        ],
        compiler_params=params(),
        name="bounces",
    )(
        got.reshape(rows, sent_width),
        jnp.asarray(sort_table, BF16),
        jnp.asarray(sort_table.T, BF16),
        jnp.asarray(offset_of),
        spectral_dirs,
        receiver_dirs,
        jnp.asarray(np.cos(short), F32),
        jnp.asarray(np.sin(short), F32),
        jnp.asarray(np.cos(twist), F32),
        jnp.asarray(np.sin(twist), F32),
        jnp.asarray(long_table, F32),
        rad_pattern,
        far_map,
    )
    back = lax.all_to_all(answer.reshape(devices, block, back_width), axes, 0, 0, tiled=True)

    owned = illum_count // n_py
    per_row = 128 // (tile // splits)
    place = jnp.stack([lax.axis_index("px") % per_row, lax.axis_index("py")]).astype(jnp.int32)
    currents, image = pl.pallas_call(
        functools.partial(unpack_kernel, per_row),
        out_shape=(
            jax.ShapeDtypeStruct((rows, unit_count), BF16),
            jax.ShapeDtypeStruct((owned, tile), F32),
        ),
        in_specs=[whole(m) for m in (smem, vmem, vmem)],
        out_specs=(whole(vmem), whole(vmem)),
        compiler_params=params(),
        name="unpack",
    )(place, back.reshape(rows, back_width), jnp.asarray(send_table.T, BF16))
    return (currents.reshape(currents_in.shape), image)


def fits(mesh):
    def check(currents_in, far_map):
        n_px, n_py = mesh.shape["px"], mesh.shape["py"]
        total_rows, total_cols, _, illum_count, unit_count = currents_in.shape
        local = (total_rows // n_px) * (total_cols // n_py)
        return (
            illum_count == n_px * n_py
            and local == 4
            and n_px == 8
            and unit_count % 256 == 0
            and far_map.shape[1] == n_px * 256
            and illum_count % n_py == 0
            and total_cols > 2 * COL_REACH
        )

    return check


def solution(mesh):
    in_specs = (
        P("px", "py", None, None, None),
        P(),
        P(),
        P("px", "py", None),
        P(None, "px", "py"),
        P(),
        P(),
        P("px", "py", None),
        P("px", "py"),
        P("px", "py", None),
    )
    out_specs = (P("px", "py", None, None, None), P("py", "px"))
    check = fits(mesh)

    def run(*args):
        local = illumination_sharded if check(args[0], args[2]) else patch_sharded
        mapped = jax.shard_map(
            local, mesh=mesh, in_specs=in_specs, out_specs=out_specs, check_vma=False
        )
        return mapped(*args)

    return run
```

profile of v0, /device:TPU:0, one launch (start us, length us, event | category | flops | bytes accessed | tf_op | source)
XLA Modules:
  0.0 59.3 jit_solution(16726535193811125085)
XLA Ops:
  0.6 0.0 copy-start.2
  0.6 0.0 copy-start.1
  0.7 0.8 %convert_element_type.3.weight = f32[2,2,12]{2,1,0:T(2,128)S(1)} convert(bf16[2,2,12]{2,1,0:T(2,128)(2,1)} %param.29) | non-fusion elementwise | flops 48 | bytes 288 | tf_op jit(solution)/shard_map/convert_element_type | solution.py:474
  1.5 0.8 %copy.22.centres = f32[3,2,2]{2,1,0:T(2,128)S(1)} copy(f32[3,2,2]{0,2,1:T(2,128)} %param.24) | data formatting | bytes 96 | tf_op args[4]
  2.2 0.1 pad_add_fusion.1.base
  2.3 0.0 copy-start.3
  2.3 0.9 %copy-done.3 = bf16[2,2,2,32,512]{4,3,2,1,0:T(8,128)(2,1)S(1)} copy-done((bf16[2,2,2,32,512]{4,3,2,1,0:T(8,128)(2,1)S(1)}, bf16[2,2,2,32,512]{4,3,2,1,0:T(8,128)(2,1)}, u32[]{:S(2)}) %copy-start.3) | copy-done | bytes 262168
  3.3 0.0 copy-start.7
  3.3 0.9 %copy-done.7 = bf16[256,256]{1,0:T(8,128)(2,1)S(1)} copy-done((bf16[256,256]{1,0:T(8,128)(2,1)S(1)}, bf16[256,256]{1,0:T(8,128)(2,1)}, u32[]{:S(2)}) %copy-start.7) | copy-done | bytes 131096
  4.2 0.0 copy-start.10
  4.2 0.7 %copy-done.10 = f32[2,2,512]{2,1,0:T(2,128)S(1)} copy-done((f32[2,2,512]{2,1,0:T(2,128)S(1)}, f32[2,2,512]{2,1,0:T(2,128)}, u32[]{:S(2)}) %copy-start.10) | copy-done | bytes 8216
  4.9 0.0 copy-start.16
  4.9 0.7 %copy-done.16 = s32[2,2,12]{2,1,0:T(2,128)S(1)} copy-done((s32[2,2,12]{2,1,0:T(2,128)S(1)}, s32[2,2,12]{2,1,0:T(2,128)}, u32[]{:S(2)}) %copy-start.16) | copy-done | bytes 216
  5.5 0.0 copy-start.17
  5.5 0.7 %copy-done.17 = s32[2,2]{1,0:T(2,128)S(1)} copy-done((s32[2,2]{1,0:T(2,128)S(1)}, s32[2,2]{1,0:T(2,128)}, u32[]{:S(2)}) %copy-start.17) | copy-done | bytes 40
  6.2 0.9 %pack.1 = bf16[256,896]{1,0:T(8,128)(2,1)S(1)} custom-call(s32[2]{0:T(128)S(1)} %pad_add_fusion.1.base, bf16[256,512]{1,0:T(8,128)(2,1)S(1)} %bitcast.13, bf16[256,256]{1,0:T(8,128)(2,1)S(1)} %copy-done.7, f32[2,2,512]{2,1,0:T(2,128)S(1)} %copy-done.10, f32[2,2,12]{2,1,0:T(2,128)S(1)} %convert_element_type.3.weight, s32[2,2,12]{2,1,0:T(2,128)S(1)} %copy-done.16, ...), custom_call_target="tpu_custom_call" | custom-call | tf_op jit(solution)/shard_map/pack/pallas_call | solution.py:462
  7.1 20.2 %all_to_all.10 = bf16[32,8,896]{2,1,0:T(8,128)(2,1)S(1)} all-to-all(bf16[32,8,896]{2,1,0:T(8,128)(2,1)S(1)} %bitcast.11), channel_id=1, replica_groups=mesh['px'=8,'py'=4] {'px','py'}, dimensions={0} | all-to-all | bytes 917504 | tf_op jit(solution)/shard_map/all_to_all | solution.py:480
  27.3 0.0 copy-done.2
  27.3 0.0 copy-done.1
  27.3 0.0 copy-start
  27.3 1.6 %copy-done = bf16[512,2048]{1,0:T(8,128)(2,1)S(1)} copy-done((bf16[512,2048]{1,0:T(8,128)(2,1)S(1)}, bf16[512,2048]{1,0:T(8,128)(2,1)}, u32[]{:S(2)}) %copy-start) | copy-done | bytes 2097176
  28.9 0.0 copy-start.4
  28.9 0.9 %copy-done.4 = bf16[256,256]{1,0:T(8,128)(2,1)S(1)} copy-done((bf16[256,256]{1,0:T(8,128)(2,1)S(1)}, bf16[256,256]{1,0:T(8,128)(2,1)}, u32[]{:S(2)}) %copy-start.4) | copy-done | bytes 131096
  29.8 0.0 copy-start.5
  29.8 0.9 %copy-done.5 = bf16[256,256]{1,0:T(8,128)(2,1)S(1)} copy-done((bf16[256,256]{1,0:T(8,128)(2,1)S(1)}, bf16[256,256]{1,0:T(8,128)(2,1)}, u32[]{:S(2)}) %copy-start.5) | copy-done | bytes 131096
  30.7 0.0 copy-start.8
  30.7 0.8 %copy-done.8 = s32[128,128]{1,0:T(8,128)S(1)} copy-done((s32[128,128]{1,0:T(8,128)S(1)}, s32[128,128]{1,0:T(8,128)}, u32[]{:S(2)}) %copy-start.8) | copy-done | bytes 65560
  31.6 0.0 copy-start.9
  31.6 0.8 %copy-done.9 = f32[3,2048]{1,0:T(4,128)S(1)} copy-done((f32[3,2048]{1,0:T(4,128)S(1)}, f32[3,2048]{1,0:T(4,128)}, u32[]{:S(2)}) %copy-start.9) | copy-done | bytes 24600
  32.3 0.0 copy-start.11
  32.3 0.7 %copy-done.11 = f32[3,512]{1,0:T(4,128)S(1)} copy-done((f32[3,512]{1,0:T(4,128)S(1)}, f32[3,512]{1,0:T(4,128)}, u32[]{:S(2)}) %copy-start.11) | copy-done | bytes 6168
  33.0 0.0 copy-start.12
  33.0 0.7 %copy-done.12 = f32[8,256]{1,0:T(8,128)S(1)} copy-done((f32[8,256]{1,0:T(8,128)S(1)}, f32[8,256]{1,0:T(8,128)}, u32[]{:S(2)}) %copy-start.12) | copy-done | bytes 8216
  33.7 0.0 copy-start.13
  33.7 0.7 %copy-done.13 = f32[8,256]{1,0:T(8,128)S(1)} copy-done((f32[8,256]{1,0:T(8,128)S(1)}, f32[8,256]{1,0:T(8,128)}, u32[]{:S(2)}) %copy-start.13) | copy-done | bytes 8216
  34.4 0.0 copy-start.14
  34.4 0.7 %copy-done.14 = f32[8,8]{1,0:T(8,128)S(1)} copy-done((f32[8,8]{1,0:T(8,128)S(1)}, f32[8,8]{1,0:T(8,128)}, u32[]{:S(2)}) %copy-start.14) | copy-done | bytes 280
  35.1 0.0 copy-start.15
  35.1 0.7 %copy-done.15 = f32[8,8]{1,0:T(8,128)S(1)} copy-done((f32[8,8]{1,0:T(8,128)S(1)}, f32[8,8]{1,0:T(8,128)}, u32[]{:S(2)}) %copy-start.15) | copy-done | bytes 280
  35.8 0.0 copy-start.6
  35.8 7.0 %bounces.1 = bf16[256,640]{1,0:T(8,128)(2,1)} custom-call(bf16[256,896]{1,0:T(8,128)(2,1)S(1)} %bitcast.10, bf16[256,256]{1,0:T(8,128)(2,1)S(1)} %copy-done.5, bf16[256,256]{1,0:T(8,128)(2,1)S(1)} %copy-done.4, s32[128,128]{1,0:T(8,128)S(1)} %copy-done.8, f32[3,512]{1,0:T(4,128)S(1)} %copy-done.11, f32[3,2048]{1,0:T(4,128)S(1)} %copy-done.9, ...), custom_call_target="tpu_custom_call" | custom-call | tf_op jit(solution)/shard_map/bounces/pallas_call | solution.py:484
  42.9 4.0 %all-to-all-start.1 = ((bf16[32,8,640]{2,1,0:T(8,128)(2,1)}), bf16[32,8,640]{2,1,0:T(8,128)(2,1)S(1)}, u32[]{:S(2)}, u32[]{:S(2)}) async-start(bf16[32,8,640]{2,1,0:T(8,128)(2,1)} %bitcast.7), calls=%async_computation.1 | async-start | bytes 655360 | tf_op jit(solution)/shard_map/all_to_all | solution.py:512
  46.9 0.1 pad_add_fusion.place
  46.9 10.9 %all-to-all-done.1 = bf16[32,8,640]{2,1,0:T(8,128)(2,1)S(1)} async-done(((bf16[32,8,640]{2,1,0:T(8,128)(2,1)}), bf16[32,8,640]{2,1,0:T(8,128)(2,1)S(1)}, u32[]{:S(2)}, u32[]{:S(2)}) %all-to-all-start.1) | async-done | bytes 327712 | tf_op jit(solution)/shard_map/all_to_all | solution.py:512
  57.8 0.0 copy-done.6
  57.8 1.5 %unpack.1 = (bf16[256,512]{1,0:T(8,128)(2,1)}, f32[8,256]{1,0:T(8,128)}) custom-call(s32[2]{0:T(128)S(1)} %pad_add_fusion.place, bf16[256,640]{1,0:T(8,128)(2,1)S(1)} %bitcast.12, bf16[256,256]{1,0:T(8,128)(2,1)S(1)} %copy-done.6), custom_call_target="tpu_custom_call" | custom-call | tf_op jit(solution)/shard_map/unpack/pallas_call | solution.py:517
Async XLA Ops:
  0.6 26.7 %copy-start.2 = (f32[256,512]{1,0:T(8,128)S(1)}, f32[256,512]{1,0:T(8,128)}, u32[]{:S(2)}) copy-start(f32[256,512]{1,0:T(8,128)} %constant.52.clone.long_table) | copy-start | bytes 1572868
  0.6 26.7 %copy-start.1 = (bf16[2,512,512]{2,1,0:T(8,128)(2,1)S(1)}, bf16[2,512,512]{2,1,0:T(8,128)(2,1)}, u32[]{:S(2)}) copy-start(bf16[2,512,512]{2,1,0:T(8,128)(2,1)} %rad_hbm.1) | copy-start | bytes 3145732
  2.3 0.9 %copy-start.3 = (bf16[2,2,2,32,512]{4,3,2,1,0:T(8,128)(2,1)S(1)}, bf16[2,2,2,32,512]{4,3,2,1,0:T(8,128)(2,1)}, u32[]{:S(2)}) copy-start(bf16[2,2,2,32,512]{4,3,2,1,0:T(8,128)(2,1)} %param.20) | copy-start | bytes 786436
  3.3 0.9 %copy-start.7 = (bf16[256,256]{1,0:T(8,128)(2,1)S(1)}, bf16[256,256]{1,0:T(8,128)(2,1)}, u32[]{:S(2)}) copy-start(bf16[256,256]{1,0:T(8,128)(2,1)} %constant.44.clone.order) | copy-start | bytes 393220
  4.2 0.7 %copy-start.10 = (f32[2,2,512]{2,1,0:T(2,128)S(1)}, f32[2,2,512]{2,1,0:T(2,128)}, u32[]{:S(2)}) copy-start(f32[2,2,512]{2,1,0:T(2,128)} %reflect.1) | copy-start | bytes 24580
  4.9 0.7 %copy-start.16 = (s32[2,2,12]{2,1,0:T(2,128)S(1)}, s32[2,2,12]{2,1,0:T(2,128)}, u32[]{:S(2)}) copy-start(s32[2,2,12]{2,1,0:T(2,128)} %partners.1) | copy-start | bytes 580
  5.5 0.7 %copy-start.17 = (s32[2,2]{1,0:T(2,128)S(1)}, s32[2,2]{1,0:T(2,128)}, u32[]{:S(2)}) copy-start(s32[2,2]{1,0:T(2,128)} %count.1) | copy-start | bytes 52
  27.3 1.6 %copy-start = (bf16[512,2048]{1,0:T(8,128)(2,1)S(1)}, bf16[512,2048]{1,0:T(8,128)(2,1)}, u32[]{:S(2)}) copy-start(bf16[512,2048]{1,0:T(8,128)(2,1)} %far_hbm.1) | copy-start | bytes 6291460
  28.9 0.9 %copy-start.4 = (bf16[256,256]{1,0:T(8,128)(2,1)S(1)}, bf16[256,256]{1,0:T(8,128)(2,1)}, u32[]{:S(2)}) copy-start(bf16[256,256]{1,0:T(8,128)(2,1)} %constant.46.clone.back) | copy-start | bytes 393220
  29.8 0.9 %copy-start.5 = (bf16[256,256]{1,0:T(8,128)(2,1)S(1)}, bf16[256,256]{1,0:T(8,128)(2,1)}, u32[]{:S(2)}) copy-start(bf16[256,256]{1,0:T(8,128)(2,1)} %constant.45.clone.order) | copy-start | bytes 393220
  30.7 0.8 %copy-start.8 = (s32[128,128]{1,0:T(8,128)S(1)}, s32[128,128]{1,0:T(8,128)}, u32[]{:S(2)}) copy-start(s32[128,128]{1,0:T(8,128)} %constant.47.clone.offset_of) | copy-start | bytes 196612
  31.6 0.8 %copy-start.9 = (f32[3,2048]{1,0:T(4,128)S(1)}, f32[3,2048]{1,0:T(4,128)}, u32[]{:S(2)}) copy-start(f32[3,2048]{1,0:T(4,128)} %receiver_dirs.1) | copy-start | bytes 73732
  32.3 0.7 %copy-start.11 = (f32[3,512]{1,0:T(4,128)S(1)}, f32[3,512]{1,0:T(4,128)}, u32[]{:S(2)}) copy-start(f32[3,512]{1,0:T(4,128)} %spectral_dirs.1) | copy-start | bytes 18436
  33.0 0.7 %copy-start.12 = (f32[8,256]{1,0:T(8,128)S(1)}, f32[8,256]{1,0:T(8,128)}, u32[]{:S(2)}) copy-start(f32[8,256]{1,0:T(8,128)} %constant.51.clone.twist_sin) | copy-start | bytes 24580
  33.7 0.7 %copy-start.13 = (f32[8,256]{1,0:T(8,128)S(1)}, f32[8,256]{1,0:T(8,128)}, u32[]{:S(2)}) copy-start(f32[8,256]{1,0:T(8,128)} %constant.50.clone.twist_cos) | copy-start | bytes 24580
  34.4 0.7 %copy-start.14 = (f32[8,8]{1,0:T(8,128)S(1)}, f32[8,8]{1,0:T(8,128)}, u32[]{:S(2)}) copy-start(f32[8,8]{1,0:T(8,128)} %constant.49.clone.short_sin) | copy-start | bytes 772
  35.1 0.7 %copy-start.15 = (f32[8,8]{1,0:T(8,128)S(1)}, f32[8,8]{1,0:T(8,128)}, u32[]{:S(2)}) copy-start(f32[8,8]{1,0:T(8,128)} %constant.48.clone.short_cos) | copy-start | bytes 772
  35.8 22.0 %copy-start.6 = (bf16[256,256]{1,0:T(8,128)(2,1)S(1)}, bf16[256,256]{1,0:T(8,128)(2,1)}, u32[]{:S(2)}) copy-start(bf16[256,256]{1,0:T(8,128)(2,1)} %constant.53.clone.order) | copy-start | bytes 393220
  42.9 15.0 %all-to-all-start.1 = ((bf16[32,8,640]{2,1,0:T(8,128)(2,1)}), bf16[32,8,640]{2,1,0:T(8,128)(2,1)S(1)}, u32[]{:S(2)}, u32[]{:S(2)}) async-start(bf16[32,8,640]{2,1,0:T(8,128)(2,1)} %bitcast.7), calls=%async_computation.1 | async-start | bytes 655360 | tf_op jit(solution)/shard_map/all_to_all | solution.py:512
where the time goes:
time: 60.4 us; the launch traced here: 59.3 us
  blocking collectives  20.2 us (33%)
  local copies, waits for them, and re-layouts  13.2 us (22%)
  waiting for transfers between devices  10.9 us (18%)
  Pallas kernels  9.41 us (16%)
  starting transfers between devices  3.98 us (7%)
  other arithmetic  0.95 us (2%)
  between operations  0.71 us (1%)
    all_to_all x1, blocking collectives, illumination_sharded(): lax.all_to_all(packed.reshape(devices, block, sent_width), axes, 0, 0, ti...  20.2 us
    unnamed x37, local copies, waits for them, and re-layouts  13.2 us
    all_to_all x1, waiting for transfers between devices, illumination_sharded(): lax.all_to_all(answer.reshape(devices, block, back_width), axes, 0, 0, ti...  10.9 us
    pallas_call x1, Pallas kernels, illumination_sharded(): pl.pallas_call(functools.partial(main_kernel, scale, splits), out_shape=j...  7.05 us
    all_to_all x1, starting transfers between devices, illumination_sharded(): lax.all_to_all(answer.reshape(devices, block, back_width), axes, 0, 0, ti...  3.98 us
    pallas_call x1, Pallas kernels, illumination_sharded(): pl.pallas_call(functools.partial(unpack_kernel, per_row), out_shape=(jax....  1.47 us
  transfers between devices with their start and end apart: 1, of which 1 were waited for; matrix products, arithmetic and copies ran while one was open for 0% of the time, Pallas kernels for 0%

commit v1 on v0

--- a/solution.py
+++ b/solution.py
@@ -20,7 +20,7 @@
 F32 = jnp.float32
 BF16 = jnp.bfloat16
 HIGH = lax.Precision.HIGHEST
-VMEM_LIMIT = 48 * 1024 * 1024
+VMEM_LIMIT = 62 * 1024 * 1024
 
 
 def padded(block, sides, width, periodic):
@@ -201,93 +201,159 @@
     return lax.dot_general(left, right, (((1,), (1,)), ((), ())), preferred_element_type=F32)
 
 
-def one_hot_rows(sources):
-    table = np.zeros((len(sources), len(sources)), np.float32)
-    table[np.arange(len(sources)), sources] = 1.0
-    return table
+def sorter(rows, outer, inner):
+    out_id = lax.broadcasted_iota(jnp.int32, (rows, rows), 0)
+    in_id = lax.broadcasted_iota(jnp.int32, (rows, rows), 1)
+    i = out_id // (2 * outer)
+    part = (out_id // outer) % 2
+    o = out_id % outer
+    return jnp.where(in_id == (o * 2 + part) * inner + i, 1.0, 0.0).astype(BF16)
+
+
+def part_sorter(rows, inner, back):
+    first = lax.broadcasted_iota(jnp.int32, (rows, rows), 1 if back else 0)
+    second = lax.broadcasted_iota(jnp.int32, (rows, rows), 0 if back else 1)
+    half = rows // 2
+    part = first // half
+    o = (first % half) // inner
+    i = first % inner
+    return jnp.where(second == (o * 2 + part) * inner + i, 1.0, 0.0).astype(BF16)
+
+
+def fetch(pairs, sems):
+    copies = [
+        pltpu.make_async_copy(source, target, sems.at[n])
+        for n, (source, target) in enumerate(pairs)
+    ]
+    for copy in copies:
+        copy.start()
+    return copies
 
 
 def pack_kernel(
-    rows, total_cols, base, cur, order, reflect, weight, partners, count, centres, out
+    total_cols,
+    cur_hbm,
+    reflect_hbm,
+    weight_hbm,
+    partners_hbm,
+    count_hbm,
+    centres_hbm,
+    out,
+    cur,
+    reflect,
+    weight,
+    partners,
+    count,
+    centres,
+    sems,
 ):
+    copies = fetch(
+        [
+            (partners_hbm, partners),
+            (weight_hbm, weight),
+            (count_hbm, count),
+            (centres_hbm, centres),
+            (reflect_hbm, reflect),
+            (cur_hbm, cur),
+        ],
+        sems,
+    )
+    rows = cur.shape[0]
     local_rows, local_cols, unit_count = reflect.shape
     local = local_rows * local_cols
     half = unit_count // 2
-    width = unit_count + half
-    out[:, :unit_count] = dot(order[...], cur[...]).astype(BF16)
-    refl = reflect[...].reshape(local, unit_count)
-    refl = jnp.concatenate([refl[:, :half], refl[:, half:]], axis=0)
+    base_row = lax.axis_index("px") * local_rows
+    base_col = lax.axis_index("py") * local_cols
+    order = sorter(rows, local, rows // (2 * local))
     lane = lax.broadcasted_iota(jnp.int32, (local, 128), 1)
     row = lax.broadcasted_iota(jnp.int32, (local, 128), 0)
-    patch_row = base[0] + row // local_cols
-    patch_col = base[1] + row % local_cols
+    patch_row = base_row + row // local_cols
+    patch_col = base_col + row % local_cols
     target = jnp.full((local, 128), -1, jnp.int32)
     for o, (a, b) in enumerate(OFFSETS):
         col = patch_col + b
         col = jnp.where(col < 0, col + total_cols, col)
         col = jnp.where(col >= total_cols, col - total_cols, col)
         target = jnp.where(lane == o, (patch_row + a) * total_cols + col, target)
-    small = jnp.zeros((local, 128), F32)
+    for copy in copies[:5]:
+        copy.wait()
+    ids = partners[...].reshape(local, SLOTS)
+    weights = weight[...].astype(F32).reshape(local, SLOTS)
+    spots = centres[...].reshape(local, 3)
+    counts = count[...]
+    live = jnp.zeros((local, 128), jnp.int32)
     for r in range(local_rows):
         for c in range(local_cols):
-            here = row == r * local_cols + c
-            for s in range(SLOTS):
-                w = jnp.where(s < count[r, c], weight[r, c, s], 0.0)
-                small = small + jnp.where(here & (target == partners[r, c, s]), w, 0.0)
-    spot = jnp.zeros((local, 128), F32)
+            live = jnp.where(row == r * local_cols + c, counts[r : r + 1, c : c + 1], live)
+    small = jnp.zeros((local, 128), F32)
+    for s in range(SLOTS):
+        hit = (ids[:, s : s + 1] == target) & (live > s)
+        small = small + jnp.where(hit, weights[:, s : s + 1], 0.0)
     first = len(OFFSETS)
     for d in range(3):
-        in_place = (lane >= first + 3 * d) & (lane < first + 3 * d + 3)
-        for r in range(local_rows):
-            for c in range(local_cols):
-                here = row == r * local_cols + c
-                spot = jnp.where(in_place & here, centres[d, r, c], spot)
-    top = spot.astype(BF16).astype(F32)
-    rest = spot - top
-    middle = rest.astype(BF16).astype(F32)
-    bottom = rest - middle
-    term = lane - first
-    term = term - jnp.where(term >= 6, 6, jnp.where(term >= 3, 3, 0))
-    parts = jnp.where(term == 0, top, jnp.where(term == 1, middle, bottom))
-    small = jnp.where((lane >= first) & (lane < first + 9), parts, small)
+        spot = spots[:, d : d + 1]
+        top = spot.astype(BF16).astype(F32)
+        rest = spot - top
+        middle = rest.astype(BF16).astype(F32)
+        small = jnp.where(lane == first + 3 * d, top, small)
+        small = jnp.where(lane == first + 3 * d + 1, middle, small)
+        small = jnp.where(lane == first + 3 * d + 2, rest - middle, small)
+    refl = reflect[...].reshape(local, unit_count)
+    refl = jnp.concatenate([refl[:, :half], refl[:, half:]], axis=0)
     small = jnp.concatenate([small, jnp.zeros_like(small)], axis=0)
     tail = jnp.concatenate([refl, small], axis=1)
     tail = jnp.concatenate([tail, tail], axis=0).astype(BF16)
     step = tail.shape[0]
     for s in range(rows // step):
         out[step * s : step * (s + 1), unit_count:] = tail
+    copies[5].wait()
+    out[:, :unit_count] = dot(order, cur[...]).astype(BF16)
+
+
+def table_kernel(long_table):
+    tile = long_table.shape[0]
+    row = lax.broadcasted_iota(jnp.int32, (tile, tile), 0)
+    column = lax.broadcasted_iota(jnp.int32, (tile, tile), 1)
+    cosine, sine = cos_sin(((row * column) % tile).astype(F32) * (1.0 / tile))
+    long_table[:, :tile] = cosine
+    long_table[:, tile:] = sine
 
 
 def main_kernel(
     scale,
-    splits,
+    grid_shape,
+    local_shape,
     got,
-    order,
-    back,
-    offset_of,
-    spectral_dirs,
-    receiver_dirs,
-    short_cos,
-    short_sin,
-    twist_cos,
-    twist_sin,
     long_table,
+    spectral_hbm,
+    receiver_hbm,
     rad_hbm,
     far_hbm,
     out,
+    spectral_dirs,
+    receiver_dirs,
     rad,
     far_map,
-    rad_sem,
-    far_sem,
+    sems,
 ):
-    rad_copy = pltpu.make_async_copy(rad_hbm, rad, rad_sem)
-    far_copy = pltpu.make_async_copy(far_hbm, far_map, far_sem)
-    rad_copy.start()
-    far_copy.start()
+    copies = fetch(
+        [
+            (spectral_hbm, spectral_dirs),
+            (rad_hbm, rad),
+            (receiver_hbm, receiver_dirs),
+            (far_hbm, far_map),
+        ],
+        sems,
+    )
     unit_count = rad.shape[1]
     half = unit_count // 2
-    patches = got.shape[0] // 2
-    sorted_rows = dot(order[...], got[...])
+    rows = got.shape[0]
+    patches = rows // 2
+    local_rows, local_cols = local_shape
+    local = local_rows * local_cols
+    splits, n_py = grid_shape
+    total_cols = n_py * local_cols
+    sorted_rows = dot(part_sorter(rows, local, False), got[...])
     start = sorted_rows[:, :unit_count]
     reflect = jnp.concatenate(
         [
@@ -307,13 +373,30 @@
     def turns(dirs):
         return centre[0] * dirs[0:1] + centre[1] * dirs[1:2] + centre[2] * dirs[2:3]
 
+    def place(axis):
+        ids = lax.broadcasted_iota(jnp.int32, (patches, patches), axis)
+        device, within = ids // local, ids % local
+        return (
+            device // n_py * local_rows + within // local_cols,
+            device % n_py * local_cols + within % local_cols,
+        )
+
+    (here_row, here_col), (there_row, there_col) = place(0), place(1)
+    down = there_row - here_row
+    across = there_col - here_col
+    across = jnp.where(across > COL_REACH, across - total_cols, across)
+    across = jnp.where(across < -COL_REACH, across + total_cols, across)
+    near = (down >= -ROW_REACH) & (down <= ROW_REACH)
+    near = near & (across >= -COL_REACH) & (across <= COL_REACH)
+    offset = (down + ROW_REACH) * (2 * COL_REACH + 1) + across + COL_REACH
+    offset = jnp.where(near, offset, -1)
     coef = jnp.zeros((patches, patches), F32)
-    offsets = offset_of[...]
     for o in range(len(OFFSETS)):
-        coef = coef + jnp.where(offsets == o, small[:, o : o + 1], 0.0)
+        coef = jnp.where(offset == o, small[:, o : o + 1], coef)
     coef = coef.astype(BF16)
+    copies[0].wait()
     cosine, sine = cos_sin(turns(spectral_dirs[...]))
-    rad_copy.wait()
+    copies[1].wait()
 
     def spectrum(current):
         first_part = dot(current, rad[0])
@@ -343,11 +426,12 @@
         current = jnp.concatenate(
             [start[:patches] + reflect * recv_re, start[patches:] + reflect * recv_im], axis=0
         ).astype(BF16)
-    out[:, :unit_count] = dot(back[...], current).astype(BF16)
+    out[:, :unit_count] = dot(part_sorter(rows, local, True), current).astype(BF16)
 
     spec_re, spec_im = spectrum(current)
     final = jnp.concatenate([spec_re, spec_im], axis=0).astype(BF16)
-    far_copy.wait()
+    copies[2].wait()
+    copies[3].wait()
     tile = far_map.shape[1] // splits
     far_re, far_im = [], []
     for t in range(splits):
@@ -357,6 +441,12 @@
         beam_im = beams[patches:]
         far_re.append(jnp.sum(beam_re * cos_view - beam_im * sin_view, axis=0, keepdims=True))
         far_im.append(jnp.sum(beam_re * sin_view + beam_im * cos_view, axis=0, keepdims=True))
+    row = lax.broadcasted_iota(jnp.int32, (splits, 128), 0)
+    column = lax.broadcasted_iota(jnp.int32, (splits, 128), 1)
+    short_cos, short_sin = cos_sin((row * column % splits).astype(F32) * (1.0 / splits))
+    row = lax.broadcasted_iota(jnp.int32, (splits, tile), 0)
+    column = lax.broadcasted_iota(jnp.int32, (splits, tile), 1)
+    twist_cos, twist_sin = cos_sin((row * column).astype(F32) * (1.0 / (splits * tile)))
     mid_re = jnp.zeros((splits, tile), F32)
     mid_im = jnp.zeros((splits, tile), F32)
     for t in range(splits):
@@ -364,35 +454,36 @@
         s = short_sin[:, t : t + 1]
         mid_re = mid_re + (c * far_re[t] + s * far_im[t])
         mid_im = mid_im + (c * far_im[t] - s * far_re[t])
-    tw_re = mid_re * twist_cos[...] + mid_im * twist_sin[...]
-    tw_im = mid_im * twist_cos[...] - mid_re * twist_sin[...]
+    tw_re = mid_re * twist_cos + mid_im * twist_sin
+    tw_im = mid_im * twist_cos - mid_re * twist_sin
     both = jnp.concatenate([tw_re, tw_im], axis=0)
     answer = jnp.dot(both, long_table[...], precision=HIGH, preferred_element_type=F32)
     image_re = answer[:splits, :tile] + answer[splits:, tile:]
     image_im = answer[splits:, :tile] - answer[:splits, tile:]
-    image = (scale * (image_re * image_re + image_im * image_im)).astype(BF16)
+    image = scale * (image_re * image_re + image_im * image_im)
     pieces = tile // 128
-    rows_each = out.shape[0] // pieces
+    rows_each = rows // pieces
     for p in range(pieces):
-        piece = image[:, 128 * p : 128 * (p + 1)].astype(F32)
+        piece = image[:, 128 * p : 128 * (p + 1)]
         piece = jnp.concatenate([piece, piece], axis=0).astype(BF16)
         for s in range(rows_each // piece.shape[0]):
             at = p * rows_each + s * piece.shape[0]
             out[at : at + piece.shape[0], unit_count:] = piece
 
 
-def unpack_kernel(per_row, place, got, order, currents, image):
-    unit_count = currents.shape[1]
-    currents[...] = dot(order[...], got[:, :unit_count]).astype(BF16)
-    splits = 8
+def unpack_kernel(splits, local, got, currents, image):
+    rows, unit_count = currents.shape
+    order = sorter(rows, rows // (2 * local), local)
+    currents[...] = dot(order, got[:, :unit_count]).astype(BF16)
     owned, bins = image.shape
     height = owned * splits
-    at = pl.multiple_of(place[1] * height, height)
+    each = bins // splits
+    at = pl.multiple_of(lax.axis_index("py") * height, height)
+    lanes_from = lax.axis_index("px") % (128 // each) * each
     block = got[pl.ds(at, height), unit_count:]
-    each = bins // splits
     lane = lax.broadcasted_iota(jnp.int32, (128, bins), 0)
     column = lax.broadcasted_iota(jnp.int32, (128, bins), 1)
-    pick = jnp.where(lane == place[0] * each + column // splits, 1.0, 0.0).astype(BF16)
+    pick = jnp.where(lane == lanes_from + column // splits, 1.0, 0.0).astype(BF16)
     spread = dot(block, pick)
     row = lax.broadcasted_iota(jnp.int32, (height, bins), 0)
     column = lax.broadcasted_iota(jnp.int32, (height, bins), 1)
@@ -400,12 +491,18 @@
     image[...] = jnp.sum(spread.reshape(owned, splits, bins), axis=1)
 
 
-def params():
-    return pltpu.CompilerParams(vmem_limit_bytes=VMEM_LIMIT)
-
-
-def whole(memory_space):
-    return pl.BlockSpec(memory_space=memory_space)
+def call(kernel, name, outs, operands, spaces, scratch=(), cost=None):
+    vmem = pl.BlockSpec(memory_space=pltpu.VMEM)
+    return pl.pallas_call(
+        kernel,
+        out_shape=outs,
+        in_specs=[pl.BlockSpec(memory_space=m) for m in spaces],
+        out_specs=jax.tree.map(lambda _: vmem, outs),
+        scratch_shapes=list(scratch),
+        compiler_params=pltpu.CompilerParams(vmem_limit_bytes=VMEM_LIMIT),
+        cost_estimate=cost,
+        name=name,
+    )(*operands)
 
 
 def illumination_sharded(
@@ -426,105 +523,72 @@
     local = local_rows * local_cols
     rows = 2 * local * illum_count
     total_cols = local_cols * n_py
-    total_rows = local_rows * n_px
-    patches = total_rows * total_cols
+    patches = local_rows * n_px * total_cols
     rcv_count = far_map.shape[1]
+    tile = rcv_count // n_px
     block = 2 * local
-
-    ids = np.arange(rows).reshape(local, 2, illum_count)
-    to_send = np.ascontiguousarray(ids.transpose(2, 1, 0)).reshape(-1)
-    send_table = one_hot_rows(to_send)
-    ids = np.arange(rows).reshape(devices, 2, local)
-    to_sort = np.ascontiguousarray(ids.transpose(1, 0, 2)).reshape(-1)
-    sort_table = one_hot_rows(to_sort)
-
-    patch = np.arange(patches)
-    device, within = patch // local, patch % local
-    patch_row = device // n_py * local_rows + within // local_cols
-    patch_col = device % n_py * local_cols + within % local_cols
-    offset_of = np.full((patches, patches), -1, np.int32)
-    for o, (a, b) in enumerate(OFFSETS):
-        match = (patch_row[None, :] - patch_row[:, None] == a) & (
-            (patch_col[None, :] - patch_col[:, None] - b) % total_cols == 0
-        )
-        offset_of[match] = o
-
-    splits = n_px
-    tile = rcv_count // splits
-    short = 2 * np.pi / splits * (np.arange(splits)[:, None] * np.arange(splits)[None, :] % splits)
-    twist = 2 * np.pi / rcv_count * (np.arange(splits)[:, None] * np.arange(tile)[None, :])
-    long = 2 * np.pi / tile * (np.arange(tile)[:, None] * np.arange(tile)[None, :] % tile)
-    long_table = np.concatenate([np.cos(long), np.sin(long)], axis=1)
-
-    vmem, smem, anywhere = pltpu.VMEM, pltpu.SMEM, pl.ANY
-    base = jnp.stack([lax.axis_index("px") * local_rows, lax.axis_index("py") * local_cols])
+    axes = ("px", "py")
+    vmem, hbm = pltpu.VMEM, pltpu.HBM
+
+    def like(array):
+        return pltpu.VMEM(array.shape, array.dtype)
+
     sent_width = unit_count + unit_count // 2 + 128
-    packed = pl.pallas_call(
-        functools.partial(pack_kernel, rows, total_cols),
-        out_shape=jax.ShapeDtypeStruct((rows, sent_width), BF16),
-        in_specs=[whole(m) for m in (smem, vmem, vmem, vmem, smem, smem, smem, smem)],
-        out_specs=whole(vmem),
-        compiler_params=params(),
-        name="pack",
-    )(
-        base.astype(jnp.int32),
+    sources = (
         currents_in.reshape(rows, unit_count),
-        jnp.asarray(send_table, BF16),
         reflect,
-        pair_weight.astype(F32),
+        pair_weight,
         partners,
         partner_count,
-        centres,
-    )
-    axes = ("px", "py")
+        jnp.transpose(centres, (1, 2, 0)),
+    )
+    packed = call(
+        functools.partial(pack_kernel, total_cols),
+        "pack",
+        jax.ShapeDtypeStruct((rows, sent_width), BF16),
+        sources,
+        [hbm] * 6,
+        [like(s) for s in sources] + [pltpu.SemaphoreType.DMA((6,))],
+    )
     got = lax.all_to_all(packed.reshape(devices, block, sent_width), axes, 0, 0, tiled=True)
-
+    long_table = call(
+        table_kernel,
+        "table",
+        jax.ShapeDtypeStruct((tile, 2 * tile), F32),
+        (),
+        [],
+        cost=pl.CostEstimate(flops=10**7, bytes_accessed=10**6, transcendentals=0),
+    )
     scale = 0.125 / (patches * rcv_count)
     back_width = unit_count + 128
-    answer = pl.pallas_call(
-        functools.partial(main_kernel, scale, splits),
-        out_shape=jax.ShapeDtypeStruct((rows, back_width), BF16),
-        in_specs=[whole(vmem)] * 11 + [whole(anywhere)] * 2,
-        out_specs=whole(vmem),
-        scratch_shapes=[
-            pltpu.VMEM(rad_pattern.shape, BF16),
-            pltpu.VMEM(far_map.shape, BF16),
-            pltpu.SemaphoreType.DMA,
-            pltpu.SemaphoreType.DMA,
-        ],
-        compiler_params=params(),
-        name="bounces",
-    )(
-        got.reshape(rows, sent_width),
-        jnp.asarray(sort_table, BF16),
-        jnp.asarray(sort_table.T, BF16),
-        jnp.asarray(offset_of),
-        spectral_dirs,
-        receiver_dirs,
-        jnp.asarray(np.cos(short), F32),
-        jnp.asarray(np.sin(short), F32),
-        jnp.asarray(np.cos(twist), F32),
-        jnp.asarray(np.sin(twist), F32),
-        jnp.asarray(long_table, F32),
-        rad_pattern,
-        far_map,
+    answer = call(
+        functools.partial(main_kernel, scale, (n_px, n_py), (local_rows, local_cols)),
+        "bounces",
+        jax.ShapeDtypeStruct((rows, back_width), BF16),
+        (
+            got.reshape(rows, sent_width),
+            long_table,
+            spectral_dirs,
+            receiver_dirs,
+            rad_pattern,
+            far_map,
+        ),
+        [vmem] * 2 + [hbm] * 4,
+        [like(a) for a in (spectral_dirs, receiver_dirs, rad_pattern, far_map)]
+        + [pltpu.SemaphoreType.DMA((4,))],
     )
     back = lax.all_to_all(answer.reshape(devices, block, back_width), axes, 0, 0, tiled=True)
-
     owned = illum_count // n_py
-    per_row = 128 // (tile // splits)
-    place = jnp.stack([lax.axis_index("px") % per_row, lax.axis_index("py")]).astype(jnp.int32)
-    currents, image = pl.pallas_call(
-        functools.partial(unpack_kernel, per_row),
-        out_shape=(
+    currents, image = call(
+        functools.partial(unpack_kernel, n_px, local),
+        "unpack",
+        (
             jax.ShapeDtypeStruct((rows, unit_count), BF16),
             jax.ShapeDtypeStruct((owned, tile), F32),
         ),
-        in_specs=[whole(m) for m in (smem, vmem, vmem)],
-        out_specs=(whole(vmem), whole(vmem)),
-        compiler_params=params(),
-        name="unpack",
-    )(place, back.reshape(rows, back_width), jnp.asarray(send_table.T, BF16))
+        (back.reshape(rows, back_width),),
+        [vmem],
+    )
     return (currents.reshape(currents_in.shape), image)
 
 

time: 60.4 us -> 49.9 us (0.83)
  local copies, waits for them, and re-layouts: 13.2 us -> 0.77 us
  blocking collectives: 20.2 us -> 15.1 us
  Pallas kernels: 9.41 us -> 13.4 us
  starting transfers between devices: 3.98 us -> 7.3 us
  waiting for transfers between devices: 10.9 us -> 11.9 us
  other arithmetic: 0.95 us -> 0 us
    unnamed x37 -> x2, local copies, waits for them, and re-layouts: 13.2 us -> 0.77 us
    all_to_all x1, blocking collectives: 20.2 us -> 15.1 us  [illumination_sharded(): lax.all_to_all(answer.reshape(devices, block, back_width), axes, 0, 0, ti...]
    pallas_call x3 -> x4, Pallas kernels: 9.41 us -> 13.4 us  [call(): pl.pallas_call(kernel, out_shape=outs, in_specs=[pl.BlockSpec(memory_spac...]
    all_to_all x1, starting transfers between devices: 3.98 us -> 7.3 us  [illumination_sharded(): lax.all_to_all(packed.reshape(devices, block, sent_width), axes, 0, 0, ti...]
    all_to_all x1, waiting for transfers between devices: 10.9 us -> 11.9 us  [illumination_sharded(): lax.all_to_all(packed.reshape(devices, block, sent_width), axes, 0, 0, ti...]
    convert_element_type x1 -> x0, other arithmetic: 0.8 us -> none  [illumination_sharded(): pair_weight.astype(F32)]
  transfers between devices with their start and end apart: 1 -> 1, of which waited for: 1 -> 1; matrix products, arithmetic and copies ran while one was open for 0% -> 0% of each run, Pallas kernels for 0% -> 2%
where the time goes in v1:
time: 49.9 us; the launch traced here: 49.1 us
  blocking collectives  15.1 us (30%)
  Pallas kernels  13.4 us (27%)
  waiting for transfers between devices  11.9 us (24%)
  starting transfers between devices  7.3 us (15%)
  local copies, waits for them, and re-layouts  0.77 us (2%)
  between operations  0.66 us (1%)
    all_to_all x1, blocking collectives, illumination_sharded(): lax.all_to_all(answer.reshape(devices, block, back_width), axes, 0, 0, ti...  15.1 us
    pallas_call x4, Pallas kernels, call(): pl.pallas_call(kernel, out_shape=outs, in_specs=[pl.BlockSpec(memory_spac...  13.4 us
    all_to_all x1, waiting for transfers between devices, illumination_sharded(): lax.all_to_all(packed.reshape(devices, block, sent_width), axes, 0, 0, ti...  11.9 us
    all_to_all x1, starting transfers between devices, illumination_sharded(): lax.all_to_all(packed.reshape(devices, block, sent_width), axes, 0, 0, ti...  7.3 us
  transfers between devices with their start and end apart: 1, of which 1 were waited for; matrix products, arithmetic and copies ran while one was open for 0% of the time, Pallas kernels for 2%

profile of v1, /device:TPU:0, one launch (start us, length us, event | category | flops | bytes accessed | tf_op | source)
XLA Modules:
  0.0 49.1 jit_solution(13509323470092248832)
XLA Ops:
  0.6 2.1 %pack.1 = bf16[256,896]{1,0:T(8,128)(2,1)} custom-call(bf16[256,512]{1,0:T(8,128)(2,1)} %bitcast.11, f32[2,2,512]{2,1,0:T(2,128)} %reflect_hbm.1, bf16[2,2,12]{2,1,0:T(2,128)(2,1)} %weight_hbm.1, s32[2,2,12]{2,1,0:T(2,128)} %partners_hbm.1, s32[2,2]{1,0:T(2,128)} %count_hbm.1, f32[2,2,3]{2,1,0:T(2,128)} %bitcast.12), custom_call_target="tpu_custom_call" | custom-call | tf_op jit(solution)/shard_map/pack/pallas_call | solution.py:496
  2.7 7.3 %all-to-all-start = ((bf16[32,8,896]{2,1,0:T(8,128)(2,1)}), bf16[32,8,896]{2,1,0:T(8,128)(2,1)S(1)}, u32[]{:S(2)}, u32[]{:S(2)}) async-start(bf16[32,8,896]{2,1,0:T(8,128)(2,1)} %bitcast.8), calls=%async_computation | async-start | bytes 917504 | tf_op jit(solution)/shard_map/all_to_all | solution.py:553
  10.0 1.2 %table.1.long_table = f32[256,512]{1,0:T(8,128)} custom-call(), custom_call_target="tpu_custom_call" | custom-call | flops 10000000 | bytes 1000000 | tf_op jit(solution)/shard_map/table/pallas_call | solution.py:496
  11.2 11.9 %all-to-all-done = bf16[32,8,896]{2,1,0:T(8,128)(2,1)S(1)} async-done(((bf16[32,8,896]{2,1,0:T(8,128)(2,1)}), bf16[32,8,896]{2,1,0:T(8,128)(2,1)S(1)}, u32[]{:S(2)}, u32[]{:S(2)}) %all-to-all-start) | async-done | bytes 458784 | tf_op jit(solution)/shard_map/all_to_all | solution.py:553
  23.1 0.0 copy-start
  23.1 0.8 %copy-done = bf16[32,8,896]{2,1,0:T(8,128)(2,1)} copy-done((bf16[32,8,896]{2,1,0:T(8,128)(2,1)}, bf16[32,8,896]{2,1,0:T(8,128)(2,1)S(1)}, u32[]{:S(2)}) %copy-start) | copy-done | bytes 458776
  23.9 8.2 %bounces.1 = bf16[256,640]{1,0:T(8,128)(2,1)} custom-call(bf16[256,896]{1,0:T(8,128)(2,1)} %bitcast.7, f32[256,512]{1,0:T(8,128)} %table.1.long_table, f32[3,512]{1,0:T(4,128)} %spectral_hbm.1, f32[3,2048]{1,0:T(4,128)} %receiver_hbm.1, bf16[2,512,512]{2,1,0:T(8,128)(2,1)} %rad_hbm.1, bf16[512,2048]{1,0:T(8,128)(2,1)} %far_hbm.1), custom_call_target="tpu_custom_call" | custom-call | tf_op jit(solution)/shard_map/bounces/pallas_call | solution.py:496
  32.1 15.1 %all_to_all.10 = bf16[32,8,640]{2,1,0:T(8,128)(2,1)} all-to-all(bf16[32,8,640]{2,1,0:T(8,128)(2,1)} %bitcast.9), channel_id=1, replica_groups=mesh['px'=8,'py'=4] {'px','py'}, dimensions={0} | all-to-all | bytes 655360 | tf_op jit(solution)/shard_map/all_to_all | solution.py:580
  47.2 1.9 %unpack.1 = (bf16[256,512]{1,0:T(8,128)(2,1)}, f32[8,256]{1,0:T(8,128)}) custom-call(bf16[256,640]{1,0:T(8,128)(2,1)} %bitcast.10), custom_call_target="tpu_custom_call" | custom-call | tf_op jit(solution)/shard_map/unpack/pallas_call | solution.py:496
Async XLA Ops:
  2.7 20.4 %all-to-all-start = ((bf16[32,8,896]{2,1,0:T(8,128)(2,1)}), bf16[32,8,896]{2,1,0:T(8,128)(2,1)S(1)}, u32[]{:S(2)}, u32[]{:S(2)}) async-start(bf16[32,8,896]{2,1,0:T(8,128)(2,1)} %bitcast.8), calls=%async_computation | async-start | bytes 917504 | tf_op jit(solution)/shard_map/all_to_all | solution.py:553
  23.1 0.8 %copy-start = (bf16[32,8,896]{2,1,0:T(8,128)(2,1)}, bf16[32,8,896]{2,1,0:T(8,128)(2,1)S(1)}, u32[]{:S(2)}) copy-start(bf16[32,8,896]{2,1,0:T(8,128)(2,1)S(1)} %all-to-all-done) | copy-start | bytes 1376260

commit v2 on v1

--- a/solution.py
+++ b/solution.py
@@ -20,7 +20,7 @@
 F32 = jnp.float32
 BF16 = jnp.bfloat16
 HIGH = lax.Precision.HIGHEST
-VMEM_LIMIT = 62 * 1024 * 1024
+MIB = 1024 * 1024
 
 
 def padded(block, sides, width, periodic):
@@ -310,48 +310,50 @@
     out[:, :unit_count] = dot(order, cur[...]).astype(BF16)
 
 
-def table_kernel(long_table):
+def table_kernel(rad_hbm, far_hbm, rad, far_map, long_table, sems):
+    copies = fetch([(rad_hbm, rad), (far_hbm, far_map)], sems)
     tile = long_table.shape[0]
     row = lax.broadcasted_iota(jnp.int32, (tile, tile), 0)
     column = lax.broadcasted_iota(jnp.int32, (tile, tile), 1)
     cosine, sine = cos_sin(((row * column) % tile).astype(F32) * (1.0 / tile))
     long_table[:, :tile] = cosine
     long_table[:, tile:] = sine
-
-
-def main_kernel(
-    scale,
-    grid_shape,
-    local_shape,
-    got,
-    long_table,
-    spectral_hbm,
-    receiver_hbm,
-    rad_hbm,
-    far_hbm,
-    out,
-    spectral_dirs,
-    receiver_dirs,
-    rad,
-    far_map,
-    sems,
-):
-    copies = fetch(
-        [
-            (spectral_hbm, spectral_dirs),
-            (rad_hbm, rad),
-            (receiver_hbm, receiver_dirs),
-            (far_hbm, far_map),
-        ],
-        sems,
-    )
+    for copy in copies:
+        copy.wait()
+
+
+def centres_of(small):
+    first = len(OFFSETS)
+    centre = []
+    for d in range(3):
+        at = first + 3 * d
+        value = small[:, at : at + 1] + small[:, at + 1 : at + 2] + small[:, at + 2 : at + 3]
+        centre.append(value * (0.5 / math.pi))
+    return centre
+
+
+def turns(centre, dirs):
+    return centre[0] * dirs[0:1] + centre[1] * dirs[1:2] + centre[2] * dirs[2:3]
+
+
+def spectrum(current, rad):
+    patches = current.shape[0] // 2
+    first_part = dot(current, rad[0])
+    second_part = dot(current, rad[1])
+    return (
+        first_part[:patches] - second_part[patches:],
+        second_part[:patches] + first_part[patches:],
+    )
+
+
+def bounce_kernel(grid_shape, local_shape, got, rad, spectral_dirs, out, last, kept):
     unit_count = rad.shape[1]
     half = unit_count // 2
     rows = got.shape[0]
     patches = rows // 2
     local_rows, local_cols = local_shape
     local = local_rows * local_cols
-    splits, n_py = grid_shape
+    n_px, n_py = grid_shape
     total_cols = n_py * local_cols
     sorted_rows = dot(part_sorter(rows, local, False), got[...])
     start = sorted_rows[:, :unit_count]
@@ -363,22 +365,14 @@
         axis=1,
     )
     small = sorted_rows[:patches, unit_count + half :]
-    first = len(OFFSETS)
-    centre = []
-    for d in range(3):
-        at = first + 3 * d
-        value = small[:, at : at + 1] + small[:, at + 1 : at + 2] + small[:, at + 2 : at + 3]
-        centre.append(value * (0.5 / math.pi))
-
-    def turns(dirs):
-        return centre[0] * dirs[0:1] + centre[1] * dirs[1:2] + centre[2] * dirs[2:3]
+    kept[...] = small
 
     def place(axis):
         ids = lax.broadcasted_iota(jnp.int32, (patches, patches), axis)
         device, within = ids // local, ids % local
         return (
-            device // n_py * local_rows + within // local_cols,
-            device % n_py * local_cols + within % local_cols,
+            device % n_px * local_rows + within // local_cols,
+            device // n_px * local_cols + within % local_cols,
         )
 
     (here_row, here_col), (there_row, there_col) = place(0), place(1)
@@ -394,21 +388,10 @@
     for o in range(len(OFFSETS)):
         coef = jnp.where(offset == o, small[:, o : o + 1], coef)
     coef = coef.astype(BF16)
-    copies[0].wait()
-    cosine, sine = cos_sin(turns(spectral_dirs[...]))
-    copies[1].wait()
-
-    def spectrum(current):
-        first_part = dot(current, rad[0])
-        second_part = dot(current, rad[1])
-        return (
-            first_part[:patches] - second_part[patches:],
-            second_part[:patches] + first_part[patches:],
-        )
-
+    cosine, sine = cos_sin(turns(centres_of(small), spectral_dirs[...]))
     current = start.astype(BF16)
     for _ in range(2):
-        spec_re, spec_im = spectrum(current)
+        spec_re, spec_im = spectrum(current, rad)
         outgoing = jnp.concatenate(
             [spec_re * cosine + spec_im * sine, spec_im * cosine - spec_re * sine], axis=1
         ).astype(BF16)
@@ -426,17 +409,19 @@
         current = jnp.concatenate(
             [start[:patches] + reflect * recv_re, start[patches:] + reflect * recv_im], axis=0
         ).astype(BF16)
-    out[:, :unit_count] = dot(part_sorter(rows, local, True), current).astype(BF16)
-
-    spec_re, spec_im = spectrum(current)
-    final = jnp.concatenate([spec_re, spec_im], axis=0).astype(BF16)
-    copies[2].wait()
-    copies[3].wait()
-    tile = far_map.shape[1] // splits
+    last[...] = current
+    out[...] = dot(part_sorter(rows, local, True), current).astype(BF16)
+
+
+def image_kernel(scale, last, kept, long_table, receiver_dirs, rad, far_map, image):
+    splits, tile = image.shape
+    patches = kept.shape[0]
+    centre = centres_of(kept[...])
+    final = jnp.concatenate(spectrum(last[...], rad), axis=0).astype(BF16)
     far_re, far_im = [], []
     for t in range(splits):
         beams = dot(final, far_map[:, tile * t : tile * (t + 1)])
-        cos_view, sin_view = cos_sin(turns(receiver_dirs[:, tile * t : tile * (t + 1)]))
+        cos_view, sin_view = cos_sin(turns(centre, receiver_dirs[:, tile * t : tile * (t + 1)]))
         beam_re = beams[:patches]
         beam_im = beams[patches:]
         far_re.append(jnp.sum(beam_re * cos_view - beam_im * sin_view, axis=0, keepdims=True))
@@ -460,38 +445,40 @@
     answer = jnp.dot(both, long_table[...], precision=HIGH, preferred_element_type=F32)
     image_re = answer[:splits, :tile] + answer[splits:, tile:]
     image_im = answer[splits:, :tile] - answer[:splits, tile:]
-    image = scale * (image_re * image_re + image_im * image_im)
-    pieces = tile // 128
-    rows_each = rows // pieces
-    for p in range(pieces):
-        piece = image[:, 128 * p : 128 * (p + 1)]
-        piece = jnp.concatenate([piece, piece], axis=0).astype(BF16)
-        for s in range(rows_each // piece.shape[0]):
-            at = p * rows_each + s * piece.shape[0]
-            out[at : at + piece.shape[0], unit_count:] = piece
-
-
-def unpack_kernel(splits, local, got, currents, image):
-    rows, unit_count = currents.shape
+    power = scale * (image_re * image_re + image_im * image_im)
+    each = tile // splits
+    lane = lax.broadcasted_iota(jnp.int32, (splits, tile), 1)
+    row = lax.broadcasted_iota(jnp.int32, (splits, tile), 0)
+    fast = jnp.where(lane % splits == row, 1.0, 0.0)
+    spread = lax.dot_general(
+        power, fast, (((0,), (0,)), ((), ())), precision=HIGH, preferred_element_type=F32
+    )
+    row = lax.broadcasted_iota(jnp.int32, (tile, tile), 0)
+    column = lax.broadcasted_iota(jnp.int32, (tile, tile), 1)
+    spread = jnp.where(row % each == column // splits, spread, 0.0)
+    image[...] = jnp.sum(spread.reshape(splits, each, tile), axis=1)
+
+
+def unpack_kernel(local, got, currents):
+    rows = currents.shape[0]
     order = sorter(rows, rows // (2 * local), local)
-    currents[...] = dot(order, got[:, :unit_count]).astype(BF16)
-    owned, bins = image.shape
-    height = owned * splits
-    each = bins // splits
-    at = pl.multiple_of(lax.axis_index("py") * height, height)
-    lanes_from = lax.axis_index("px") % (128 // each) * each
-    block = got[pl.ds(at, height), unit_count:]
-    lane = lax.broadcasted_iota(jnp.int32, (128, bins), 0)
-    column = lax.broadcasted_iota(jnp.int32, (128, bins), 1)
-    pick = jnp.where(lane == lanes_from + column // splits, 1.0, 0.0).astype(BF16)
-    spread = dot(block, pick)
-    row = lax.broadcasted_iota(jnp.int32, (height, bins), 0)
-    column = lax.broadcasted_iota(jnp.int32, (height, bins), 1)
-    spread = jnp.where(row % splits == column % splits, spread, 0.0)
-    image[...] = jnp.sum(spread.reshape(owned, splits, bins), axis=1)
-
-
-def call(kernel, name, outs, operands, spaces, scratch=(), cost=None):
+    currents[...] = dot(order, got[...]).astype(BF16)
+
+
+def gather_kernel(*refs):
+    pairs, image = refs[:-1], refs[-1]
+    splits = pairs[0].shape[0] // 2
+    me = lax.axis_index("px")
+    row = lax.broadcasted_iota(jnp.int32, image.shape, 0)
+    whole = jnp.zeros(image.shape, F32)
+    for n, pair in enumerate(pairs):
+        for half in range(2):
+            mine = pair[pl.ds(half * splits + me, 1), :]
+            whole = jnp.where(row == (me ^ (2 * n + half)), mine, whole)
+    image[...] = whole
+
+
+def call(kernel, name, outs, operands, spaces, scratch=(), cost=None, limit=62):
     vmem = pl.BlockSpec(memory_space=pltpu.VMEM)
     return pl.pallas_call(
         kernel,
@@ -499,7 +486,7 @@
         in_specs=[pl.BlockSpec(memory_space=m) for m in spaces],
         out_specs=jax.tree.map(lambda _: vmem, outs),
         scratch_shapes=list(scratch),
-        compiler_params=pltpu.CompilerParams(vmem_limit_bytes=VMEM_LIMIT),
+        compiler_params=pltpu.CompilerParams(vmem_limit_bytes=limit * MIB),
         cost_estimate=cost,
         name=name,
     )(*operands)
@@ -527,11 +514,15 @@
     rcv_count = far_map.shape[1]
     tile = rcv_count // n_px
     block = 2 * local
-    axes = ("px", "py")
+    axes = ("py", "px")
     vmem, hbm = pltpu.VMEM, pltpu.HBM
 
-    def like(array):
-        return pltpu.VMEM(array.shape, array.dtype)
+    def like(*arrays):
+        scratch = [pltpu.VMEM(a.shape, a.dtype) for a in arrays]
+        return scratch + [pltpu.SemaphoreType.DMA((len(arrays),))]
+
+    def shape(*dims, dtype=BF16):
+        return jax.ShapeDtypeStruct(dims, dtype)
 
     sent_width = unit_count + unit_count // 2 + 128
     sources = (
@@ -545,49 +536,61 @@
     packed = call(
         functools.partial(pack_kernel, total_cols),
         "pack",
-        jax.ShapeDtypeStruct((rows, sent_width), BF16),
+        shape(rows, sent_width),
         sources,
         [hbm] * 6,
-        [like(s) for s in sources] + [pltpu.SemaphoreType.DMA((6,))],
+        like(*sources),
     )
     got = lax.all_to_all(packed.reshape(devices, block, sent_width), axes, 0, 0, tiled=True)
-    long_table = call(
+    rad, far, long_table = call(
         table_kernel,
         "table",
-        jax.ShapeDtypeStruct((tile, 2 * tile), F32),
-        (),
-        [],
-        cost=pl.CostEstimate(flops=10**7, bytes_accessed=10**6, transcendentals=0),
-    )
-    scale = 0.125 / (patches * rcv_count)
-    back_width = unit_count + 128
-    answer = call(
-        functools.partial(main_kernel, scale, (n_px, n_py), (local_rows, local_cols)),
+        (shape(*rad_pattern.shape), shape(*far_map.shape), shape(tile, 2 * tile, dtype=F32)),
+        (rad_pattern, far_map),
+        [hbm] * 2,
+        [pltpu.SemaphoreType.DMA((2,))],
+        limit=32,
+        cost=pl.CostEstimate(flops=10**7, bytes_accessed=4 * 10**6, transcendentals=0),
+    )
+    answer, last, kept = call(
+        functools.partial(bounce_kernel, (n_px, n_py), (local_rows, local_cols)),
         "bounces",
-        jax.ShapeDtypeStruct((rows, back_width), BF16),
-        (
-            got.reshape(rows, sent_width),
-            long_table,
-            spectral_dirs,
-            receiver_dirs,
-            rad_pattern,
-            far_map,
-        ),
-        [vmem] * 2 + [hbm] * 4,
-        [like(a) for a in (spectral_dirs, receiver_dirs, rad_pattern, far_map)]
-        + [pltpu.SemaphoreType.DMA((4,))],
-    )
-    back = lax.all_to_all(answer.reshape(devices, block, back_width), axes, 0, 0, tiled=True)
-    owned = illum_count // n_py
-    currents, image = call(
-        functools.partial(unpack_kernel, n_px, local),
+        (shape(rows, unit_count), shape(rows, unit_count), shape(patches, 128, dtype=F32)),
+        (got.reshape(rows, sent_width), rad, spectral_dirs),
+        [vmem] * 3,
+        limit=32,
+    )
+    back = lax.all_to_all(answer.reshape(devices, block, unit_count), axes, 0, 0, tiled=True)
+    part = call(
+        functools.partial(image_kernel, 0.125 / (patches * rcv_count)),
+        "image",
+        shape(n_px, tile, dtype=F32),
+        (last, kept, long_table, receiver_dirs, rad, far),
+        [vmem] * 6,
+        cost=pl.CostEstimate(flops=2 * 10**9, bytes_accessed=4 * 10**6, transcendentals=0),
+        limit=32,
+    )
+
+    def swapped(array, bits):
+        return lax.ppermute(array, "px", [(i, i ^ bits) for i in range(n_px)])
+
+    pair = jnp.concatenate([part, swapped(part, 1)], axis=0)
+    pairs = [pair] + [swapped(pair, bits) for bits in range(2, n_px, 2)]
+    image = call(
+        gather_kernel,
+        "gather",
+        shape(illum_count // n_py, tile, dtype=F32),
+        pairs,
+        [vmem] * len(pairs),
+        limit=16,
+    )
+    currents = call(
+        functools.partial(unpack_kernel, local),
         "unpack",
-        (
-            jax.ShapeDtypeStruct((rows, unit_count), BF16),
-            jax.ShapeDtypeStruct((owned, tile), F32),
-        ),
-        (back.reshape(rows, back_width),),
+        shape(rows, unit_count),
+        (back.reshape(rows, unit_count),),
         [vmem],
+        limit=16,
     )
     return (currents.reshape(currents_in.shape), image)
 
@@ -603,7 +606,6 @@
             and n_px == 8
             and unit_count % 256 == 0
             and far_map.shape[1] == n_px * 256
-            and illum_count % n_py == 0
             and total_cols > 2 * COL_REACH
         )
 

time: 49.9 us -> 46 us (0.922)
  blocking collectives: 15.1 us -> 0 us
  starting transfers between devices: 7.3 us -> 14 us
  local copies, waits for them, and re-layouts: 0.77 us -> 4.51 us
  waiting for transfers between devices: 11.9 us -> 15.2 us
  Pallas kernels: 13.4 us -> 11.3 us
    all_to_all x1 -> x0, blocking collectives: 15.1 us -> none  [illumination_sharded(): lax.all_to_all(answer.reshape(devices, block, back_width), axes, 0, 0, ti...]
    ppermute x0 -> x4, waiting for transfers between devices: none -> 4.39 us  [swapped(): return lax.ppermute(array, 'px', [(i, i ^ bits) for i in range(n_px)])]
    ppermute x0 -> x4, starting transfers between devices: none -> 3.8 us  [swapped(): return lax.ppermute(array, 'px', [(i, i ^ bits) for i in range(n_px)])]
    unnamed x2 -> x12, local copies, waits for them, and re-layouts: 0.77 us -> 4.51 us
    all_to_all x0 -> x1, starting transfers between devices: none -> 2.87 us  [illumination_sharded(): lax.all_to_all(answer.reshape(devices, block, unit_count), axes, 0, 0, ti...]
    pallas_call x4 -> x6, Pallas kernels: 13.4 us -> 11.3 us  [call(): pl.pallas_call(kernel, out_shape=outs, in_specs=[pl.BlockSpec(memory_spac...]
    all_to_all x1, waiting for transfers between devices: 11.9 us -> 10.8 us  [illumination_sharded(): lax.all_to_all(packed.reshape(devices, block, sent_width), axes, 0, 0, ti...]
  transfers between devices with their start and end apart: 1 -> 6, of which waited for: 1 -> 5; matrix products, arithmetic and copies ran while one was open for 0% -> 0% of each run, Pallas kernels for 2% -> 10%
where the time goes in v2:
time: 46 us; the launch traced here: 45.6 us
  waiting for transfers between devices  15.2 us (33%)
  starting transfers between devices  14 us (30%)
  Pallas kernels  11.3 us (25%)
  local copies, waits for them, and re-layouts  4.51 us (10%)
  between operations  0.74 us (2%)
    pallas_call x6, Pallas kernels, call(): pl.pallas_call(kernel, out_shape=outs, in_specs=[pl.BlockSpec(memory_spac...  11.3 us
    all_to_all x1, waiting for transfers between devices, illumination_sharded(): lax.all_to_all(packed.reshape(devices, block, sent_width), axes, 0, 0, ti...  10.8 us
    all_to_all x1, starting transfers between devices, illumination_sharded(): lax.all_to_all(packed.reshape(devices, block, sent_width), axes, 0, 0, ti...  7.3 us
    unnamed x12, local copies, waits for them, and re-layouts  4.51 us
    ppermute x4, waiting for transfers between devices, swapped(): return lax.ppermute(array, 'px', [(i, i ^ bits) for i in range(n_px)])  4.39 us
    ppermute x4, starting transfers between devices, swapped(): return lax.ppermute(array, 'px', [(i, i ^ bits) for i in range(n_px)])  3.8 us
    all_to_all x1, starting transfers between devices, illumination_sharded(): lax.all_to_all(answer.reshape(devices, block, unit_count), axes, 0, 0, ti...  2.87 us
  transfers between devices with their start and end apart: 6, of which 5 were waited for; matrix products, arithmetic and copies ran while one was open for 0% of the time, Pallas kernels for 10%

profile of v2, /device:TPU:0, one launch (start us, length us, event | category | flops | bytes accessed | tf_op | source)
XLA Modules:
  0.0 45.6 jit_solution(9237643750198038878)
XLA Ops:
  0.6 0.0 copy-start.1
  0.6 2.2 %pack.1 = bf16[256,896]{1,0:T(8,128)(2,1)} custom-call(bf16[256,512]{1,0:T(8,128)(2,1)} %bitcast.10, f32[2,2,512]{2,1,0:T(2,128)} %reflect_hbm.1, bf16[2,2,12]{2,1,0:T(2,128)(2,1)} %weight_hbm.1, s32[2,2,12]{2,1,0:T(2,128)} %partners_hbm.1, s32[2,2]{1,0:T(2,128)} %count_hbm.1, f32[2,2,3]{2,1,0:T(2,128)} %bitcast.12), custom_call_target="tpu_custom_call" | custom-call | tf_op jit(solution)/shard_map/pack/pallas_call | solution.py:483
  2.8 0.0 copy-start.2
  2.8 7.3 %all-to-all-start = ((bf16[32,8,896]{2,1,0:T(8,128)(2,1)}), bf16[32,8,896]{2,1,0:T(8,128)(2,1)S(1)}, u32[]{:S(2)}, u32[]{:S(2)}) async-start(bf16[32,8,896]{2,1,0:T(8,128)(2,1)} %bitcast.9), calls=%async_computation | async-start | bytes 917504 | tf_op jit(solution)/shard_map/all_to_all | solution.py:544
  10.1 0.0 copy-done.1
  10.2 0.0 copy-start
  10.2 1.6 %copy-done = bf16[512,2048]{1,0:T(8,128)(2,1)S(1)} copy-done((bf16[512,2048]{1,0:T(8,128)(2,1)S(1)}, bf16[512,2048]{1,0:T(8,128)(2,1)}, u32[]{:S(2)}) %copy-start) | copy-done | bytes 2097176
  11.7 0.0 copy-start.5
  11.8 0.6 %table.1 = (bf16[2,512,512]{2,1,0:T(8,128)(2,1)S(1)}, bf16[512,2048]{1,0:T(8,128)(2,1)S(1)}, f32[256,512]{1,0:T(8,128)S(1)}) custom-call(bf16[2,512,512]{2,1,0:T(8,128)(2,1)S(1)} %copy-done.1, bf16[512,2048]{1,0:T(8,128)(2,1)S(1)} %copy-done), custom_call_target="tpu_custom_call" | custom-call | flops 10000000 | bytes 4000000 | tf_op jit(solution)/shard_map/table/pallas_call | solution.py:483
  12.4 0.0 copy-start.3
  12.4 1.3 %copy-done.3 = bf16[512,2048]{1,0:T(8,128)(2,1)} copy-done((bf16[512,2048]{1,0:T(8,128)(2,1)}, bf16[512,2048]{1,0:T(8,128)(2,1)S(1)}, u32[]{:S(2)}) %copy-start.3) | copy-done | bytes 2097176
  13.7 10.8 %all-to-all-done = bf16[32,8,896]{2,1,0:T(8,128)(2,1)S(1)} async-done(((bf16[32,8,896]{2,1,0:T(8,128)(2,1)}), bf16[32,8,896]{2,1,0:T(8,128)(2,1)S(1)}, u32[]{:S(2)}, u32[]{:S(2)}) %all-to-all-start) | async-done | bytes 458784 | tf_op jit(solution)/shard_map/all_to_all | solution.py:544
  24.5 0.0 copy-done.2
  24.5 3.5 %bounces.1 = (bf16[256,512]{1,0:T(8,128)(2,1)}, bf16[256,512]{1,0:T(8,128)(2,1)S(1)}, f32[128,128]{1,0:T(8,128)S(1)}) custom-call(bf16[256,896]{1,0:T(8,128)(2,1)S(1)} %bitcast.7, bf16[2,512,512]{2,1,0:T(8,128)(2,1)S(1)} %get-tuple-element.8.rad, f32[3,512]{1,0:T(4,128)S(1)} %copy-done.2), custom_call_target="tpu_custom_call" | custom-call | tf_op jit(solution)/shard_map/bounces/pallas_call | solution.py:483
  28.0 2.9 %all-to-all-start.1 = ((bf16[32,8,512]{2,1,0:T(8,128)(2,1)}), bf16[32,8,512]{2,1,0:T(8,128)(2,1)S(1)}, u32[]{:S(2)}, u32[]{:S(2)}) async-start(bf16[32,8,512]{2,1,0:T(8,128)(2,1)} %bitcast.4), calls=%async_computation.1 | async-start | bytes 524288 | tf_op jit(solution)/shard_map/all_to_all | solution.py:563
  30.9 0.0 copy-done.5
  30.9 0.0 copy-start.4
  30.9 1.6 %copy-done.4 = bf16[512,2048]{1,0:T(8,128)(2,1)S(1)} copy-done((bf16[512,2048]{1,0:T(8,128)(2,1)S(1)}, bf16[512,2048]{1,0:T(8,128)(2,1)}, u32[]{:S(2)}) %copy-start.4) | copy-done | bytes 2097176
  32.5 3.4 %image.1 = f32[8,256]{1,0:T(8,128)S(1)} custom-call(bf16[256,512]{1,0:T(8,128)(2,1)S(1)} %get-tuple-element.10.last, f32[128,128]{1,0:T(8,128)S(1)} %get-tuple-element.11.kept, f32[256,512]{1,0:T(8,128)S(1)} %get-tuple-element.12.long_table, f32[3,2048]{1,0:T(4,128)S(1)} %copy-done.5, bf16[2,512,512]{2,1,0:T(8,128)(2,1)S(1)} %get-tuple-element.8.rad, ...), custom_call_target="tpu_custom_call" | custom-call | flops 2000000000 | bytes 4000000 | tf_op jit(solution)/shard_map/image/pallas_call | solution.py:483
  35.9 0.3 collective-permute-start
  36.2 0.9 %collective-permute-done = f32[8,256]{1,0:T(8,128)S(1)} collective-permute-done((f32[8,256]{1,0:T(8,128)S(1)}, f32[8,256]{1,0:T(8,128)S(1)}, u32[]{:S(2)}, u32[]{:S(2)}) %collective-permute-start) | collective-permute-done | bytes 8224 | tf_op jit(solution)/shard_map/ppermute | solution.py:575
  37.1 2.7 %collective-permute-start.3 = (f32[16,256]{1,0:T(8,128)S(1)}, f32[16,256]{1,0:T(8,128)S(1)}, u32[]{:S(2)}, u32[]{:S(2)}) collective-permute-start(f32[16,256]{1,0:T(8,128)S(1)} %pad_maximum_fusion.refs_0_), channel_id=1, source_target_pairs={{0,24},{4,28},{8,16},{12,20},{16,8},{20,12},{24,0},{28,4},{1,25},{... | collective-permute-start | bytes 49160 | tf_op jit(solution)/shard_map/ppermute | solution.py:575
  39.8 0.6 %collective-permute-start.2 = (f32[16,256]{1,0:T(8,128)S(1)}, f32[16,256]{1,0:T(8,128)S(1)}, u32[]{:S(2)}, u32[]{:S(2)}) collective-permute-start(f32[16,256]{1,0:T(8,128)S(1)} %pad_maximum_fusion.refs_0_), channel_id=1, source_target_pairs={{0,16},{4,20},{8,24},{12,28},{16,0},{20,4},{24,8},{28,12},{1,17},{... | collective-permute-start | bytes 49160 | tf_op jit(solution)/shard_map/ppermute | solution.py:575
  40.4 0.3 collective-permute-start.1
  40.6 1.1 %collective-permute-done.3.refs_3_ = f32[16,256]{1,0:T(8,128)S(1)} collective-permute-done((f32[16,256]{1,0:T(8,128)S(1)}, f32[16,256]{1,0:T(8,128)S(1)}, u32[]{:S(2)}, u32[]{:S(2)}) %collective-permute-start.3) | collective-permute-done | bytes 16416 | tf_op jit(solution)/shard_map/ppermute | solution.py:575
  41.8 1.8 %collective-permute-done.2.refs_2_ = f32[16,256]{1,0:T(8,128)S(1)} collective-permute-done((f32[16,256]{1,0:T(8,128)S(1)}, f32[16,256]{1,0:T(8,128)S(1)}, u32[]{:S(2)}, u32[]{:S(2)}) %collective-permute-start.2) | collective-permute-done | bytes 16416 | tf_op jit(solution)/shard_map/ppermute | solution.py:575
  43.5 0.6 %collective-permute-done.1.refs_1_ = f32[16,256]{1,0:T(8,128)S(1)} collective-permute-done((f32[16,256]{1,0:T(8,128)S(1)}, f32[16,256]{1,0:T(8,128)S(1)}, u32[]{:S(2)}, u32[]{:S(2)}) %collective-permute-start.1) | collective-permute-done | bytes 16416 | tf_op jit(solution)/shard_map/ppermute | solution.py:575
  44.1 0.6 %gather.1 = f32[8,256]{1,0:T(8,128)} custom-call(f32[16,256]{1,0:T(8,128)S(1)} %pad_maximum_fusion.refs_0_, f32[16,256]{1,0:T(8,128)S(1)} %collective-permute-done.1.refs_1_, f32[16,256]{1,0:T(8,128)S(1)} %collective-permute-done.2.refs_2_, f32[16,256]{1,0:T(8,128)S(1)} %collective-permute-done.3.refs_3_), custom_call_target="tpu_custom_call" | custom-call | tf_op jit(solution)/shard_map/gather/pallas_call | solution.py:483
  44.7 0.0 all-to-all-done.1
  44.7 0.9 %unpack.1 = bf16[256,512]{1,0:T(8,128)(2,1)} custom-call(bf16[256,512]{1,0:T(8,128)(2,1)S(1)} %bitcast.8), custom_call_target="tpu_custom_call" | custom-call | tf_op jit(solution)/shard_map/unpack/pallas_call | solution.py:483
  (1 shorter events, 0.0 us)
Async XLA Ops:
  0.6 9.5 %copy-start.1 = (bf16[2,512,512]{2,1,0:T(8,128)(2,1)S(1)}, bf16[2,512,512]{2,1,0:T(8,128)(2,1)}, u32[]{:S(2)}) copy-start(bf16[2,512,512]{2,1,0:T(8,128)(2,1)} %rad_hbm.1) | copy-start | bytes 3145732
  2.8 21.7 %copy-start.2 = (f32[3,512]{1,0:T(4,128)S(1)}, f32[3,512]{1,0:T(4,128)}, u32[]{:S(2)}) copy-start(f32[3,512]{1,0:T(4,128)} %spectral_dirs.1) | copy-start | bytes 18436
  2.8 21.7 %all-to-all-start = ((bf16[32,8,896]{2,1,0:T(8,128)(2,1)}), bf16[32,8,896]{2,1,0:T(8,128)(2,1)S(1)}, u32[]{:S(2)}, u32[]{:S(2)}) async-start(bf16[32,8,896]{2,1,0:T(8,128)(2,1)} %bitcast.9), calls=%async_computation | async-start | bytes 917504 | tf_op jit(solution)/shard_map/all_to_all | solution.py:544
  10.2 1.6 %copy-start = (bf16[512,2048]{1,0:T(8,128)(2,1)S(1)}, bf16[512,2048]{1,0:T(8,128)(2,1)}, u32[]{:S(2)}) copy-start(bf16[512,2048]{1,0:T(8,128)(2,1)} %far_hbm.1) | copy-start | bytes 6291460
  11.7 19.1 %copy-start.5 = (f32[3,2048]{1,0:T(4,128)S(1)}, f32[3,2048]{1,0:T(4,128)}, u32[]{:S(2)}) copy-start(f32[3,2048]{1,0:T(4,128)} %receiver_dirs.1) | copy-start | bytes 73732
  12.4 1.3 %copy-start.3 = (bf16[512,2048]{1,0:T(8,128)(2,1)}, bf16[512,2048]{1,0:T(8,128)(2,1)S(1)}, u32[]{:S(2)}) copy-start(bf16[512,2048]{1,0:T(8,128)(2,1)S(1)} %get-tuple-element.13.far_map) | copy-start | bytes 6291460
  28.0 16.7 %all-to-all-start.1 = ((bf16[32,8,512]{2,1,0:T(8,128)(2,1)}), bf16[32,8,512]{2,1,0:T(8,128)(2,1)S(1)}, u32[]{:S(2)}, u32[]{:S(2)}) async-start(bf16[32,8,512]{2,1,0:T(8,128)(2,1)} %bitcast.4), calls=%async_computation.1 | async-start | bytes 524288 | tf_op jit(solution)/shard_map/all_to_all | solution.py:563
  30.9 1.6 %copy-start.4 = (bf16[512,2048]{1,0:T(8,128)(2,1)S(1)}, bf16[512,2048]{1,0:T(8,128)(2,1)}, u32[]{:S(2)}) copy-start(bf16[512,2048]{1,0:T(8,128)(2,1)} %copy-done.3) | copy-start | bytes 6291460
  35.9 1.2 %collective-permute-start = (f32[8,256]{1,0:T(8,128)S(1)}, f32[8,256]{1,0:T(8,128)S(1)}, u32[]{:S(2)}, u32[]{:S(2)}) collective-permute-start(f32[8,256]{1,0:T(8,128)S(1)} %image.1), channel_id=1, source_target_pairs={{0,4},{4,0},{8,12},{12,8},{16,20},{20,16},{24,28},{28,24},{1,5},{5... | collective-permute-start | bytes 24584 | tf_op jit(solution)/shard_map/ppermute | solution.py:575
  37.1 4.6 %collective-permute-start.3 = (f32[16,256]{1,0:T(8,128)S(1)}, f32[16,256]{1,0:T(8,128)S(1)}, u32[]{:S(2)}, u32[]{:S(2)}) collective-permute-start(f32[16,256]{1,0:T(8,128)S(1)} %pad_maximum_fusion.refs_0_), channel_id=1, source_target_pairs={{0,24},{4,28},{8,16},{12,20},{16,8},{20,12},{24,0},{28,4},{1,25},{... | collective-permute-start | bytes 49160 | tf_op jit(solution)/shard_map/ppermute | solution.py:575
  39.8 3.7 %collective-permute-start.2 = (f32[16,256]{1,0:T(8,128)S(1)}, f32[16,256]{1,0:T(8,128)S(1)}, u32[]{:S(2)}, u32[]{:S(2)}) collective-permute-start(f32[16,256]{1,0:T(8,128)S(1)} %pad_maximum_fusion.refs_0_), channel_id=1, source_target_pairs={{0,16},{4,20},{8,24},{12,28},{16,0},{20,4},{24,8},{28,12},{1,17},{... | collective-permute-start | bytes 49160 | tf_op jit(solution)/shard_map/ppermute | solution.py:575
  40.4 3.7 %collective-permute-start.1 = (f32[16,256]{1,0:T(8,128)S(1)}, f32[16,256]{1,0:T(8,128)S(1)}, u32[]{:S(2)}, u32[]{:S(2)}) collective-permute-start(f32[16,256]{1,0:T(8,128)S(1)} %pad_maximum_fusion.refs_0_), channel_id=1, source_target_pairs={{0,8},{4,12},{8,0},{12,4},{16,24},{20,28},{24,16},{28,20},{1,9},{5... | collective-permute-start | bytes 49160 | tf_op jit(solution)/shard_map/ppermute | solution.py:575

commit v3 on v2

--- a/solution.py
+++ b/solution.py
@@ -172,8 +172,8 @@
     cosine = np.cos(2 * np.pi * np.sqrt(grid))
     make = np.polynomial.chebyshev.Chebyshev.fit
     power = np.polynomial.Polynomial
-    sine_fit = make(grid, sine_over, 6).convert(kind=power).coef
-    cosine_fit = make(grid, cosine, 7).convert(kind=power).coef
+    sine_fit = make(grid, sine_over, 5).convert(kind=power).coef
+    cosine_fit = make(grid, cosine, 6).convert(kind=power).coef
     return [float(c) for c in sine_fit], [float(c) for c in cosine_fit]
 
 
@@ -201,13 +201,18 @@
     return lax.dot_general(left, right, (((1,), (1,)), ((), ())), preferred_element_type=F32)
 
 
-def sorter(rows, outer, inner):
+def sorter(rows, outer, inner, outer_at=lambda o: o, inner_at=lambda i: i):
     out_id = lax.broadcasted_iota(jnp.int32, (rows, rows), 0)
     in_id = lax.broadcasted_iota(jnp.int32, (rows, rows), 1)
     i = out_id // (2 * outer)
     part = (out_id // outer) % 2
     o = out_id % outer
-    return jnp.where(in_id == (o * 2 + part) * inner + i, 1.0, 0.0).astype(BF16)
+    column = (outer_at(o) * 2 + part) * inner + inner_at(i)
+    return jnp.where(in_id == column, 1.0, 0.0).astype(BF16)
+
+
+def swapped_digits(value, high, low):
+    return value % low * high + value // low
 
 
 def part_sorter(rows, inner, back):
@@ -232,6 +237,7 @@
 
 def pack_kernel(
     total_cols,
+    grid_shape,
     cur_hbm,
     reflect_hbm,
     weight_hbm,
@@ -249,12 +255,12 @@
 ):
     copies = fetch(
         [
+            (cur_hbm, cur),
+            (reflect_hbm, reflect),
             (partners_hbm, partners),
             (weight_hbm, weight),
             (count_hbm, count),
             (centres_hbm, centres),
-            (reflect_hbm, reflect),
-            (cur_hbm, cur),
         ],
         sems,
     )
@@ -264,7 +270,9 @@
     half = unit_count // 2
     base_row = lax.axis_index("px") * local_rows
     base_col = lax.axis_index("py") * local_cols
-    order = sorter(rows, local, rows // (2 * local))
+    order = sorter(
+        rows, local, rows // (2 * local), inner_at=lambda i: swapped_digits(i, *grid_shape)
+    )
     lane = lax.broadcasted_iota(jnp.int32, (local, 128), 1)
     row = lax.broadcasted_iota(jnp.int32, (local, 128), 0)
     patch_row = base_row + row // local_cols
@@ -275,7 +283,7 @@
         col = jnp.where(col < 0, col + total_cols, col)
         col = jnp.where(col >= total_cols, col - total_cols, col)
         target = jnp.where(lane == o, (patch_row + a) * total_cols + col, target)
-    for copy in copies[:5]:
+    for copy in copies[1:]:
         copy.wait()
     ids = partners[...].reshape(local, SLOTS)
     weights = weight[...].astype(F32).reshape(local, SLOTS)
@@ -306,18 +314,18 @@
     step = tail.shape[0]
     for s in range(rows // step):
         out[step * s : step * (s + 1), unit_count:] = tail
-    copies[5].wait()
+    copies[0].wait()
     out[:, :unit_count] = dot(order, cur[...]).astype(BF16)
 
 
-def table_kernel(rad_hbm, far_hbm, rad, far_map, long_table, sems):
-    copies = fetch([(rad_hbm, rad), (far_hbm, far_map)], sems)
+def table_kernel(rad_hbm, rad, long_table, sems):
+    copies = fetch([(rad_hbm, rad)], sems)
     tile = long_table.shape[0]
     row = lax.broadcasted_iota(jnp.int32, (tile, tile), 0)
     column = lax.broadcasted_iota(jnp.int32, (tile, tile), 1)
     cosine, sine = cos_sin(((row * column) % tile).astype(F32) * (1.0 / tile))
-    long_table[:, :tile] = cosine
-    long_table[:, tile:] = sine
+    long_table[:, :tile] = cosine.astype(BF16)
+    long_table[:, tile:] = sine.astype(BF16)
     for copy in copies:
         copy.wait()
 
@@ -371,8 +379,8 @@
         ids = lax.broadcasted_iota(jnp.int32, (patches, patches), axis)
         device, within = ids // local, ids % local
         return (
-            device % n_px * local_rows + within // local_cols,
-            device // n_px * local_cols + within % local_cols,
+            device // n_py * local_rows + within // local_cols,
+            device % n_py * local_cols + within % local_cols,
         )
 
     (here_row, here_col), (there_row, there_col) = place(0), place(1)
@@ -413,19 +421,26 @@
     out[...] = dot(part_sorter(rows, local, True), current).astype(BF16)
 
 
-def image_kernel(scale, last, kept, long_table, receiver_dirs, rad, far_map, image):
+def image_kernel(
+    scale, last, kept, long_table, receiver_dirs, rad, far_hbm, image, far_map, cos_view, sin_view, sems
+):
+    copies = fetch([(far_hbm, far_map)], sems)
     splits, tile = image.shape
     patches = kept.shape[0]
     centre = centres_of(kept[...])
+    cuts = [slice(tile * t, tile * (t + 1)) for t in range(splits)]
+    for cut in cuts:
+        cos_view[:, cut], sin_view[:, cut] = cos_sin(turns(centre, receiver_dirs[:, cut]))
     final = jnp.concatenate(spectrum(last[...], rad), axis=0).astype(BF16)
+    copies[0].wait()
     far_re, far_im = [], []
-    for t in range(splits):
-        beams = dot(final, far_map[:, tile * t : tile * (t + 1)])
-        cos_view, sin_view = cos_sin(turns(centre, receiver_dirs[:, tile * t : tile * (t + 1)]))
+    for cut in cuts:
+        beams = dot(final, far_map[:, cut])
+        c, s = cos_view[:, cut], sin_view[:, cut]
         beam_re = beams[:patches]
         beam_im = beams[patches:]
-        far_re.append(jnp.sum(beam_re * cos_view - beam_im * sin_view, axis=0, keepdims=True))
-        far_im.append(jnp.sum(beam_re * sin_view + beam_im * cos_view, axis=0, keepdims=True))
+        far_re.append(jnp.sum(beam_re * c - beam_im * s, axis=0, keepdims=True))
+        far_im.append(jnp.sum(beam_re * s + beam_im * c, axis=0, keepdims=True))
     row = lax.broadcasted_iota(jnp.int32, (splits, 128), 0)
     column = lax.broadcasted_iota(jnp.int32, (splits, 128), 1)
     short_cos, short_sin = cos_sin((row * column % splits).astype(F32) * (1.0 / splits))
@@ -442,7 +457,10 @@
     tw_re = mid_re * twist_cos + mid_im * twist_sin
     tw_im = mid_im * twist_cos - mid_re * twist_sin
     both = jnp.concatenate([tw_re, tw_im], axis=0)
-    answer = jnp.dot(both, long_table[...], precision=HIGH, preferred_element_type=F32)
+    upper = both.astype(BF16)
+    lower = (both - upper.astype(F32)).astype(BF16)
+    answer = dot(jnp.concatenate([upper, lower], axis=0), long_table[...])
+    answer = answer[: 2 * splits] + answer[2 * splits :]
     image_re = answer[:splits, :tile] + answer[splits:, tile:]
     image_im = answer[splits:, :tile] - answer[:splits, tile:]
     power = scale * (image_re * image_re + image_im * image_im)
@@ -459,27 +477,29 @@
     image[...] = jnp.sum(spread.reshape(splits, each, tile), axis=1)
 
 
-def unpack_kernel(local, got, currents):
+def unpack_kernel(local, grid_shape, got, *refs):
+    pairs, (currents, image) = refs[:-2], refs[-2:]
     rows = currents.shape[0]
-    order = sorter(rows, rows // (2 * local), local)
+    n_px, n_py = grid_shape
+    order = sorter(
+        rows, rows // (2 * local), local, outer_at=lambda o: swapped_digits(o, n_py, n_px)
+    )
     currents[...] = dot(order, got[...]).astype(BF16)
-
-
-def gather_kernel(*refs):
-    pairs, image = refs[:-1], refs[-1]
-    splits = pairs[0].shape[0] // 2
     me = lax.axis_index("px")
     row = lax.broadcasted_iota(jnp.int32, image.shape, 0)
     whole = jnp.zeros(image.shape, F32)
-    for n, pair in enumerate(pairs):
-        for half in range(2):
-            mine = pair[pl.ds(half * splits + me, 1), :]
-            whole = jnp.where(row == (me ^ (2 * n + half)), mine, whole)
+    for n in range(n_px):
+        mine = pairs[n // 2][pl.ds(n % 2 * n_px + me, 1), :]
+        whole = jnp.where(row == (me ^ n), mine, whole)
     image[...] = whole
 
 
-def call(kernel, name, outs, operands, spaces, scratch=(), cost=None, limit=62):
+def call(kernel, name, outs, operands, spaces, scratch=(), cost=None, limit=32):
     vmem = pl.BlockSpec(memory_space=pltpu.VMEM)
+    operands = [
+        pltpu.with_memory_space_constraint(a, pltpu.HBM) if m is pltpu.HBM else a
+        for a, m in zip(operands, spaces)
+    ]
     return pl.pallas_call(
         kernel,
         out_shape=outs,
@@ -514,7 +534,7 @@
     rcv_count = far_map.shape[1]
     tile = rcv_count // n_px
     block = 2 * local
-    axes = ("py", "px")
+    axes = ("px", "py")
     vmem, hbm = pltpu.VMEM, pltpu.HBM
 
     def like(*arrays):
@@ -534,7 +554,7 @@
         jnp.transpose(centres, (1, 2, 0)),
     )
     packed = call(
-        functools.partial(pack_kernel, total_cols),
+        functools.partial(pack_kernel, total_cols, (n_px, n_py)),
         "pack",
         shape(rows, sent_width),
         sources,
@@ -542,14 +562,13 @@
         like(*sources),
     )
     got = lax.all_to_all(packed.reshape(devices, block, sent_width), axes, 0, 0, tiled=True)
-    rad, far, long_table = call(
+    rad, long_table = call(
         table_kernel,
         "table",
-        (shape(*rad_pattern.shape), shape(*far_map.shape), shape(tile, 2 * tile, dtype=F32)),
-        (rad_pattern, far_map),
-        [hbm] * 2,
-        [pltpu.SemaphoreType.DMA((2,))],
-        limit=32,
+        (shape(*rad_pattern.shape), shape(tile, 2 * tile)),
+        (rad_pattern,),
+        [hbm],
+        [pltpu.SemaphoreType.DMA((1,))],
         cost=pl.CostEstimate(flops=10**7, bytes_accessed=4 * 10**6, transcendentals=0),
     )
     answer, last, kept = call(
@@ -558,17 +577,21 @@
         (shape(rows, unit_count), shape(rows, unit_count), shape(patches, 128, dtype=F32)),
         (got.reshape(rows, sent_width), rad, spectral_dirs),
         [vmem] * 3,
-        limit=32,
     )
     back = lax.all_to_all(answer.reshape(devices, block, unit_count), axes, 0, 0, tiled=True)
     part = call(
         functools.partial(image_kernel, 0.125 / (patches * rcv_count)),
         "image",
         shape(n_px, tile, dtype=F32),
-        (last, kept, long_table, receiver_dirs, rad, far),
-        [vmem] * 6,
+        (last, kept, long_table, receiver_dirs, rad, far_map),
+        [vmem] * 5 + [hbm],
+        [
+            pltpu.VMEM(far_map.shape, BF16),
+            pltpu.VMEM((patches, rcv_count), F32),
+            pltpu.VMEM((patches, rcv_count), F32),
+            pltpu.SemaphoreType.DMA((1,)),
+        ],
         cost=pl.CostEstimate(flops=2 * 10**9, bytes_accessed=4 * 10**6, transcendentals=0),
-        limit=32,
     )
 
     def swapped(array, bits):
@@ -576,21 +599,12 @@
 
     pair = jnp.concatenate([part, swapped(part, 1)], axis=0)
     pairs = [pair] + [swapped(pair, bits) for bits in range(2, n_px, 2)]
-    image = call(
-        gather_kernel,
-        "gather",
-        shape(illum_count // n_py, tile, dtype=F32),
-        pairs,
-        [vmem] * len(pairs),
-        limit=16,
-    )
-    currents = call(
-        functools.partial(unpack_kernel, local),
+    currents, image = call(
+        functools.partial(unpack_kernel, local, (n_px, n_py)),
         "unpack",
-        shape(rows, unit_count),
-        (back.reshape(rows, unit_count),),
-        [vmem],
-        limit=16,
+        (shape(rows, unit_count), shape(illum_count // n_py, tile, dtype=F32)),
+        (back.reshape(rows, unit_count), *pairs),
+        [vmem] * (1 + len(pairs)),
     )
     return (currents.reshape(currents_in.shape), image)
 

time: 46 us -> 43.7 us (0.950)
  local copies, waits for them, and re-layouts: 4.51 us -> 0.01 us
  waiting for transfers between devices: 15.2 us -> 16.3 us
  starting transfers between devices: 14 us -> 15.1 us
    unnamed x12 -> x4, local copies, waits for them, and re-layouts: 4.51 us -> 0.01 us
    all_to_all x1, starting transfers between devices: 2.87 us -> 3.97 us  [illumination_sharded(): lax.all_to_all(answer.reshape(devices, block, unit_count), axes, 0, 0, ti...]
    all_to_all x1, waiting for transfers between devices: 10.8 us -> 11.9 us  [illumination_sharded(): lax.all_to_all(packed.reshape(devices, block, sent_width), axes, 0, 0, ti...]
    pallas_call x6 -> x5, Pallas kernels: 11.3 us -> 11.3 us  [call(): pl.pallas_call(kernel, out_shape=outs, in_specs=[pl.BlockSpec(memory_spac...]
  transfers between devices with their start and end apart: 6 -> 6, of which waited for: 5 -> 5; matrix products, arithmetic and copies ran while one was open for 0% -> 0% of each run, Pallas kernels for 10% -> 11%
where the time goes in v3:
time: 43.7 us; the launch traced here: 43.3 us
  waiting for transfers between devices  16.3 us (37%)
  starting transfers between devices  15.1 us (35%)
  Pallas kernels  11.3 us (26%)
  between operations  0.7 us (2%)
    all_to_all x1, waiting for transfers between devices, illumination_sharded(): lax.all_to_all(packed.reshape(devices, block, sent_width), axes, 0, 0, ti...  11.9 us
    pallas_call x5, Pallas kernels, call(): pl.pallas_call(kernel, out_shape=outs, in_specs=[pl.BlockSpec(memory_spac...  11.3 us
    all_to_all x1, starting transfers between devices, illumination_sharded(): lax.all_to_all(packed.reshape(devices, block, sent_width), axes, 0, 0, ti...  7.3 us
    ppermute x4, waiting for transfers between devices, swapped(): return lax.ppermute(array, 'px', [(i, i ^ bits) for i in range(n_px)])  4.4 us
    all_to_all x1, starting transfers between devices, illumination_sharded(): lax.all_to_all(answer.reshape(devices, block, unit_count), axes, 0, 0, ti...  3.97 us
    ppermute x4, starting transfers between devices, swapped(): return lax.ppermute(array, 'px', [(i, i ^ bits) for i in range(n_px)])  3.8 us
  transfers between devices with their start and end apart: 6, of which 5 were waited for; matrix products, arithmetic and copies ran while one was open for 0% of the time, Pallas kernels for 11%

profile of v3, /device:TPU:0, one launch (start us, length us, event | category | flops | bytes accessed | tf_op | source)
XLA Modules:
  0.0 43.3 jit_solution(11517880366268133030)
XLA Ops:
  0.6 0.0 copy-start
  0.6 2.1 %pack.1 = bf16[256,896]{1,0:T(8,128)(2,1)} custom-call(bf16[256,512]{1,0:T(8,128)(2,1)} %bitcast.9, f32[2,2,512]{2,1,0:T(2,128)} %reflect_hbm.1, bf16[2,2,12]{2,1,0:T(2,128)(2,1)} %weight_hbm.1, s32[2,2,12]{2,1,0:T(2,128)} %partners_hbm.1, s32[2,2]{1,0:T(2,128)} %count_hbm.1, f32[2,2,3]{2,1,0:T(2,128)} %bitcast.10), custom_call_target="tpu_custom_call" | custom-call | tf_op jit(solution)/shard_map/pack/pallas_call | solution.py:503
  2.7 0.0 copy-start.1
  2.7 7.3 %all-to-all-start = ((bf16[32,8,896]{2,1,0:T(8,128)(2,1)}), bf16[32,8,896]{2,1,0:T(8,128)(2,1)S(1)}, u32[]{:S(2)}, u32[]{:S(2)}) async-start(bf16[32,8,896]{2,1,0:T(8,128)(2,1)} %bitcast.2), calls=%async_computation | async-start | bytes 917504 | tf_op jit(solution)/shard_map/all_to_all | solution.py:564
  10.0 1.2 %table.1 = (bf16[2,512,512]{2,1,0:T(8,128)(2,1)S(1)}, bf16[256,512]{1,0:T(8,128)(2,1)S(1)}) custom-call(bf16[2,512,512]{2,1,0:T(8,128)(2,1)} %rad_hbm.1), custom_call_target="tpu_custom_call" | custom-call | flops 10000000 | bytes 4000000 | tf_op jit(solution)/shard_map/table/pallas_call | solution.py:503
  11.3 11.9 %all-to-all-done = bf16[32,8,896]{2,1,0:T(8,128)(2,1)S(1)} async-done(((bf16[32,8,896]{2,1,0:T(8,128)(2,1)}), bf16[32,8,896]{2,1,0:T(8,128)(2,1)S(1)}, u32[]{:S(2)}, u32[]{:S(2)}) %all-to-all-start) | async-done | bytes 458784 | tf_op jit(solution)/shard_map/all_to_all | solution.py:564
  23.1 0.0 copy-done
  23.1 3.5 %bounces.1 = (bf16[256,512]{1,0:T(8,128)(2,1)}, bf16[256,512]{1,0:T(8,128)(2,1)S(1)}, f32[128,128]{1,0:T(8,128)S(1)}) custom-call(bf16[256,896]{1,0:T(8,128)(2,1)S(1)} %bitcast.7, bf16[2,512,512]{2,1,0:T(8,128)(2,1)S(1)} %get-tuple-element.9.rad, f32[3,512]{1,0:T(4,128)S(1)} %copy-done), custom_call_target="tpu_custom_call" | custom-call | tf_op jit(solution)/shard_map/bounces/pallas_call | solution.py:503
  26.6 4.0 %all-to-all-start.1 = ((bf16[32,8,512]{2,1,0:T(8,128)(2,1)}), bf16[32,8,512]{2,1,0:T(8,128)(2,1)S(1)}, u32[]{:S(2)}, u32[]{:S(2)}) async-start(bf16[32,8,512]{2,1,0:T(8,128)(2,1)} %bitcast.4), calls=%async_computation.1 | async-start | bytes 524288 | tf_op jit(solution)/shard_map/all_to_all | solution.py:581
  30.6 0.0 copy-done.1
  30.6 3.5 %image.1 = f32[8,256]{1,0:T(8,128)S(1)} custom-call(bf16[256,512]{1,0:T(8,128)(2,1)S(1)} %get-tuple-element.11.last, f32[128,128]{1,0:T(8,128)S(1)} %get-tuple-element.12.kept, bf16[256,512]{1,0:T(8,128)(2,1)S(1)} %get-tuple-element.13.long_table, f32[3,2048]{1,0:T(4,128)S(1)} %copy-done.1, bf16[2,512,512]{2,1,0:T(8,128)(2,1)S(1)} %get-tuple-element.9.rad, ...), custom_call_target="tpu_custom_call" | custom-call | flops 2000000000 | bytes 4000000 | tf_op jit(solution)/shard_map/image/pallas_call | solution.py:503
  34.1 0.3 collective-permute-start
  34.5 0.9 %collective-permute-done = f32[8,256]{1,0:T(8,128)S(1)} collective-permute-done((f32[8,256]{1,0:T(8,128)S(1)}, f32[8,256]{1,0:T(8,128)S(1)}, u32[]{:S(2)}, u32[]{:S(2)}) %collective-permute-start) | collective-permute-done | bytes 8224 | tf_op jit(solution)/shard_map/ppermute | solution.py:598
  35.4 2.7 %collective-permute-start.3 = (f32[16,256]{1,0:T(8,128)S(1)}, f32[16,256]{1,0:T(8,128)S(1)}, u32[]{:S(2)}, u32[]{:S(2)}) collective-permute-start(f32[16,256]{1,0:T(8,128)S(1)} %pad_maximum_fusion.refs_0_), channel_id=1, source_target_pairs={{0,24},{4,28},{8,16},{12,20},{16,8},{20,12},{24,0},{28,4},{1,25},{... | collective-permute-start | bytes 49160 | tf_op jit(solution)/shard_map/ppermute | solution.py:598
  38.1 0.6 %collective-permute-start.2 = (f32[16,256]{1,0:T(8,128)S(1)}, f32[16,256]{1,0:T(8,128)S(1)}, u32[]{:S(2)}, u32[]{:S(2)}) collective-permute-start(f32[16,256]{1,0:T(8,128)S(1)} %pad_maximum_fusion.refs_0_), channel_id=1, source_target_pairs={{0,16},{4,20},{8,24},{12,28},{16,0},{20,4},{24,8},{28,12},{1,17},{... | collective-permute-start | bytes 49160 | tf_op jit(solution)/shard_map/ppermute | solution.py:598
  38.6 0.3 collective-permute-start.1
  38.9 1.1 %collective-permute-done.3.refs_3_ = f32[16,256]{1,0:T(8,128)S(1)} collective-permute-done((f32[16,256]{1,0:T(8,128)S(1)}, f32[16,256]{1,0:T(8,128)S(1)}, u32[]{:S(2)}, u32[]{:S(2)}) %collective-permute-start.3) | collective-permute-done | bytes 16416 | tf_op jit(solution)/shard_map/ppermute | solution.py:598
  40.0 1.8 %collective-permute-done.2.refs_2_ = f32[16,256]{1,0:T(8,128)S(1)} collective-permute-done((f32[16,256]{1,0:T(8,128)S(1)}, f32[16,256]{1,0:T(8,128)S(1)}, u32[]{:S(2)}, u32[]{:S(2)}) %collective-permute-start.2) | collective-permute-done | bytes 16416 | tf_op jit(solution)/shard_map/ppermute | solution.py:598
  41.8 0.6 %collective-permute-done.1.refs_1_ = f32[16,256]{1,0:T(8,128)S(1)} collective-permute-done((f32[16,256]{1,0:T(8,128)S(1)}, f32[16,256]{1,0:T(8,128)S(1)}, u32[]{:S(2)}, u32[]{:S(2)}) %collective-permute-start.1) | collective-permute-done | bytes 16416 | tf_op jit(solution)/shard_map/ppermute | solution.py:598
  42.4 0.0 all-to-all-done.1
  42.4 0.9 %unpack.1 = (bf16[256,512]{1,0:T(8,128)(2,1)}, f32[8,256]{1,0:T(8,128)}) custom-call(bf16[256,512]{1,0:T(8,128)(2,1)S(1)} %bitcast.8, f32[16,256]{1,0:T(8,128)S(1)} %pad_maximum_fusion.refs_0_, f32[16,256]{1,0:T(8,128)S(1)} %collective-permute-done.1.refs_1_, f32[16,256]{1,0:T(8,128)S(1)} %collective-permute-done.2.refs_2_, ...), custom_call_target="tpu_custom_call" | custom-call | tf_op jit(solution)/shard_map/unpack/pallas_call | solution.py:503
  (1 shorter events, 0.0 us)
Async XLA Ops:
  0.6 22.5 %copy-start = (f32[3,512]{1,0:T(4,128)S(1)}, f32[3,512]{1,0:T(4,128)}, u32[]{:S(2)}) copy-start(f32[3,512]{1,0:T(4,128)} %spectral_dirs.1) | copy-start | bytes 18436
  2.7 27.9 %copy-start.1 = (f32[3,2048]{1,0:T(4,128)S(1)}, f32[3,2048]{1,0:T(4,128)}, u32[]{:S(2)}) copy-start(f32[3,2048]{1,0:T(4,128)} %receiver_dirs.1) | copy-start | bytes 73732
  2.7 20.4 %all-to-all-start = ((bf16[32,8,896]{2,1,0:T(8,128)(2,1)}), bf16[32,8,896]{2,1,0:T(8,128)(2,1)S(1)}, u32[]{:S(2)}, u32[]{:S(2)}) async-start(bf16[32,8,896]{2,1,0:T(8,128)(2,1)} %bitcast.2), calls=%async_computation | async-start | bytes 917504 | tf_op jit(solution)/shard_map/all_to_all | solution.py:564
  26.6 15.7 %all-to-all-start.1 = ((bf16[32,8,512]{2,1,0:T(8,128)(2,1)}), bf16[32,8,512]{2,1,0:T(8,128)(2,1)S(1)}, u32[]{:S(2)}, u32[]{:S(2)}) async-start(bf16[32,8,512]{2,1,0:T(8,128)(2,1)} %bitcast.4), calls=%async_computation.1 | async-start | bytes 524288 | tf_op jit(solution)/shard_map/all_to_all | solution.py:581
  34.1 1.2 %collective-permute-start = (f32[8,256]{1,0:T(8,128)S(1)}, f32[8,256]{1,0:T(8,128)S(1)}, u32[]{:S(2)}, u32[]{:S(2)}) collective-permute-start(f32[8,256]{1,0:T(8,128)S(1)} %image.1), channel_id=1, source_target_pairs={{0,4},{4,0},{8,12},{12,8},{16,20},{20,16},{24,28},{28,24},{1,5},{5... | collective-permute-start | bytes 24584 | tf_op jit(solution)/shard_map/ppermute | solution.py:598
  35.4 4.6 %collective-permute-start.3 = (f32[16,256]{1,0:T(8,128)S(1)}, f32[16,256]{1,0:T(8,128)S(1)}, u32[]{:S(2)}, u32[]{:S(2)}) collective-permute-start(f32[16,256]{1,0:T(8,128)S(1)} %pad_maximum_fusion.refs_0_), channel_id=1, source_target_pairs={{0,24},{4,28},{8,16},{12,20},{16,8},{20,12},{24,0},{28,4},{1,25},{... | collective-permute-start | bytes 49160 | tf_op jit(solution)/shard_map/ppermute | solution.py:598
  38.1 3.7 %collective-permute-start.2 = (f32[16,256]{1,0:T(8,128)S(1)}, f32[16,256]{1,0:T(8,128)S(1)}, u32[]{:S(2)}, u32[]{:S(2)}) collective-permute-start(f32[16,256]{1,0:T(8,128)S(1)} %pad_maximum_fusion.refs_0_), channel_id=1, source_target_pairs={{0,16},{4,20},{8,24},{12,28},{16,0},{20,4},{24,8},{28,12},{1,17},{... | collective-permute-start | bytes 49160 | tf_op jit(solution)/shard_map/ppermute | solution.py:598
  38.6 3.7 %collective-permute-start.1 = (f32[16,256]{1,0:T(8,128)S(1)}, f32[16,256]{1,0:T(8,128)S(1)}, u32[]{:S(2)}, u32[]{:S(2)}) collective-permute-start(f32[16,256]{1,0:T(8,128)S(1)} %pad_maximum_fusion.refs_0_), channel_id=1, source_target_pairs={{0,8},{4,12},{8,0},{12,4},{16,24},{20,28},{24,16},{28,20},{1,9},{5... | collective-permute-start | bytes 49160 | tf_op jit(solution)/shard_map/ppermute | solution.py:598

commit v4 on v3

--- a/solution.py
+++ b/solution.py
@@ -318,8 +318,9 @@
     out[:, :unit_count] = dot(order, cur[...]).astype(BF16)
 
 
-def table_kernel(rad_hbm, rad, long_table, sems):
-    copies = fetch([(rad_hbm, rad)], sems)
+def table_kernel(rad_hbm, far_hbm, rad, far_head, long_table, sems):
+    head = far_hbm.at[:, : far_head.shape[1]]
+    copies = fetch([(rad_hbm, rad), (head, far_head)], sems)
     tile = long_table.shape[0]
     row = lax.broadcasted_iota(jnp.int32, (tile, tile), 0)
     column = lax.broadcasted_iota(jnp.int32, (tile, tile), 1)
@@ -354,7 +355,20 @@
     )
 
 
-def bounce_kernel(grid_shape, local_shape, got, rad, spectral_dirs, out, last, kept):
+def bounce_kernel(
+    grid_shape,
+    local_shape,
+    got,
+    rad,
+    spectral_dirs,
+    far_head,
+    out_hbm,
+    final,
+    kept,
+    out,
+    sems,
+):
+    del far_head
     unit_count = rad.shape[1]
     half = unit_count // 2
     rows = got.shape[0]
@@ -417,30 +431,47 @@
         current = jnp.concatenate(
             [start[:patches] + reflect * recv_re, start[patches:] + reflect * recv_im], axis=0
         ).astype(BF16)
-    last[...] = current
     out[...] = dot(part_sorter(rows, local, True), current).astype(BF16)
+    out_copy = pltpu.make_async_copy(out, out_hbm, sems.at[0])
+    out_copy.start()
+    final[...] = jnp.concatenate(spectrum(current, rad), axis=0).astype(BF16)
+    out_copy.wait()
 
 
 def image_kernel(
-    scale, last, kept, long_table, receiver_dirs, rad, far_hbm, image, far_map, cos_view, sin_view, sems
+    scale,
+    final,
+    kept,
+    long_table,
+    receiver_dirs,
+    far_head,
+    far_hbm,
+    same,
+    other,
+    image,
+    far_rest,
+    sems,
 ):
-    copies = fetch([(far_hbm, far_map)], sems)
+    head = far_head.shape[1]
+    rest_copy = pltpu.make_async_copy(far_hbm.at[:, head:], far_rest, sems.at[0])
+    rest_copy.start()
     splits, tile = image.shape
     patches = kept.shape[0]
     centre = centres_of(kept[...])
-    cuts = [slice(tile * t, tile * (t + 1)) for t in range(splits)]
-    for cut in cuts:
-        cos_view[:, cut], sin_view[:, cut] = cos_sin(turns(centre, receiver_dirs[:, cut]))
-    final = jnp.concatenate(spectrum(last[...], rad), axis=0).astype(BF16)
-    copies[0].wait()
     far_re, far_im = [], []
-    for cut in cuts:
-        beams = dot(final, far_map[:, cut])
-        c, s = cos_view[:, cut], sin_view[:, cut]
+    for t in range(splits):
+        cut = slice(tile * t, tile * (t + 1))
+        if tile * t == head:
+            rest_copy.wait()
+        if tile * t < head:
+            beams = dot(final[...], far_head[:, cut])
+        else:
+            beams = dot(final[...], far_rest[:, tile * t - head : tile * (t + 1) - head])
+        cos_view, sin_view = cos_sin(turns(centre, receiver_dirs[:, cut]))
         beam_re = beams[:patches]
         beam_im = beams[patches:]
-        far_re.append(jnp.sum(beam_re * c - beam_im * s, axis=0, keepdims=True))
-        far_im.append(jnp.sum(beam_re * s + beam_im * c, axis=0, keepdims=True))
+        far_re.append(jnp.sum(beam_re * cos_view - beam_im * sin_view, axis=0, keepdims=True))
+        far_im.append(jnp.sum(beam_re * sin_view + beam_im * cos_view, axis=0, keepdims=True))
     row = lax.broadcasted_iota(jnp.int32, (splits, 128), 0)
     column = lax.broadcasted_iota(jnp.int32, (splits, 128), 1)
     short_cos, short_sin = cos_sin((row * column % splits).astype(F32) * (1.0 / splits))
@@ -465,16 +496,25 @@
     image_im = answer[splits:, :tile] - answer[:splits, tile:]
     power = scale * (image_re * image_re + image_im * image_im)
     each = tile // splits
-    lane = lax.broadcasted_iota(jnp.int32, (splits, tile), 1)
-    row = lax.broadcasted_iota(jnp.int32, (splits, tile), 0)
-    fast = jnp.where(lane % splits == row, 1.0, 0.0)
+    upper = power.astype(BF16)
+    lower = (power - upper.astype(F32)).astype(BF16)
+    lane = lax.broadcasted_iota(jnp.int32, (2 * splits, tile), 1)
+    row = lax.broadcasted_iota(jnp.int32, (2 * splits, tile), 0)
+    fast = jnp.where(lane % splits == row % splits, 1.0, 0.0).astype(BF16)
     spread = lax.dot_general(
-        power, fast, (((0,), (0,)), ((), ())), precision=HIGH, preferred_element_type=F32
+        jnp.concatenate([upper, lower], axis=0),
+        fast,
+        (((0,), (0,)), ((), ())),
+        preferred_element_type=F32,
     )
     row = lax.broadcasted_iota(jnp.int32, (tile, tile), 0)
     column = lax.broadcasted_iota(jnp.int32, (tile, tile), 1)
     spread = jnp.where(row % each == column // splits, spread, 0.0)
     image[...] = jnp.sum(spread.reshape(splits, each, tile), axis=1)
+    me = lax.axis_index("px")
+    for n in range(splits // 2):
+        same[n : n + 1, :] = image[pl.ds(me ^ (2 * n), 1), :]
+        other[n : n + 1, :] = image[pl.ds(me ^ (2 * n + 1), 1), :]
 
 
 def unpack_kernel(local, grid_shape, got, *refs):
@@ -489,13 +529,18 @@
     row = lax.broadcasted_iota(jnp.int32, image.shape, 0)
     whole = jnp.zeros(image.shape, F32)
     for n in range(n_px):
-        mine = pairs[n // 2][pl.ds(n % 2 * n_px + me, 1), :]
+        at = n // 2 + n % 2 * (n_px // 2)
+        mine = pairs[n // 2][at : at + 1, :]
         whole = jnp.where(row == (me ^ n), mine, whole)
     image[...] = whole
 
 
-def call(kernel, name, outs, operands, spaces, scratch=(), cost=None, limit=32):
-    vmem = pl.BlockSpec(memory_space=pltpu.VMEM)
+def call(kernel, name, outs, operands, spaces, scratch=(), cost=None, limit=32, left=()):
+    specs = jax.tree.map(lambda _: pl.BlockSpec(memory_space=pltpu.VMEM), outs)
+    if left:
+        specs = tuple(
+            pl.BlockSpec(memory_space=pl.ANY) if n in left else s for n, s in enumerate(specs)
+        )
     operands = [
         pltpu.with_memory_space_constraint(a, pltpu.HBM) if m is pltpu.HBM else a
         for a, m in zip(operands, spaces)
@@ -504,7 +549,7 @@
         kernel,
         out_shape=outs,
         in_specs=[pl.BlockSpec(memory_space=m) for m in spaces],
-        out_specs=jax.tree.map(lambda _: vmem, outs),
+        out_specs=specs,
         scratch_shapes=list(scratch),
         compiler_params=pltpu.CompilerParams(vmem_limit_bytes=limit * MIB),
         cost_estimate=cost,
@@ -562,33 +607,36 @@
         like(*sources),
     )
     got = lax.all_to_all(packed.reshape(devices, block, sent_width), axes, 0, 0, tiled=True)
-    rad, long_table = call(
+    depth, head = far_map.shape[0], rcv_count // 2
+    rad, far_head, long_table = call(
         table_kernel,
         "table",
-        (shape(*rad_pattern.shape), shape(tile, 2 * tile)),
-        (rad_pattern,),
-        [hbm],
-        [pltpu.SemaphoreType.DMA((1,))],
+        (shape(*rad_pattern.shape), shape(depth, head), shape(tile, 2 * tile)),
+        (rad_pattern, far_map),
+        [hbm] * 2,
+        [pltpu.SemaphoreType.DMA((2,))],
         cost=pl.CostEstimate(flops=10**7, bytes_accessed=4 * 10**6, transcendentals=0),
     )
-    answer, last, kept = call(
+    answer, final, kept = call(
         functools.partial(bounce_kernel, (n_px, n_py), (local_rows, local_cols)),
         "bounces",
         (shape(rows, unit_count), shape(rows, unit_count), shape(patches, 128, dtype=F32)),
-        (got.reshape(rows, sent_width), rad, spectral_dirs),
-        [vmem] * 3,
+        (got.reshape(rows, sent_width), rad, spectral_dirs, far_head),
+        [vmem] * 3 + [pl.ANY],
+        [pltpu.VMEM((rows, unit_count), BF16), pltpu.SemaphoreType.DMA((1,))],
+        left=(0,),
     )
     back = lax.all_to_all(answer.reshape(devices, block, unit_count), axes, 0, 0, tiled=True)
-    part = call(
+    half = n_px // 2
+    same, other = call(
         functools.partial(image_kernel, 0.125 / (patches * rcv_count)),
         "image",
-        shape(n_px, tile, dtype=F32),
-        (last, kept, long_table, receiver_dirs, rad, far_map),
+        (shape(half, tile, dtype=F32), shape(half, tile, dtype=F32)),
+        (final, kept, long_table, receiver_dirs, far_head, far_map),
         [vmem] * 5 + [hbm],
         [
-            pltpu.VMEM(far_map.shape, BF16),
-            pltpu.VMEM((patches, rcv_count), F32),
-            pltpu.VMEM((patches, rcv_count), F32),
+            pltpu.VMEM((n_px, tile), F32),
+            pltpu.VMEM((depth, rcv_count - head), BF16),
             pltpu.SemaphoreType.DMA((1,)),
         ],
         cost=pl.CostEstimate(flops=2 * 10**9, bytes_accessed=4 * 10**6, transcendentals=0),
@@ -597,7 +645,7 @@
     def swapped(array, bits):
         return lax.ppermute(array, "px", [(i, i ^ bits) for i in range(n_px)])
 
-    pair = jnp.concatenate([part, swapped(part, 1)], axis=0)
+    pair = jnp.concatenate([same, swapped(other, 1)], axis=0)
     pairs = [pair] + [swapped(pair, bits) for bits in range(2, n_px, 2)]
     currents, image = call(
         functools.partial(unpack_kernel, local, (n_px, n_py)),

time: 43.7 us -> 42.7 us (0.977)
  Pallas kernels: 11.3 us -> 10.7 us
  waiting for transfers between devices: 16.3 us -> 15.8 us
    pallas_call x5, Pallas kernels: 11.3 us -> 10.7 us  [call(): pl.pallas_call(kernel, out_shape=outs, in_specs=[pl.BlockSpec(memory_spac...]
  transfers between devices with their start and end apart: 6 -> 6, of which waited for: 5 -> 5; matrix products, arithmetic and copies ran while one was open for 0% -> 0% of each run, Pallas kernels for 11% -> 10%
where the time goes in v4:
time: 42.7 us; the launch traced here: 42.3 us
  waiting for transfers between devices  15.8 us (37%)
  starting transfers between devices  15.1 us (35%)
  Pallas kernels  10.7 us (25%)
  between operations  0.71 us (2%)
    all_to_all x1, waiting for transfers between devices, illumination_sharded(): lax.all_to_all(packed.reshape(devices, block, sent_width), axes, 0, 0, ti...  11.5 us
    pallas_call x5, Pallas kernels, call(): pl.pallas_call(kernel, out_shape=outs, in_specs=[pl.BlockSpec(memory_spac...  10.7 us
    all_to_all x1, starting transfers between devices, illumination_sharded(): lax.all_to_all(packed.reshape(devices, block, sent_width), axes, 0, 0, ti...  7.3 us
    ppermute x4, waiting for transfers between devices, swapped(): return lax.ppermute(array, 'px', [(i, i ^ bits) for i in range(n_px)])  4.31 us
    all_to_all x1, starting transfers between devices, illumination_sharded(): lax.all_to_all(answer.reshape(devices, block, unit_count), axes, 0, 0, ti...  3.98 us
    ppermute x4, starting transfers between devices, swapped(): return lax.ppermute(array, 'px', [(i, i ^ bits) for i in range(n_px)])  3.8 us
  transfers between devices with their start and end apart: 6, of which 5 were waited for; matrix products, arithmetic and copies ran while one was open for 0% of the time, Pallas kernels for 10%

profile of v4, /device:TPU:0, one launch (start us, length us, event | category | flops | bytes accessed | tf_op | source)
XLA Modules:
  0.0 42.3 jit_solution(14595182892677757597)
XLA Ops:
  0.6 2.0 %pack.1 = bf16[256,896]{1,0:T(8,128)(2,1)} custom-call(bf16[256,512]{1,0:T(8,128)(2,1)} %bitcast.9, f32[2,2,512]{2,1,0:T(2,128)} %reflect_hbm.1, bf16[2,2,12]{2,1,0:T(2,128)(2,1)} %weight_hbm.1, s32[2,2,12]{2,1,0:T(2,128)} %partners_hbm.1, s32[2,2]{1,0:T(2,128)} %count_hbm.1, f32[2,2,3]{2,1,0:T(2,128)} %bitcast.10), custom_call_target="tpu_custom_call" | custom-call | tf_op jit(solution)/shard_map/pack/pallas_call | solution.py:548
  2.7 0.0 copy-start
  2.7 7.3 %all-to-all-start = ((bf16[32,8,896]{2,1,0:T(8,128)(2,1)}), bf16[32,8,896]{2,1,0:T(8,128)(2,1)S(1)}, u32[]{:S(2)}, u32[]{:S(2)}) async-start(bf16[32,8,896]{2,1,0:T(8,128)(2,1)} %bitcast.2), calls=%async_computation | async-start | bytes 917504 | tf_op jit(solution)/shard_map/all_to_all | solution.py:609
  10.0 1.6 %table.1 = (bf16[2,512,512]{2,1,0:T(8,128)(2,1)S(1)}, bf16[512,1024]{1,0:T(8,128)(2,1)S(1)}, bf16[256,512]{1,0:T(8,128)(2,1)S(1)}) custom-call(bf16[2,512,512]{2,1,0:T(8,128)(2,1)} %rad_hbm.1, bf16[512,2048]{1,0:T(8,128)(2,1)} %far_hbm.3), custom_call_target="tpu_custom_call" | custom-call | flops 10000000 | bytes 4000000 | tf_op jit(solution)/shard_map/table/pallas_call | solution.py:548
  11.6 0.0 copy-start.1
  11.6 11.5 %all-to-all-done = bf16[32,8,896]{2,1,0:T(8,128)(2,1)S(1)} async-done(((bf16[32,8,896]{2,1,0:T(8,128)(2,1)}), bf16[32,8,896]{2,1,0:T(8,128)(2,1)S(1)}, u32[]{:S(2)}, u32[]{:S(2)}) %all-to-all-start) | async-done | bytes 458784 | tf_op jit(solution)/shard_map/all_to_all | solution.py:609
  23.1 0.0 copy-done
  23.1 3.5 %bounces.1 = (bf16[256,512]{1,0:T(8,128)(2,1)}, bf16[256,512]{1,0:T(8,128)(2,1)S(1)}, f32[128,128]{1,0:T(8,128)S(1)}) custom-call(bf16[256,896]{1,0:T(8,128)(2,1)S(1)} %bitcast.7, bf16[2,512,512]{2,1,0:T(8,128)(2,1)S(1)} %get-tuple-element.12.rad, f32[3,512]{1,0:T(4,128)S(1)} %copy-done, bf16[512,1024]{1,0:T(8,128)(2,1)S(1)} %get-tuple-element.13.far_head), custom_call_target="tpu_custom_call" | custom-call | tf_op jit(solution)/shard_map/bounces/pallas_call | solution.py:548
  26.6 4.0 %all-to-all-start.1 = ((bf16[32,8,512]{2,1,0:T(8,128)(2,1)}), bf16[32,8,512]{2,1,0:T(8,128)(2,1)S(1)}, u32[]{:S(2)}, u32[]{:S(2)}) async-start(bf16[32,8,512]{2,1,0:T(8,128)(2,1)} %bitcast.4), calls=%async_computation.1 | async-start | bytes 524288 | tf_op jit(solution)/shard_map/all_to_all | solution.py:629
  30.6 0.0 copy-done.1
  30.6 2.6 %image.1 = (f32[4,256]{1,0:T(4,128)S(1)}, f32[4,256]{1,0:T(4,128)S(1)}) custom-call(bf16[256,512]{1,0:T(8,128)(2,1)S(1)} %get-tuple-element.15.final, f32[128,128]{1,0:T(8,128)S(1)} %get-tuple-element.16.kept, bf16[256,512]{1,0:T(8,128)(2,1)S(1)} %get-tuple-element.17.long_table, f32[3,2048]{1,0:T(4,128)S(1)} %copy-done.1, ...), custom_call_target="tpu_custom_call" | custom-call | flops 2000000000 | bytes 4000000 | tf_op jit(solution)/shard_map/image/pallas_call | solution.py:548
  33.3 0.3 collective-permute-start
  33.6 0.9 %collective-permute-done = f32[4,256]{1,0:T(4,128)S(1)} collective-permute-done((f32[4,256]{1,0:T(4,128)S(1)}, f32[4,256]{1,0:T(4,128)S(1)}, u32[]{:S(2)}, u32[]{:S(2)}) %collective-permute-start) | collective-permute-done | bytes 4128 | tf_op jit(solution)/shard_map/ppermute | solution.py:646
  34.5 2.7 %collective-permute-start.3 = (f32[8,256]{1,0:T(8,128)S(1)}, f32[8,256]{1,0:T(8,128)S(1)}, u32[]{:S(2)}, u32[]{:S(2)}) collective-permute-start(f32[8,256]{1,0:T(8,128)S(1)} %pad_maximum_fusion.refs_0_), channel_id=1, source_target_pairs={{0,24},{4,28},{8,16},{12,20},{16,8},{20,12},{24,0},{28,4},{1,25},{... | collective-permute-start | bytes 24584 | tf_op jit(solution)/shard_map/ppermute | solution.py:646
  37.2 0.6 %collective-permute-start.2 = (f32[8,256]{1,0:T(8,128)S(1)}, f32[8,256]{1,0:T(8,128)S(1)}, u32[]{:S(2)}, u32[]{:S(2)}) collective-permute-start(f32[8,256]{1,0:T(8,128)S(1)} %pad_maximum_fusion.refs_0_), channel_id=1, source_target_pairs={{0,16},{4,20},{8,24},{12,28},{16,0},{20,4},{24,8},{28,12},{1,17},{... | collective-permute-start | bytes 24584 | tf_op jit(solution)/shard_map/ppermute | solution.py:646
  37.7 0.3 collective-permute-start.1
  38.0 1.1 %collective-permute-done.3.refs_3_ = f32[8,256]{1,0:T(8,128)S(1)} collective-permute-done((f32[8,256]{1,0:T(8,128)S(1)}, f32[8,256]{1,0:T(8,128)S(1)}, u32[]{:S(2)}, u32[]{:S(2)}) %collective-permute-start.3) | collective-permute-done | bytes 8224 | tf_op jit(solution)/shard_map/ppermute | solution.py:646
  39.1 1.8 %collective-permute-done.2.refs_2_ = f32[8,256]{1,0:T(8,128)S(1)} collective-permute-done((f32[8,256]{1,0:T(8,128)S(1)}, f32[8,256]{1,0:T(8,128)S(1)}, u32[]{:S(2)}, u32[]{:S(2)}) %collective-permute-start.2) | collective-permute-done | bytes 8224 | tf_op jit(solution)/shard_map/ppermute | solution.py:646
  40.9 0.5 %collective-permute-done.1.refs_1_ = f32[8,256]{1,0:T(8,128)S(1)} collective-permute-done((f32[8,256]{1,0:T(8,128)S(1)}, f32[8,256]{1,0:T(8,128)S(1)}, u32[]{:S(2)}, u32[]{:S(2)}) %collective-permute-start.1) | collective-permute-done | bytes 8224 | tf_op jit(solution)/shard_map/ppermute | solution.py:646
  41.4 0.0 all-to-all-done.1
  41.4 0.9 %unpack.1 = (bf16[256,512]{1,0:T(8,128)(2,1)}, f32[8,256]{1,0:T(8,128)}) custom-call(bf16[256,512]{1,0:T(8,128)(2,1)S(1)} %bitcast.8, f32[8,256]{1,0:T(8,128)S(1)} %pad_maximum_fusion.refs_0_, f32[8,256]{1,0:T(8,128)S(1)} %collective-permute-done.1.refs_1_, f32[8,256]{1,0:T(8,128)S(1)} %collective-permute-done.2.refs_2_, ...), custom_call_target="tpu_custom_call" | custom-call | tf_op jit(solution)/shard_map/unpack/pallas_call | solution.py:548
  (1 shorter events, 0.0 us)
Async XLA Ops:
  2.7 20.4 %copy-start = (f32[3,512]{1,0:T(4,128)S(1)}, f32[3,512]{1,0:T(4,128)}, u32[]{:S(2)}) copy-start(f32[3,512]{1,0:T(4,128)} %spectral_dirs.1) | copy-start | bytes 18436
  2.7 20.4 %all-to-all-start = ((bf16[32,8,896]{2,1,0:T(8,128)(2,1)}), bf16[32,8,896]{2,1,0:T(8,128)(2,1)S(1)}, u32[]{:S(2)}, u32[]{:S(2)}) async-start(bf16[32,8,896]{2,1,0:T(8,128)(2,1)} %bitcast.2), calls=%async_computation | async-start | bytes 917504 | tf_op jit(solution)/shard_map/all_to_all | solution.py:609
  11.6 19.0 %copy-start.1 = (f32[3,2048]{1,0:T(4,128)S(1)}, f32[3,2048]{1,0:T(4,128)}, u32[]{:S(2)}) copy-start(f32[3,2048]{1,0:T(4,128)} %receiver_dirs.1) | copy-start | bytes 73732
  26.6 14.7 %all-to-all-start.1 = ((bf16[32,8,512]{2,1,0:T(8,128)(2,1)}), bf16[32,8,512]{2,1,0:T(8,128)(2,1)S(1)}, u32[]{:S(2)}, u32[]{:S(2)}) async-start(bf16[32,8,512]{2,1,0:T(8,128)(2,1)} %bitcast.4), calls=%async_computation.1 | async-start | bytes 524288 | tf_op jit(solution)/shard_map/all_to_all | solution.py:629
  33.3 1.2 %collective-permute-start = (f32[4,256]{1,0:T(4,128)S(1)}, f32[4,256]{1,0:T(4,128)S(1)}, u32[]{:S(2)}, u32[]{:S(2)}) collective-permute-start(f32[4,256]{1,0:T(4,128)S(1)} %get-tuple-element.19), channel_id=1, source_target_pairs={{0,4},{4,0},{8,12},{12,8},{16,20},{20,16},{24,28},{28,24},{1,5},{5... | collective-permute-start | bytes 12296 | tf_op jit(solution)/shard_map/ppermute | solution.py:646
  34.5 4.6 %collective-permute-start.3 = (f32[8,256]{1,0:T(8,128)S(1)}, f32[8,256]{1,0:T(8,128)S(1)}, u32[]{:S(2)}, u32[]{:S(2)}) collective-permute-start(f32[8,256]{1,0:T(8,128)S(1)} %pad_maximum_fusion.refs_0_), channel_id=1, source_target_pairs={{0,24},{4,28},{8,16},{12,20},{16,8},{20,12},{24,0},{28,4},{1,25},{... | collective-permute-start | bytes 24584 | tf_op jit(solution)/shard_map/ppermute | solution.py:646
  37.2 3.7 %collective-permute-start.2 = (f32[8,256]{1,0:T(8,128)S(1)}, f32[8,256]{1,0:T(8,128)S(1)}, u32[]{:S(2)}, u32[]{:S(2)}) collective-permute-start(f32[8,256]{1,0:T(8,128)S(1)} %pad_maximum_fusion.refs_0_), channel_id=1, source_target_pairs={{0,16},{4,20},{8,24},{12,28},{16,0},{20,4},{24,8},{28,12},{1,17},{... | collective-permute-start | bytes 24584 | tf_op jit(solution)/shard_map/ppermute | solution.py:646
  37.7 3.7 %collective-permute-start.1 = (f32[8,256]{1,0:T(8,128)S(1)}, f32[8,256]{1,0:T(8,128)S(1)}, u32[]{:S(2)}, u32[]{:S(2)}) collective-permute-start(f32[8,256]{1,0:T(8,128)S(1)} %pad_maximum_fusion.refs_0_), channel_id=1, source_target_pairs={{0,8},{4,12},{8,0},{12,4},{16,24},{20,28},{24,16},{28,20},{1,9},{5... | collective-permute-start | bytes 24584 | tf_op jit(solution)/shard_map/ppermute | solution.py:646

commit v5 on v4

--- a/solution.py
+++ b/solution.py
@@ -267,12 +267,14 @@
     rows = cur.shape[0]
     local_rows, local_cols, unit_count = reflect.shape
     local = local_rows * local_cols
-    half = unit_count // 2
     base_row = lax.axis_index("px") * local_rows
     base_col = lax.axis_index("py") * local_cols
-    order = sorter(
-        rows, local, rows // (2 * local), inner_at=lambda i: swapped_digits(i, *grid_shape)
-    )
+    row_id = lax.broadcasted_iota(jnp.int32, (rows, rows), 0)
+    in_id = lax.broadcasted_iota(jnp.int32, (rows, rows), 1)
+    illum_count = rows // (2 * local)
+    part, chunk, o = row_id // (rows // 2), row_id % (rows // 2) // local, row_id % local
+    column = (o * 2 + part) * illum_count + swapped_digits(chunk, *grid_shape)
+    order = jnp.where(in_id == column, 1.0, 0.0).astype(BF16)
     lane = lax.broadcasted_iota(jnp.int32, (local, 128), 1)
     row = lax.broadcasted_iota(jnp.int32, (local, 128), 0)
     patch_row = base_row + row // local_cols
@@ -307,15 +309,14 @@
         small = jnp.where(lane == first + 3 * d + 1, middle, small)
         small = jnp.where(lane == first + 3 * d + 2, rest - middle, small)
     refl = reflect[...].reshape(local, unit_count)
-    refl = jnp.concatenate([refl[:, :half], refl[:, half:]], axis=0)
-    small = jnp.concatenate([small, jnp.zeros_like(small)], axis=0)
-    tail = jnp.concatenate([refl, small], axis=1)
-    tail = jnp.concatenate([tail, tail], axis=0).astype(BF16)
-    step = tail.shape[0]
-    for s in range(rows // step):
-        out[step * s : step * (s + 1), unit_count:] = tail
+    tail = jnp.concatenate([refl, small], axis=1).astype(BF16)
+    for n in range(illum_count):
+        out[n, :, 2 * unit_count :] = tail
     copies[0].wait()
-    out[:, :unit_count] = dot(order, cur[...]).astype(BF16)
+    both = dot(order, cur[...])
+    both = jnp.concatenate([both[: rows // 2], both[rows // 2 :]], axis=1)
+    for n in range(illum_count):
+        out[n, :, : 2 * unit_count] = both[local * n : local * (n + 1)].astype(BF16)
 
 
 def table_kernel(rad_hbm, far_hbm, rad, far_head, long_table, sems):
@@ -370,23 +371,16 @@
 ):
     del far_head
     unit_count = rad.shape[1]
-    half = unit_count // 2
-    rows = got.shape[0]
-    patches = rows // 2
+    patches = got.shape[0] * got.shape[1]
+    rows = 2 * patches
     local_rows, local_cols = local_shape
     local = local_rows * local_cols
     n_px, n_py = grid_shape
     total_cols = n_py * local_cols
-    sorted_rows = dot(part_sorter(rows, local, False), got[...])
-    start = sorted_rows[:, :unit_count]
-    reflect = jnp.concatenate(
-        [
-            sorted_rows[:patches, unit_count : unit_count + half],
-            sorted_rows[patches:, unit_count : unit_count + half],
-        ],
-        axis=1,
-    )
-    small = sorted_rows[:patches, unit_count + half :]
+    whole = jnp.concatenate([got[n].astype(F32) for n in range(got.shape[0])], axis=0)
+    start = jnp.concatenate([whole[:, :unit_count], whole[:, unit_count : 2 * unit_count]], axis=0)
+    reflect = whole[:, 2 * unit_count : 3 * unit_count]
+    small = whole[:, 3 * unit_count :]
     kept[...] = small
 
     def place(axis):
@@ -589,7 +583,7 @@
     def shape(*dims, dtype=BF16):
         return jax.ShapeDtypeStruct(dims, dtype)
 
-    sent_width = unit_count + unit_count // 2 + 128
+    sent_width = 3 * unit_count + 128
     sources = (
         currents_in.reshape(rows, unit_count),
         reflect,
@@ -601,12 +595,12 @@
     packed = call(
         functools.partial(pack_kernel, total_cols, (n_px, n_py)),
         "pack",
-        shape(rows, sent_width),
+        shape(devices, local, sent_width),
         sources,
         [hbm] * 6,
         like(*sources),
     )
-    got = lax.all_to_all(packed.reshape(devices, block, sent_width), axes, 0, 0, tiled=True)
+    got = lax.all_to_all(packed, axes, 0, 0, tiled=True)
     depth, head = far_map.shape[0], rcv_count // 2
     rad, far_head, long_table = call(
         table_kernel,
@@ -621,7 +615,7 @@
         functools.partial(bounce_kernel, (n_px, n_py), (local_rows, local_cols)),
         "bounces",
         (shape(rows, unit_count), shape(rows, unit_count), shape(patches, 128, dtype=F32)),
-        (got.reshape(rows, sent_width), rad, spectral_dirs, far_head),
+        (got, rad, spectral_dirs, far_head),
         [vmem] * 3 + [pl.ANY],
         [pltpu.VMEM((rows, unit_count), BF16), pltpu.SemaphoreType.DMA((1,))],
         left=(0,),

time: 42.7 us -> 41.8 us (0.979)
  waiting for transfers between devices: 15.8 us -> 15.2 us
    all_to_all x1, waiting for transfers between devices: 11.5 us -> 10.9 us  [illumination_sharded(): got = lax.all_to_all(packed, axes, 0, 0, tiled=True)]
where the time goes in v5:
time: 41.8 us; the launch traced here: 41.5 us
  waiting for transfers between devices  15.2 us (36%)
  starting transfers between devices  15 us (36%)
  Pallas kernels  10.5 us (25%)
  between operations  0.71 us (2%)
    all_to_all x1, waiting for transfers between devices, illumination_sharded(): got = lax.all_to_all(packed, axes, 0, 0, tiled=True)  10.9 us
    pallas_call x5, Pallas kernels, call(): pl.pallas_call(kernel, out_shape=outs, in_specs=[pl.BlockSpec(memory_spac...  10.5 us
    all_to_all x1, starting transfers between devices, illumination_sharded(): got = lax.all_to_all(packed, axes, 0, 0, tiled=True)  7.3 us
    ppermute x4, waiting for transfers between devices, swapped(): return lax.ppermute(array, 'px', [(i, i ^ bits) for i in range(n_px)])  4.31 us
    all_to_all x1, starting transfers between devices, illumination_sharded(): lax.all_to_all(answer.reshape(devices, block, unit_count), axes, 0, 0, ti...  3.92 us
    ppermute x4, starting transfers between devices, swapped(): return lax.ppermute(array, 'px', [(i, i ^ bits) for i in range(n_px)])  3.81 us
  transfers between devices with their start and end apart: 6, of which 5 were waited for; matrix products, arithmetic and copies ran while one was open for 0% of the time, Pallas kernels for 10%

profile of v5, /device:TPU:0, one launch (start us, length us, event | category | flops | bytes accessed | tf_op | source)
XLA Modules:
  0.0 41.5 jit_solution(6911560250312593041)
XLA Ops:
  0.6 2.0 %pack.1 = bf16[32,4,1664]{2,1,0:T(4,128)(2,1)} custom-call(bf16[256,512]{1,0:T(8,128)(2,1)} %bitcast.6, f32[2,2,512]{2,1,0:T(2,128)} %reflect_hbm.1, bf16[2,2,12]{2,1,0:T(2,128)(2,1)} %weight_hbm.1, s32[2,2,12]{2,1,0:T(2,128)} %partners_hbm.1, s32[2,2]{1,0:T(2,128)} %count_hbm.1, f32[2,2,3]{2,1,0:T(2,128)} %bitcast.7), custom_call_target="tpu_custom_call" | custom-call | tf_op jit(solution)/shard_map/pack/pallas_call | solution.py:542
  2.7 0.0 copy-start
  2.7 7.3 %all-to-all-start = ((bf16[32,4,1664]{2,1,0:T(4,128)(2,1)}), bf16[32,4,1664]{2,1,0:T(4,128)(2,1)S(1)}, u32[]{:S(2)}, u32[]{:S(2)}) async-start(bf16[32,4,1664]{2,1,0:T(4,128)(2,1)} %pack.1), calls=%async_computation | async-start | bytes 851968 | tf_op jit(solution)/shard_map/all_to_all | solution.py:603
  10.0 1.6 %table.1 = (bf16[2,512,512]{2,1,0:T(8,128)(2,1)S(1)}, bf16[512,1024]{1,0:T(8,128)(2,1)S(1)}, bf16[256,512]{1,0:T(8,128)(2,1)S(1)}) custom-call(bf16[2,512,512]{2,1,0:T(8,128)(2,1)} %rad_hbm.1, bf16[512,2048]{1,0:T(8,128)(2,1)} %far_hbm.3), custom_call_target="tpu_custom_call" | custom-call | flops 10000000 | bytes 4000000 | tf_op jit(solution)/shard_map/table/pallas_call | solution.py:542
  11.6 0.0 copy-start.1
  11.6 10.9 %all-to-all-done.got = bf16[32,4,1664]{2,1,0:T(4,128)(2,1)S(1)} async-done(((bf16[32,4,1664]{2,1,0:T(4,128)(2,1)}), bf16[32,4,1664]{2,1,0:T(4,128)(2,1)S(1)}, u32[]{:S(2)}, u32[]{:S(2)}) %all-to-all-start) | async-done | bytes 426016 | tf_op jit(solution)/shard_map/all_to_all | solution.py:603
  22.5 0.0 copy-done
  22.5 3.4 %bounces.1 = (bf16[256,512]{1,0:T(8,128)(2,1)}, bf16[256,512]{1,0:T(8,128)(2,1)S(1)}, f32[128,128]{1,0:T(8,128)S(1)}) custom-call(bf16[32,4,1664]{2,1,0:T(4,128)(2,1)S(1)} %all-to-all-done.got, bf16[2,512,512]{2,1,0:T(8,128)(2,1)S(1)} %get-tuple-element.12.rad, f32[3,512]{1,0:T(4,128)S(1)} %copy-done, bf16[512,1024]{1,0:T(8,128)(2,1)S(1)} %get-tuple-element.13.far_head), custom_call_target="tpu_custom_call" | custom-call | tf_op jit(solution)/shard_map/bounces/pallas_call | solution.py:542
  25.8 3.9 %all-to-all-start.1 = ((bf16[32,8,512]{2,1,0:T(8,128)(2,1)}), bf16[32,8,512]{2,1,0:T(8,128)(2,1)S(1)}, u32[]{:S(2)}, u32[]{:S(2)}) async-start(bf16[32,8,512]{2,1,0:T(8,128)(2,1)} %bitcast.2), calls=%async_computation.1 | async-start | bytes 524288 | tf_op jit(solution)/shard_map/all_to_all | solution.py:623
  29.8 0.0 copy-done.1
  29.8 2.6 %image.1 = (f32[4,256]{1,0:T(4,128)S(1)}, f32[4,256]{1,0:T(4,128)S(1)}) custom-call(bf16[256,512]{1,0:T(8,128)(2,1)S(1)} %get-tuple-element.15.final, f32[128,128]{1,0:T(8,128)S(1)} %get-tuple-element.16.kept, bf16[256,512]{1,0:T(8,128)(2,1)S(1)} %get-tuple-element.17.long_table, f32[3,2048]{1,0:T(4,128)S(1)} %copy-done.1, ...), custom_call_target="tpu_custom_call" | custom-call | flops 2000000000 | bytes 4000000 | tf_op jit(solution)/shard_map/image/pallas_call | solution.py:542
  32.4 0.3 collective-permute-start
  32.7 0.9 %collective-permute-done = f32[4,256]{1,0:T(4,128)S(1)} collective-permute-done((f32[4,256]{1,0:T(4,128)S(1)}, f32[4,256]{1,0:T(4,128)S(1)}, u32[]{:S(2)}, u32[]{:S(2)}) %collective-permute-start) | collective-permute-done | bytes 4128 | tf_op jit(solution)/shard_map/ppermute | solution.py:640
  33.6 2.7 %collective-permute-start.3 = (f32[8,256]{1,0:T(8,128)S(1)}, f32[8,256]{1,0:T(8,128)S(1)}, u32[]{:S(2)}, u32[]{:S(2)}) collective-permute-start(f32[8,256]{1,0:T(8,128)S(1)} %pad_maximum_fusion.refs_0_), channel_id=1, source_target_pairs={{0,24},{4,28},{8,16},{12,20},{16,8},{20,12},{24,0},{28,4},{1,25},{... | collective-permute-start | bytes 24584 | tf_op jit(solution)/shard_map/ppermute | solution.py:640
  36.3 0.6 %collective-permute-start.2 = (f32[8,256]{1,0:T(8,128)S(1)}, f32[8,256]{1,0:T(8,128)S(1)}, u32[]{:S(2)}, u32[]{:S(2)}) collective-permute-start(f32[8,256]{1,0:T(8,128)S(1)} %pad_maximum_fusion.refs_0_), channel_id=1, source_target_pairs={{0,16},{4,20},{8,24},{12,28},{16,0},{20,4},{24,8},{28,12},{1,17},{... | collective-permute-start | bytes 24584 | tf_op jit(solution)/shard_map/ppermute | solution.py:640
  36.9 0.3 collective-permute-start.1
  37.1 1.1 %collective-permute-done.3.refs_3_ = f32[8,256]{1,0:T(8,128)S(1)} collective-permute-done((f32[8,256]{1,0:T(8,128)S(1)}, f32[8,256]{1,0:T(8,128)S(1)}, u32[]{:S(2)}, u32[]{:S(2)}) %collective-permute-start.3) | collective-permute-done | bytes 8224 | tf_op jit(solution)/shard_map/ppermute | solution.py:640
  38.2 1.8 %collective-permute-done.2.refs_2_ = f32[8,256]{1,0:T(8,128)S(1)} collective-permute-done((f32[8,256]{1,0:T(8,128)S(1)}, f32[8,256]{1,0:T(8,128)S(1)}, u32[]{:S(2)}, u32[]{:S(2)}) %collective-permute-start.2) | collective-permute-done | bytes 8224 | tf_op jit(solution)/shard_map/ppermute | solution.py:640
  40.0 0.5 %collective-permute-done.1.refs_1_ = f32[8,256]{1,0:T(8,128)S(1)} collective-permute-done((f32[8,256]{1,0:T(8,128)S(1)}, f32[8,256]{1,0:T(8,128)S(1)}, u32[]{:S(2)}, u32[]{:S(2)}) %collective-permute-start.1) | collective-permute-done | bytes 8224 | tf_op jit(solution)/shard_map/ppermute | solution.py:640
  40.5 0.0 all-to-all-done.1
  40.5 0.9 %unpack.1 = (bf16[256,512]{1,0:T(8,128)(2,1)}, f32[8,256]{1,0:T(8,128)}) custom-call(bf16[256,512]{1,0:T(8,128)(2,1)S(1)} %bitcast.5, f32[8,256]{1,0:T(8,128)S(1)} %pad_maximum_fusion.refs_0_, f32[8,256]{1,0:T(8,128)S(1)} %collective-permute-done.1.refs_1_, f32[8,256]{1,0:T(8,128)S(1)} %collective-permute-done.2.refs_2_, ...), custom_call_target="tpu_custom_call" | custom-call | tf_op jit(solution)/shard_map/unpack/pallas_call | solution.py:542
  (1 shorter events, 0.0 us)
Async XLA Ops:
  2.7 19.8 %copy-start = (f32[3,512]{1,0:T(4,128)S(1)}, f32[3,512]{1,0:T(4,128)}, u32[]{:S(2)}) copy-start(f32[3,512]{1,0:T(4,128)} %spectral_dirs.1) | copy-start | bytes 18436
  2.7 19.8 %all-to-all-start = ((bf16[32,4,1664]{2,1,0:T(4,128)(2,1)}), bf16[32,4,1664]{2,1,0:T(4,128)(2,1)S(1)}, u32[]{:S(2)}, u32[]{:S(2)}) async-start(bf16[32,4,1664]{2,1,0:T(4,128)(2,1)} %pack.1), calls=%async_computation | async-start | bytes 851968 | tf_op jit(solution)/shard_map/all_to_all | solution.py:603
  11.6 18.2 %copy-start.1 = (f32[3,2048]{1,0:T(4,128)S(1)}, f32[3,2048]{1,0:T(4,128)}, u32[]{:S(2)}) copy-start(f32[3,2048]{1,0:T(4,128)} %receiver_dirs.1) | copy-start | bytes 73732
  25.8 14.7 %all-to-all-start.1 = ((bf16[32,8,512]{2,1,0:T(8,128)(2,1)}), bf16[32,8,512]{2,1,0:T(8,128)(2,1)S(1)}, u32[]{:S(2)}, u32[]{:S(2)}) async-start(bf16[32,8,512]{2,1,0:T(8,128)(2,1)} %bitcast.2), calls=%async_computation.1 | async-start | bytes 524288 | tf_op jit(solution)/shard_map/all_to_all | solution.py:623
  32.4 1.2 %collective-permute-start = (f32[4,256]{1,0:T(4,128)S(1)}, f32[4,256]{1,0:T(4,128)S(1)}, u32[]{:S(2)}, u32[]{:S(2)}) collective-permute-start(f32[4,256]{1,0:T(4,128)S(1)} %get-tuple-element.19), channel_id=1, source_target_pairs={{0,4},{4,0},{8,12},{12,8},{16,20},{20,16},{24,28},{28,24},{1,5},{5... | collective-permute-start | bytes 12296 | tf_op jit(solution)/shard_map/ppermute | solution.py:640
  33.6 4.6 %collective-permute-start.3 = (f32[8,256]{1,0:T(8,128)S(1)}, f32[8,256]{1,0:T(8,128)S(1)}, u32[]{:S(2)}, u32[]{:S(2)}) collective-permute-start(f32[8,256]{1,0:T(8,128)S(1)} %pad_maximum_fusion.refs_0_), channel_id=1, source_target_pairs={{0,24},{4,28},{8,16},{12,20},{16,8},{20,12},{24,0},{28,4},{1,25},{... | collective-permute-start | bytes 24584 | tf_op jit(solution)/shard_map/ppermute | solution.py:640
  36.3 3.7 %collective-permute-start.2 = (f32[8,256]{1,0:T(8,128)S(1)}, f32[8,256]{1,0:T(8,128)S(1)}, u32[]{:S(2)}, u32[]{:S(2)}) collective-permute-start(f32[8,256]{1,0:T(8,128)S(1)} %pad_maximum_fusion.refs_0_), channel_id=1, source_target_pairs={{0,16},{4,20},{8,24},{12,28},{16,0},{20,4},{24,8},{28,12},{1,17},{... | collective-permute-start | bytes 24584 | tf_op jit(solution)/shard_map/ppermute | solution.py:640
  36.9 3.7 %collective-permute-start.1 = (f32[8,256]{1,0:T(8,128)S(1)}, f32[8,256]{1,0:T(8,128)S(1)}, u32[]{:S(2)}, u32[]{:S(2)}) collective-permute-start(f32[8,256]{1,0:T(8,128)S(1)} %pad_maximum_fusion.refs_0_), channel_id=1, source_target_pairs={{0,8},{4,12},{8,0},{12,4},{16,24},{20,28},{24,16},{28,20},{1,9},{5... | collective-permute-start | bytes 24584 | tf_op jit(solution)/shard_map/ppermute | solution.py:640

commit v6 on v5

--- a/solution.py
+++ b/solution.py
@@ -433,7 +433,7 @@
 
 
 def image_kernel(
-    scale,
+    root_scale,
     final,
     kept,
     long_table,
@@ -475,8 +475,8 @@
     mid_re = jnp.zeros((splits, tile), F32)
     mid_im = jnp.zeros((splits, tile), F32)
     for t in range(splits):
-        c = short_cos[:, t : t + 1]
-        s = short_sin[:, t : t + 1]
+        c = short_cos[:, t : t + 1] * root_scale
+        s = short_sin[:, t : t + 1] * root_scale
         mid_re = mid_re + (c * far_re[t] + s * far_im[t])
         mid_im = mid_im + (c * far_im[t] - s * far_re[t])
     tw_re = mid_re * twist_cos + mid_im * twist_sin
@@ -488,7 +488,7 @@
     answer = answer[: 2 * splits] + answer[2 * splits :]
     image_re = answer[:splits, :tile] + answer[splits:, tile:]
     image_im = answer[splits:, :tile] - answer[:splits, tile:]
-    power = scale * (image_re * image_re + image_im * image_im)
+    power = image_re * image_re + image_im * image_im
     each = tile // splits
     upper = power.astype(BF16)
     lower = (power - upper.astype(F32)).astype(BF16)
@@ -623,7 +623,7 @@
     back = lax.all_to_all(answer.reshape(devices, block, unit_count), axes, 0, 0, tiled=True)
     half = n_px // 2
     same, other = call(
-        functools.partial(image_kernel, 0.125 / (patches * rcv_count)),
+        functools.partial(image_kernel, math.sqrt(0.125 / (patches * rcv_count))),
         "image",
         (shape(half, tile, dtype=F32), shape(half, tile, dtype=F32)),
         (final, kept, long_table, receiver_dirs, far_head, far_map),

time: 41.8 us -> 41.8 us (level)
  no operation moved by 1% of the time
where the time goes in v6:
time: 41.8 us; the launch traced here: 41.5 us
  waiting for transfers between devices  15.2 us (36%)
  starting transfers between devices  15 us (36%)
  Pallas kernels  10.5 us (25%)
  between operations  0.71 us (2%)
    all_to_all x1, waiting for transfers between devices, illumination_sharded(): got = lax.all_to_all(packed, axes, 0, 0, tiled=True)  10.9 us
    pallas_call x5, Pallas kernels, call(): pl.pallas_call(kernel, out_shape=outs, in_specs=[pl.BlockSpec(memory_spac...  10.5 us
    all_to_all x1, starting transfers between devices, illumination_sharded(): got = lax.all_to_all(packed, axes, 0, 0, tiled=True)  7.3 us
    ppermute x4, waiting for transfers between devices, swapped(): return lax.ppermute(array, 'px', [(i, i ^ bits) for i in range(n_px)])  4.3 us
    all_to_all x1, starting transfers between devices, illumination_sharded(): lax.all_to_all(answer.reshape(devices, block, unit_count), axes, 0, 0, ti...  3.92 us
    ppermute x4, starting transfers between devices, swapped(): return lax.ppermute(array, 'px', [(i, i ^ bits) for i in range(n_px)])  3.81 us
  transfers between devices with their start and end apart: 6, of which 5 were waited for; matrix products, arithmetic and copies ran while one was open for 0% of the time, Pallas kernels for 10%

profile of v6, /device:TPU:0, one launch (start us, length us, event | category | flops | bytes accessed | tf_op | source)
XLA Modules:
  0.0 41.5 jit_solution(13437162795997682385)
XLA Ops:
  0.6 2.0 %pack.1 = bf16[32,4,1664]{2,1,0:T(4,128)(2,1)} custom-call(bf16[256,512]{1,0:T(8,128)(2,1)} %bitcast.6, f32[2,2,512]{2,1,0:T(2,128)} %reflect_hbm.1, bf16[2,2,12]{2,1,0:T(2,128)(2,1)} %weight_hbm.1, s32[2,2,12]{2,1,0:T(2,128)} %partners_hbm.1, s32[2,2]{1,0:T(2,128)} %count_hbm.1, f32[2,2,3]{2,1,0:T(2,128)} %bitcast.7), custom_call_target="tpu_custom_call" | custom-call | tf_op jit(solution)/shard_map/pack/pallas_call | solution.py:542
  2.7 0.0 copy-start
  2.7 7.3 %all-to-all-start = ((bf16[32,4,1664]{2,1,0:T(4,128)(2,1)}), bf16[32,4,1664]{2,1,0:T(4,128)(2,1)S(1)}, u32[]{:S(2)}, u32[]{:S(2)}) async-start(bf16[32,4,1664]{2,1,0:T(4,128)(2,1)} %pack.1), calls=%async_computation | async-start | bytes 851968 | tf_op jit(solution)/shard_map/all_to_all | solution.py:603
  10.0 1.6 %table.1 = (bf16[2,512,512]{2,1,0:T(8,128)(2,1)S(1)}, bf16[512,1024]{1,0:T(8,128)(2,1)S(1)}, bf16[256,512]{1,0:T(8,128)(2,1)S(1)}) custom-call(bf16[2,512,512]{2,1,0:T(8,128)(2,1)} %rad_hbm.1, bf16[512,2048]{1,0:T(8,128)(2,1)} %far_hbm.3), custom_call_target="tpu_custom_call" | custom-call | flops 10000000 | bytes 4000000 | tf_op jit(solution)/shard_map/table/pallas_call | solution.py:542
  11.6 0.0 copy-start.1
  11.6 10.9 %all-to-all-done.got = bf16[32,4,1664]{2,1,0:T(4,128)(2,1)S(1)} async-done(((bf16[32,4,1664]{2,1,0:T(4,128)(2,1)}), bf16[32,4,1664]{2,1,0:T(4,128)(2,1)S(1)}, u32[]{:S(2)}, u32[]{:S(2)}) %all-to-all-start) | async-done | bytes 426016 | tf_op jit(solution)/shard_map/all_to_all | solution.py:603
  22.5 0.0 copy-done
  22.5 3.4 %bounces.1 = (bf16[256,512]{1,0:T(8,128)(2,1)}, bf16[256,512]{1,0:T(8,128)(2,1)S(1)}, f32[128,128]{1,0:T(8,128)S(1)}) custom-call(bf16[32,4,1664]{2,1,0:T(4,128)(2,1)S(1)} %all-to-all-done.got, bf16[2,512,512]{2,1,0:T(8,128)(2,1)S(1)} %get-tuple-element.12.rad, f32[3,512]{1,0:T(4,128)S(1)} %copy-done, bf16[512,1024]{1,0:T(8,128)(2,1)S(1)} %get-tuple-element.13.far_head), custom_call_target="tpu_custom_call" | custom-call | tf_op jit(solution)/shard_map/bounces/pallas_call | solution.py:542
  25.8 3.9 %all-to-all-start.1 = ((bf16[32,8,512]{2,1,0:T(8,128)(2,1)}), bf16[32,8,512]{2,1,0:T(8,128)(2,1)S(1)}, u32[]{:S(2)}, u32[]{:S(2)}) async-start(bf16[32,8,512]{2,1,0:T(8,128)(2,1)} %bitcast.2), calls=%async_computation.1 | async-start | bytes 524288 | tf_op jit(solution)/shard_map/all_to_all | solution.py:623
  29.8 0.0 copy-done.1
  29.8 2.6 %image.1 = (f32[4,256]{1,0:T(4,128)S(1)}, f32[4,256]{1,0:T(4,128)S(1)}) custom-call(bf16[256,512]{1,0:T(8,128)(2,1)S(1)} %get-tuple-element.15.final, f32[128,128]{1,0:T(8,128)S(1)} %get-tuple-element.16.kept, bf16[256,512]{1,0:T(8,128)(2,1)S(1)} %get-tuple-element.17.long_table, f32[3,2048]{1,0:T(4,128)S(1)} %copy-done.1, ...), custom_call_target="tpu_custom_call" | custom-call | flops 2000000000 | bytes 4000000 | tf_op jit(solution)/shard_map/image/pallas_call | solution.py:542
  32.4 0.3 collective-permute-start
  32.7 0.9 %collective-permute-done = f32[4,256]{1,0:T(4,128)S(1)} collective-permute-done((f32[4,256]{1,0:T(4,128)S(1)}, f32[4,256]{1,0:T(4,128)S(1)}, u32[]{:S(2)}, u32[]{:S(2)}) %collective-permute-start) | collective-permute-done | bytes 4128 | tf_op jit(solution)/shard_map/ppermute | solution.py:640
  33.6 2.7 %collective-permute-start.3 = (f32[8,256]{1,0:T(8,128)S(1)}, f32[8,256]{1,0:T(8,128)S(1)}, u32[]{:S(2)}, u32[]{:S(2)}) collective-permute-start(f32[8,256]{1,0:T(8,128)S(1)} %pad_maximum_fusion.refs_0_), channel_id=1, source_target_pairs={{0,24},{4,28},{8,16},{12,20},{16,8},{20,12},{24,0},{28,4},{1,25},{... | collective-permute-start | bytes 24584 | tf_op jit(solution)/shard_map/ppermute | solution.py:640
  36.3 0.6 %collective-permute-start.2 = (f32[8,256]{1,0:T(8,128)S(1)}, f32[8,256]{1,0:T(8,128)S(1)}, u32[]{:S(2)}, u32[]{:S(2)}) collective-permute-start(f32[8,256]{1,0:T(8,128)S(1)} %pad_maximum_fusion.refs_0_), channel_id=1, source_target_pairs={{0,16},{4,20},{8,24},{12,28},{16,0},{20,4},{24,8},{28,12},{1,17},{... | collective-permute-start | bytes 24584 | tf_op jit(solution)/shard_map/ppermute | solution.py:640
  36.9 0.3 collective-permute-start.1
  37.1 1.1 %collective-permute-done.3.refs_3_ = f32[8,256]{1,0:T(8,128)S(1)} collective-permute-done((f32[8,256]{1,0:T(8,128)S(1)}, f32[8,256]{1,0:T(8,128)S(1)}, u32[]{:S(2)}, u32[]{:S(2)}) %collective-permute-start.3) | collective-permute-done | bytes 8224 | tf_op jit(solution)/shard_map/ppermute | solution.py:640
  38.2 1.8 %collective-permute-done.2.refs_2_ = f32[8,256]{1,0:T(8,128)S(1)} collective-permute-done((f32[8,256]{1,0:T(8,128)S(1)}, f32[8,256]{1,0:T(8,128)S(1)}, u32[]{:S(2)}, u32[]{:S(2)}) %collective-permute-start.2) | collective-permute-done | bytes 8224 | tf_op jit(solution)/shard_map/ppermute | solution.py:640
  40.0 0.5 %collective-permute-done.1.refs_1_ = f32[8,256]{1,0:T(8,128)S(1)} collective-permute-done((f32[8,256]{1,0:T(8,128)S(1)}, f32[8,256]{1,0:T(8,128)S(1)}, u32[]{:S(2)}, u32[]{:S(2)}) %collective-permute-start.1) | collective-permute-done | bytes 8224 | tf_op jit(solution)/shard_map/ppermute | solution.py:640
  40.5 0.0 all-to-all-done.1
  40.5 0.9 %unpack.1 = (bf16[256,512]{1,0:T(8,128)(2,1)}, f32[8,256]{1,0:T(8,128)}) custom-call(bf16[256,512]{1,0:T(8,128)(2,1)S(1)} %bitcast.5, f32[8,256]{1,0:T(8,128)S(1)} %pad_maximum_fusion.refs_0_, f32[8,256]{1,0:T(8,128)S(1)} %collective-permute-done.1.refs_1_, f32[8,256]{1,0:T(8,128)S(1)} %collective-permute-done.2.refs_2_, ...), custom_call_target="tpu_custom_call" | custom-call | tf_op jit(solution)/shard_map/unpack/pallas_call | solution.py:542
  (1 shorter events, 0.0 us)
Async XLA Ops:
  2.7 19.8 %copy-start = (f32[3,512]{1,0:T(4,128)S(1)}, f32[3,512]{1,0:T(4,128)}, u32[]{:S(2)}) copy-start(f32[3,512]{1,0:T(4,128)} %spectral_dirs.1) | copy-start | bytes 18436
  2.7 19.8 %all-to-all-start = ((bf16[32,4,1664]{2,1,0:T(4,128)(2,1)}), bf16[32,4,1664]{2,1,0:T(4,128)(2,1)S(1)}, u32[]{:S(2)}, u32[]{:S(2)}) async-start(bf16[32,4,1664]{2,1,0:T(4,128)(2,1)} %pack.1), calls=%async_computation | async-start | bytes 851968 | tf_op jit(solution)/shard_map/all_to_all | solution.py:603
  11.6 18.2 %copy-start.1 = (f32[3,2048]{1,0:T(4,128)S(1)}, f32[3,2048]{1,0:T(4,128)}, u32[]{:S(2)}) copy-start(f32[3,2048]{1,0:T(4,128)} %receiver_dirs.1) | copy-start | bytes 73732
  25.8 14.7 %all-to-all-start.1 = ((bf16[32,8,512]{2,1,0:T(8,128)(2,1)}), bf16[32,8,512]{2,1,0:T(8,128)(2,1)S(1)}, u32[]{:S(2)}, u32[]{:S(2)}) async-start(bf16[32,8,512]{2,1,0:T(8,128)(2,1)} %bitcast.2), calls=%async_computation.1 | async-start | bytes 524288 | tf_op jit(solution)/shard_map/all_to_all | solution.py:623
  32.4 1.2 %collective-permute-start = (f32[4,256]{1,0:T(4,128)S(1)}, f32[4,256]{1,0:T(4,128)S(1)}, u32[]{:S(2)}, u32[]{:S(2)}) collective-permute-start(f32[4,256]{1,0:T(4,128)S(1)} %get-tuple-element.19), channel_id=1, source_target_pairs={{0,4},{4,0},{8,12},{12,8},{16,20},{20,16},{24,28},{28,24},{1,5},{5... | collective-permute-start | bytes 12296 | tf_op jit(solution)/shard_map/ppermute | solution.py:640
  33.6 4.6 %collective-permute-start.3 = (f32[8,256]{1,0:T(8,128)S(1)}, f32[8,256]{1,0:T(8,128)S(1)}, u32[]{:S(2)}, u32[]{:S(2)}) collective-permute-start(f32[8,256]{1,0:T(8,128)S(1)} %pad_maximum_fusion.refs_0_), channel_id=1, source_target_pairs={{0,24},{4,28},{8,16},{12,20},{16,8},{20,12},{24,0},{28,4},{1,25},{... | collective-permute-start | bytes 24584 | tf_op jit(solution)/shard_map/ppermute | solution.py:640
  36.3 3.7 %collective-permute-start.2 = (f32[8,256]{1,0:T(8,128)S(1)}, f32[8,256]{1,0:T(8,128)S(1)}, u32[]{:S(2)}, u32[]{:S(2)}) collective-permute-start(f32[8,256]{1,0:T(8,128)S(1)} %pad_maximum_fusion.refs_0_), channel_id=1, source_target_pairs={{0,16},{4,20},{8,24},{12,28},{16,0},{20,4},{24,8},{28,12},{1,17},{... | collective-permute-start | bytes 24584 | tf_op jit(solution)/shard_map/ppermute | solution.py:640
  36.9 3.7 %collective-permute-start.1 = (f32[8,256]{1,0:T(8,128)S(1)}, f32[8,256]{1,0:T(8,128)S(1)}, u32[]{:S(2)}, u32[]{:S(2)}) collective-permute-start(f32[8,256]{1,0:T(8,128)S(1)} %pad_maximum_fusion.refs_0_), channel_id=1, source_target_pairs={{0,8},{4,12},{8,0},{12,4},{16,24},{20,28},{24,16},{28,20},{1,9},{5... | collective-permute-start | bytes 24584 | tf_op jit(solution)/shard_map/ppermute | solution.py:640

commit v7 on v6

--- a/solution.py
+++ b/solution.py
@@ -444,6 +444,8 @@
     other,
     image,
     far_rest,
+    cos_rest,
+    sin_rest,
     sems,
 ):
     head = far_head.shape[1]
@@ -456,12 +458,20 @@
     for t in range(splits):
         cut = slice(tile * t, tile * (t + 1))
         if tile * t == head:
+            for n in range(t, splits):
+                at = slice(tile * n, tile * (n + 1))
+                to = slice(tile * (n - t), tile * (n - t + 1))
+                cos_rest[:, to], sin_rest[:, to] = cos_sin(turns(centre, receiver_dirs[:, at]))
             rest_copy.wait()
         if tile * t < head:
             beams = dot(final[...], far_head[:, cut])
         else:
             beams = dot(final[...], far_rest[:, tile * t - head : tile * (t + 1) - head])
-        cos_view, sin_view = cos_sin(turns(centre, receiver_dirs[:, cut]))
+        if tile * t < head:
+            cos_view, sin_view = cos_sin(turns(centre, receiver_dirs[:, cut]))
+        else:
+            to = slice(tile * t - head, tile * (t + 1) - head)
+            cos_view, sin_view = cos_rest[:, to], sin_rest[:, to]
         beam_re = beams[:patches]
         beam_im = beams[patches:]
         far_re.append(jnp.sum(beam_re * cos_view - beam_im * sin_view, axis=0, keepdims=True))
@@ -631,6 +641,8 @@
         [
             pltpu.VMEM((n_px, tile), F32),
             pltpu.VMEM((depth, rcv_count - head), BF16),
+            pltpu.VMEM((patches, rcv_count - head), F32),
+            pltpu.VMEM((patches, rcv_count - head), F32),
             pltpu.SemaphoreType.DMA((1,)),
         ],
         cost=pl.CostEstimate(flops=2 * 10**9, bytes_accessed=4 * 10**6, transcendentals=0),

time: 41.8 us -> 41.6 us (level)
  no operation moved by 1% of the time
where the time goes in v7:
time: 41.6 us; the launch traced here: 41.3 us
  waiting for transfers between devices  15.2 us (37%)
  starting transfers between devices  15 us (36%)
  Pallas kernels  10.3 us (25%)
  between operations  0.71 us (2%)
    all_to_all x1, waiting for transfers between devices, illumination_sharded(): got = lax.all_to_all(packed, axes, 0, 0, tiled=True)  10.9 us
    pallas_call x5, Pallas kernels, call(): pl.pallas_call(kernel, out_shape=outs, in_specs=[pl.BlockSpec(memory_spac...  10.3 us
    all_to_all x1, starting transfers between devices, illumination_sharded(): got = lax.all_to_all(packed, axes, 0, 0, tiled=True)  7.3 us
    ppermute x4, waiting for transfers between devices, swapped(): return lax.ppermute(array, 'px', [(i, i ^ bits) for i in range(n_px)])  4.31 us
    all_to_all x1, starting transfers between devices, illumination_sharded(): lax.all_to_all(answer.reshape(devices, block, unit_count), axes, 0, 0, ti...  3.92 us
    ppermute x4, starting transfers between devices, swapped(): return lax.ppermute(array, 'px', [(i, i ^ bits) for i in range(n_px)])  3.8 us
  transfers between devices with their start and end apart: 6, of which 5 were waited for; matrix products, arithmetic and copies ran while one was open for 0% of the time, Pallas kernels for 10%

profile of v7, /device:TPU:0, one launch (start us, length us, event | category | flops | bytes accessed | tf_op | source)
XLA Modules:
  0.0 41.3 jit_solution(13087338831817869896)
XLA Ops:
  0.6 2.0 %pack.1 = bf16[32,4,1664]{2,1,0:T(4,128)(2,1)} custom-call(bf16[256,512]{1,0:T(8,128)(2,1)} %bitcast.6, f32[2,2,512]{2,1,0:T(2,128)} %reflect_hbm.1, bf16[2,2,12]{2,1,0:T(2,128)(2,1)} %weight_hbm.1, s32[2,2,12]{2,1,0:T(2,128)} %partners_hbm.1, s32[2,2]{1,0:T(2,128)} %count_hbm.1, f32[2,2,3]{2,1,0:T(2,128)} %bitcast.7), custom_call_target="tpu_custom_call" | custom-call | tf_op jit(solution)/shard_map/pack/pallas_call | solution.py:552
  2.7 0.0 copy-start
  2.7 7.3 %all-to-all-start = ((bf16[32,4,1664]{2,1,0:T(4,128)(2,1)}), bf16[32,4,1664]{2,1,0:T(4,128)(2,1)S(1)}, u32[]{:S(2)}, u32[]{:S(2)}) async-start(bf16[32,4,1664]{2,1,0:T(4,128)(2,1)} %pack.1), calls=%async_computation | async-start | bytes 851968 | tf_op jit(solution)/shard_map/all_to_all | solution.py:613
  10.0 1.6 %table.1 = (bf16[2,512,512]{2,1,0:T(8,128)(2,1)S(1)}, bf16[512,1024]{1,0:T(8,128)(2,1)S(1)}, bf16[256,512]{1,0:T(8,128)(2,1)S(1)}) custom-call(bf16[2,512,512]{2,1,0:T(8,128)(2,1)} %rad_hbm.1, bf16[512,2048]{1,0:T(8,128)(2,1)} %far_hbm.3), custom_call_target="tpu_custom_call" | custom-call | flops 10000000 | bytes 4000000 | tf_op jit(solution)/shard_map/table/pallas_call | solution.py:552
  11.6 0.0 copy-start.1
  11.6 10.9 %all-to-all-done.got = bf16[32,4,1664]{2,1,0:T(4,128)(2,1)S(1)} async-done(((bf16[32,4,1664]{2,1,0:T(4,128)(2,1)}), bf16[32,4,1664]{2,1,0:T(4,128)(2,1)S(1)}, u32[]{:S(2)}, u32[]{:S(2)}) %all-to-all-start) | async-done | bytes 426016 | tf_op jit(solution)/shard_map/all_to_all | solution.py:613
  22.5 0.0 copy-done
  22.5 3.4 %bounces.1 = (bf16[256,512]{1,0:T(8,128)(2,1)}, bf16[256,512]{1,0:T(8,128)(2,1)S(1)}, f32[128,128]{1,0:T(8,128)S(1)}) custom-call(bf16[32,4,1664]{2,1,0:T(4,128)(2,1)S(1)} %all-to-all-done.got, bf16[2,512,512]{2,1,0:T(8,128)(2,1)S(1)} %get-tuple-element.12.rad, f32[3,512]{1,0:T(4,128)S(1)} %copy-done, bf16[512,1024]{1,0:T(8,128)(2,1)S(1)} %get-tuple-element.13.far_head), custom_call_target="tpu_custom_call" | custom-call | tf_op jit(solution)/shard_map/bounces/pallas_call | solution.py:552
  25.8 3.9 %all-to-all-start.1 = ((bf16[32,8,512]{2,1,0:T(8,128)(2,1)}), bf16[32,8,512]{2,1,0:T(8,128)(2,1)S(1)}, u32[]{:S(2)}, u32[]{:S(2)}) async-start(bf16[32,8,512]{2,1,0:T(8,128)(2,1)} %bitcast.2), calls=%async_computation.1 | async-start | bytes 524288 | tf_op jit(solution)/shard_map/all_to_all | solution.py:633
  29.8 0.0 copy-done.1
  29.8 2.4 %image.1 = (f32[4,256]{1,0:T(4,128)S(1)}, f32[4,256]{1,0:T(4,128)S(1)}) custom-call(bf16[256,512]{1,0:T(8,128)(2,1)S(1)} %get-tuple-element.15.final, f32[128,128]{1,0:T(8,128)S(1)} %get-tuple-element.16.kept, bf16[256,512]{1,0:T(8,128)(2,1)S(1)} %get-tuple-element.17.long_table, f32[3,2048]{1,0:T(4,128)S(1)} %copy-done.1, ...), custom_call_target="tpu_custom_call" | custom-call | flops 2000000000 | bytes 4000000 | tf_op jit(solution)/shard_map/image/pallas_call | solution.py:552
  32.2 0.3 collective-permute-start
  32.5 0.9 %collective-permute-done = f32[4,256]{1,0:T(4,128)S(1)} collective-permute-done((f32[4,256]{1,0:T(4,128)S(1)}, f32[4,256]{1,0:T(4,128)S(1)}, u32[]{:S(2)}, u32[]{:S(2)}) %collective-permute-start) | collective-permute-done | bytes 4128 | tf_op jit(solution)/shard_map/ppermute | solution.py:652
  33.4 2.7 %collective-permute-start.3 = (f32[8,256]{1,0:T(8,128)S(1)}, f32[8,256]{1,0:T(8,128)S(1)}, u32[]{:S(2)}, u32[]{:S(2)}) collective-permute-start(f32[8,256]{1,0:T(8,128)S(1)} %pad_maximum_fusion.refs_0_), channel_id=1, source_target_pairs={{0,24},{4,28},{8,16},{12,20},{16,8},{20,12},{24,0},{28,4},{1,25},{... | collective-permute-start | bytes 24584 | tf_op jit(solution)/shard_map/ppermute | solution.py:652
  36.1 0.6 %collective-permute-start.2 = (f32[8,256]{1,0:T(8,128)S(1)}, f32[8,256]{1,0:T(8,128)S(1)}, u32[]{:S(2)}, u32[]{:S(2)}) collective-permute-start(f32[8,256]{1,0:T(8,128)S(1)} %pad_maximum_fusion.refs_0_), channel_id=1, source_target_pairs={{0,16},{4,20},{8,24},{12,28},{16,0},{20,4},{24,8},{28,12},{1,17},{... | collective-permute-start | bytes 24584 | tf_op jit(solution)/shard_map/ppermute | solution.py:652
  36.7 0.3 collective-permute-start.1
  36.9 1.1 %collective-permute-done.3.refs_3_ = f32[8,256]{1,0:T(8,128)S(1)} collective-permute-done((f32[8,256]{1,0:T(8,128)S(1)}, f32[8,256]{1,0:T(8,128)S(1)}, u32[]{:S(2)}, u32[]{:S(2)}) %collective-permute-start.3) | collective-permute-done | bytes 8224 | tf_op jit(solution)/shard_map/ppermute | solution.py:652
  38.0 1.7 %collective-permute-done.2.refs_2_ = f32[8,256]{1,0:T(8,128)S(1)} collective-permute-done((f32[8,256]{1,0:T(8,128)S(1)}, f32[8,256]{1,0:T(8,128)S(1)}, u32[]{:S(2)}, u32[]{:S(2)}) %collective-permute-start.2) | collective-permute-done | bytes 8224 | tf_op jit(solution)/shard_map/ppermute | solution.py:652
  39.8 0.5 %collective-permute-done.1.refs_1_ = f32[8,256]{1,0:T(8,128)S(1)} collective-permute-done((f32[8,256]{1,0:T(8,128)S(1)}, f32[8,256]{1,0:T(8,128)S(1)}, u32[]{:S(2)}, u32[]{:S(2)}) %collective-permute-start.1) | collective-permute-done | bytes 8224 | tf_op jit(solution)/shard_map/ppermute | solution.py:652
  40.3 0.0 all-to-all-done.1
  40.3 0.9 %unpack.1 = (bf16[256,512]{1,0:T(8,128)(2,1)}, f32[8,256]{1,0:T(8,128)}) custom-call(bf16[256,512]{1,0:T(8,128)(2,1)S(1)} %bitcast.5, f32[8,256]{1,0:T(8,128)S(1)} %pad_maximum_fusion.refs_0_, f32[8,256]{1,0:T(8,128)S(1)} %collective-permute-done.1.refs_1_, f32[8,256]{1,0:T(8,128)S(1)} %collective-permute-done.2.refs_2_, ...), custom_call_target="tpu_custom_call" | custom-call | tf_op jit(solution)/shard_map/unpack/pallas_call | solution.py:552
  (1 shorter events, 0.0 us)
Async XLA Ops:
  2.7 19.8 %copy-start = (f32[3,512]{1,0:T(4,128)S(1)}, f32[3,512]{1,0:T(4,128)}, u32[]{:S(2)}) copy-start(f32[3,512]{1,0:T(4,128)} %spectral_dirs.1) | copy-start | bytes 18436
  2.7 19.8 %all-to-all-start = ((bf16[32,4,1664]{2,1,0:T(4,128)(2,1)}), bf16[32,4,1664]{2,1,0:T(4,128)(2,1)S(1)}, u32[]{:S(2)}, u32[]{:S(2)}) async-start(bf16[32,4,1664]{2,1,0:T(4,128)(2,1)} %pack.1), calls=%async_computation | async-start | bytes 851968 | tf_op jit(solution)/shard_map/all_to_all | solution.py:613
  11.6 18.2 %copy-start.1 = (f32[3,2048]{1,0:T(4,128)S(1)}, f32[3,2048]{1,0:T(4,128)}, u32[]{:S(2)}) copy-start(f32[3,2048]{1,0:T(4,128)} %receiver_dirs.1) | copy-start | bytes 73732
  25.8 14.5 %all-to-all-start.1 = ((bf16[32,8,512]{2,1,0:T(8,128)(2,1)}), bf16[32,8,512]{2,1,0:T(8,128)(2,1)S(1)}, u32[]{:S(2)}, u32[]{:S(2)}) async-start(bf16[32,8,512]{2,1,0:T(8,128)(2,1)} %bitcast.2), calls=%async_computation.1 | async-start | bytes 524288 | tf_op jit(solution)/shard_map/all_to_all | solution.py:633
  32.2 1.2 %collective-permute-start = (f32[4,256]{1,0:T(4,128)S(1)}, f32[4,256]{1,0:T(4,128)S(1)}, u32[]{:S(2)}, u32[]{:S(2)}) collective-permute-start(f32[4,256]{1,0:T(4,128)S(1)} %get-tuple-element.19), channel_id=1, source_target_pairs={{0,4},{4,0},{8,12},{12,8},{16,20},{20,16},{24,28},{28,24},{1,5},{5... | collective-permute-start | bytes 12296 | tf_op jit(solution)/shard_map/ppermute | solution.py:652
  33.4 4.6 %collective-permute-start.3 = (f32[8,256]{1,0:T(8,128)S(1)}, f32[8,256]{1,0:T(8,128)S(1)}, u32[]{:S(2)}, u32[]{:S(2)}) collective-permute-start(f32[8,256]{1,0:T(8,128)S(1)} %pad_maximum_fusion.refs_0_), channel_id=1, source_target_pairs={{0,24},{4,28},{8,16},{12,20},{16,8},{20,12},{24,0},{28,4},{1,25},{... | collective-permute-start | bytes 24584 | tf_op jit(solution)/shard_map/ppermute | solution.py:652
  36.1 3.7 %collective-permute-start.2 = (f32[8,256]{1,0:T(8,128)S(1)}, f32[8,256]{1,0:T(8,128)S(1)}, u32[]{:S(2)}, u32[]{:S(2)}) collective-permute-start(f32[8,256]{1,0:T(8,128)S(1)} %pad_maximum_fusion.refs_0_), channel_id=1, source_target_pairs={{0,16},{4,20},{8,24},{12,28},{16,0},{20,4},{24,8},{28,12},{1,17},{... | collective-permute-start | bytes 24584 | tf_op jit(solution)/shard_map/ppermute | solution.py:652
  36.7 3.7 %collective-permute-start.1 = (f32[8,256]{1,0:T(8,128)S(1)}, f32[8,256]{1,0:T(8,128)S(1)}, u32[]{:S(2)}, u32[]{:S(2)}) collective-permute-start(f32[8,256]{1,0:T(8,128)S(1)} %pad_maximum_fusion.refs_0_), channel_id=1, source_target_pairs={{0,8},{4,12},{8,0},{12,4},{16,24},{20,28},{24,16},{28,20},{1,9},{5... | collective-permute-start | bytes 24584 | tf_op jit(solution)/shard_map/ppermute | solution.py:652

commit v8 on v7

--- a/solution.py
+++ b/solution.py
@@ -173,7 +173,7 @@
     make = np.polynomial.chebyshev.Chebyshev.fit
     power = np.polynomial.Polynomial
     sine_fit = make(grid, sine_over, 5).convert(kind=power).coef
-    cosine_fit = make(grid, cosine, 6).convert(kind=power).coef
+    cosine_fit = make(grid, cosine, 5).convert(kind=power).coef
     return [float(c) for c in sine_fit], [float(c) for c in cosine_fit]
 
 
@@ -319,7 +319,9 @@
         out[n, :, : 2 * unit_count] = both[local * n : local * (n + 1)].astype(BF16)
 
 
-def table_kernel(rad_hbm, far_hbm, rad, far_head, long_table, sems):
+def table_kernel(
+    local, grid_shape, rad_hbm, far_hbm, rad, far_head, long_table, to_blocks, to_rows, sems
+):
     head = far_hbm.at[:, : far_head.shape[1]]
     copies = fetch([(rad_hbm, rad), (head, far_head)], sems)
     tile = long_table.shape[0]
@@ -328,6 +330,12 @@
     cosine, sine = cos_sin(((row * column) % tile).astype(F32) * (1.0 / tile))
     long_table[:, :tile] = cosine.astype(BF16)
     long_table[:, tile:] = sine.astype(BF16)
+    rows = to_rows.shape[0]
+    n_px, n_py = grid_shape
+    to_blocks[...] = part_sorter(rows, local, True)
+    to_rows[...] = sorter(
+        rows, rows // (2 * local), local, outer_at=lambda o: swapped_digits(o, n_py, n_px)
+    )
     for copy in copies:
         copy.wait()
 
@@ -362,6 +370,7 @@
     got,
     rad,
     spectral_dirs,
+    to_blocks,
     far_head,
     out_hbm,
     final,
@@ -425,7 +434,7 @@
         current = jnp.concatenate(
             [start[:patches] + reflect * recv_re, start[patches:] + reflect * recv_im], axis=0
         ).astype(BF16)
-    out[...] = dot(part_sorter(rows, local, True), current).astype(BF16)
+    out[...] = dot(to_blocks[...], current).astype(BF16)
     out_copy = pltpu.make_async_copy(out, out_hbm, sems.at[0])
     out_copy.start()
     final[...] = jnp.concatenate(spectrum(current, rad), axis=0).astype(BF16)
@@ -521,14 +530,9 @@
         other[n : n + 1, :] = image[pl.ds(me ^ (2 * n + 1), 1), :]
 
 
-def unpack_kernel(local, grid_shape, got, *refs):
+def unpack_kernel(n_px, got, order, *refs):
     pairs, (currents, image) = refs[:-2], refs[-2:]
-    rows = currents.shape[0]
-    n_px, n_py = grid_shape
-    order = sorter(
-        rows, rows // (2 * local), local, outer_at=lambda o: swapped_digits(o, n_py, n_px)
-    )
-    currents[...] = dot(order, got[...]).astype(BF16)
+    currents[...] = dot(order[...], got[...]).astype(BF16)
     me = lax.axis_index("px")
     row = lax.broadcasted_iota(jnp.int32, image.shape, 0)
     whole = jnp.zeros(image.shape, F32)
@@ -612,10 +616,16 @@
     )
     got = lax.all_to_all(packed, axes, 0, 0, tiled=True)
     depth, head = far_map.shape[0], rcv_count // 2
-    rad, far_head, long_table = call(
-        table_kernel,
+    rad, far_head, long_table, to_blocks, to_rows = call(
+        functools.partial(table_kernel, local, (n_px, n_py)),
         "table",
-        (shape(*rad_pattern.shape), shape(depth, head), shape(tile, 2 * tile)),
+        (
+            shape(*rad_pattern.shape),
+            shape(depth, head),
+            shape(tile, 2 * tile),
+            shape(rows, rows),
+            shape(rows, rows),
+        ),
         (rad_pattern, far_map),
         [hbm] * 2,
         [pltpu.SemaphoreType.DMA((2,))],
@@ -625,8 +635,8 @@
         functools.partial(bounce_kernel, (n_px, n_py), (local_rows, local_cols)),
         "bounces",
         (shape(rows, unit_count), shape(rows, unit_count), shape(patches, 128, dtype=F32)),
-        (got, rad, spectral_dirs, far_head),
-        [vmem] * 3 + [pl.ANY],
+        (got, rad, spectral_dirs, to_blocks, far_head),
+        [vmem] * 4 + [pl.ANY],
         [pltpu.VMEM((rows, unit_count), BF16), pltpu.SemaphoreType.DMA((1,))],
         left=(0,),
     )
@@ -654,11 +664,11 @@
     pair = jnp.concatenate([same, swapped(other, 1)], axis=0)
     pairs = [pair] + [swapped(pair, bits) for bits in range(2, n_px, 2)]
     currents, image = call(
-        functools.partial(unpack_kernel, local, (n_px, n_py)),
+        functools.partial(unpack_kernel, n_px),
         "unpack",
         (shape(rows, unit_count), shape(illum_count // n_py, tile, dtype=F32)),
-        (back.reshape(rows, unit_count), *pairs),
-        [vmem] * (1 + len(pairs)),
+        (back.reshape(rows, unit_count), to_rows, *pairs),
+        [vmem] * (2 + len(pairs)),
     )
     return (currents.reshape(currents_in.shape), image)
 

time: 41.6 us -> 42.3 us (1.017)
  Pallas kernels: 10.3 us -> 11 us
    pallas_call x5, Pallas kernels: 10.3 us -> 11 us  [call(): pl.pallas_call(kernel, out_shape=outs, in_specs=[pl.BlockSpec(memory_spac...]
  transfers between devices with their start and end apart: 6 -> 6, of which waited for: 5 -> 5; matrix products, arithmetic and copies ran while one was open for 0% -> 0% of each run, Pallas kernels for 10% -> 11%
where the time goes in v8:
time: 42.3 us; the launch traced here: 42 us
  waiting for transfers between devices  15.2 us (36%)
  starting transfers between devices  15 us (35%)
  Pallas kernels  11 us (26%)
  between operations  0.71 us (2%)
    pallas_call x5, Pallas kernels, call(): pl.pallas_call(kernel, out_shape=outs, in_specs=[pl.BlockSpec(memory_spac...  11 us
    all_to_all x1, waiting for transfers between devices, illumination_sharded(): got = lax.all_to_all(packed, axes, 0, 0, tiled=True)  10.9 us
    all_to_all x1, starting transfers between devices, illumination_sharded(): got = lax.all_to_all(packed, axes, 0, 0, tiled=True)  7.3 us
    ppermute x4, waiting for transfers between devices, swapped(): return lax.ppermute(array, 'px', [(i, i ^ bits) for i in range(n_px)])  4.3 us
    all_to_all x1, starting transfers between devices, illumination_sharded(): lax.all_to_all(answer.reshape(devices, block, unit_count), axes, 0, 0, ti...  3.92 us
    ppermute x4, starting transfers between devices, swapped(): return lax.ppermute(array, 'px', [(i, i ^ bits) for i in range(n_px)])  3.81 us
  transfers between devices with their start and end apart: 6, of which 5 were waited for; matrix products, arithmetic and copies ran while one was open for 0% of the time, Pallas kernels for 11%

profile of v8, /device:TPU:0, one launch (start us, length us, event | category | flops | bytes accessed | tf_op | source)
XLA Modules:
  0.0 42.0 jit_solution(18009410275314996769)
XLA Ops:
  0.6 2.0 %pack.1 = bf16[32,4,1664]{2,1,0:T(4,128)(2,1)} custom-call(bf16[256,512]{1,0:T(8,128)(2,1)} %bitcast.6, f32[2,2,512]{2,1,0:T(2,128)} %reflect_hbm.1, bf16[2,2,12]{2,1,0:T(2,128)(2,1)} %weight_hbm.1, s32[2,2,12]{2,1,0:T(2,128)} %partners_hbm.1, s32[2,2]{1,0:T(2,128)} %count_hbm.1, f32[2,2,3]{2,1,0:T(2,128)} %bitcast.7), custom_call_target="tpu_custom_call" | custom-call | tf_op jit(solution)/shard_map/pack/pallas_call | solution.py:556
  2.7 0.0 copy-start
  2.7 7.3 %all-to-all-start = ((bf16[32,4,1664]{2,1,0:T(4,128)(2,1)}), bf16[32,4,1664]{2,1,0:T(4,128)(2,1)S(1)}, u32[]{:S(2)}, u32[]{:S(2)}) async-start(bf16[32,4,1664]{2,1,0:T(4,128)(2,1)} %pack.1), calls=%async_computation | async-start | bytes 851968 | tf_op jit(solution)/shard_map/all_to_all | solution.py:617
  10.0 1.6 %table.1 = (bf16[2,512,512]{2,1,0:T(8,128)(2,1)S(1)}, bf16[512,1024]{1,0:T(8,128)(2,1)S(1)}, bf16[256,512]{1,0:T(8,128)(2,1)S(1)}, bf16[256,256]{1,0:T(8,128)(2,1)S(1)}, bf16[256,256]{1,0:T(8,128)(2,1)S(1)}) custom-call(bf16[2,512,512]{2,1,0:T(8,128)(2,1)} %rad_hbm.1, bf16[512,2048]{1,0:T(8,128)(2,1)} %far_hbm.3), custom_call_target="tpu_custom_call" | custom-call | flops 10000000 | bytes 4000000 | tf_op jit(solution)/shard_map/table/pallas_call | solution.py:556
  11.6 0.0 copy-start.1
  11.6 10.9 %all-to-all-done.got = bf16[32,4,1664]{2,1,0:T(4,128)(2,1)S(1)} async-done(((bf16[32,4,1664]{2,1,0:T(4,128)(2,1)}), bf16[32,4,1664]{2,1,0:T(4,128)(2,1)S(1)}, u32[]{:S(2)}, u32[]{:S(2)}) %all-to-all-start) | async-done | bytes 426016 | tf_op jit(solution)/shard_map/all_to_all | solution.py:617
  22.5 0.0 copy-done
  22.5 3.4 %bounces.1 = (bf16[256,512]{1,0:T(8,128)(2,1)}, bf16[256,512]{1,0:T(8,128)(2,1)S(1)}, f32[128,128]{1,0:T(8,128)S(1)}) custom-call(bf16[32,4,1664]{2,1,0:T(4,128)(2,1)S(1)} %all-to-all-done.got, bf16[2,512,512]{2,1,0:T(8,128)(2,1)S(1)} %get-tuple-element.14.rad, f32[3,512]{1,0:T(4,128)S(1)} %copy-done, bf16[256,256]{1,0:T(8,128)(2,1)S(1)} %get-tuple-element.15.to_blocks, ...), custom_call_target="tpu_custom_call" | custom-call | tf_op jit(solution)/shard_map/bounces/pallas_call | solution.py:556
  25.8 3.9 %all-to-all-start.1 = ((bf16[32,8,512]{2,1,0:T(8,128)(2,1)}), bf16[32,8,512]{2,1,0:T(8,128)(2,1)S(1)}, u32[]{:S(2)}, u32[]{:S(2)}) async-start(bf16[32,8,512]{2,1,0:T(8,128)(2,1)} %bitcast.2), calls=%async_computation.1 | async-start | bytes 524288 | tf_op jit(solution)/shard_map/all_to_all | solution.py:643
  29.8 0.0 copy-done.1
  29.8 3.1 %image.1 = (f32[4,256]{1,0:T(4,128)S(1)}, f32[4,256]{1,0:T(4,128)S(1)}) custom-call(bf16[256,512]{1,0:T(8,128)(2,1)S(1)} %get-tuple-element.19.final, f32[128,128]{1,0:T(8,128)S(1)} %get-tuple-element.20.kept, bf16[256,512]{1,0:T(8,128)(2,1)S(1)} %get-tuple-element.21.long_table, f32[3,2048]{1,0:T(4,128)S(1)} %copy-done.1, ...), custom_call_target="tpu_custom_call" | custom-call | flops 2000000000 | bytes 4000000 | tf_op jit(solution)/shard_map/image/pallas_call | solution.py:556
  32.9 0.3 collective-permute-start
  33.2 0.9 %collective-permute-done = f32[4,256]{1,0:T(4,128)S(1)} collective-permute-done((f32[4,256]{1,0:T(4,128)S(1)}, f32[4,256]{1,0:T(4,128)S(1)}, u32[]{:S(2)}, u32[]{:S(2)}) %collective-permute-start) | collective-permute-done | bytes 4128 | tf_op jit(solution)/shard_map/ppermute | solution.py:662
  34.1 2.7 %collective-permute-start.3 = (f32[8,256]{1,0:T(8,128)S(1)}, f32[8,256]{1,0:T(8,128)S(1)}, u32[]{:S(2)}, u32[]{:S(2)}) collective-permute-start(f32[8,256]{1,0:T(8,128)S(1)} %pad_maximum_fusion.refs_0_), channel_id=1, source_target_pairs={{0,24},{4,28},{8,16},{12,20},{16,8},{20,12},{24,0},{28,4},{1,25},{... | collective-permute-start | bytes 24584 | tf_op jit(solution)/shard_map/ppermute | solution.py:662
  36.8 0.6 %collective-permute-start.2 = (f32[8,256]{1,0:T(8,128)S(1)}, f32[8,256]{1,0:T(8,128)S(1)}, u32[]{:S(2)}, u32[]{:S(2)}) collective-permute-start(f32[8,256]{1,0:T(8,128)S(1)} %pad_maximum_fusion.refs_0_), channel_id=1, source_target_pairs={{0,16},{4,20},{8,24},{12,28},{16,0},{20,4},{24,8},{28,12},{1,17},{... | collective-permute-start | bytes 24584 | tf_op jit(solution)/shard_map/ppermute | solution.py:662
  37.4 0.3 collective-permute-start.1
  37.6 1.1 %collective-permute-done.3.refs_3_ = f32[8,256]{1,0:T(8,128)S(1)} collective-permute-done((f32[8,256]{1,0:T(8,128)S(1)}, f32[8,256]{1,0:T(8,128)S(1)}, u32[]{:S(2)}, u32[]{:S(2)}) %collective-permute-start.3) | collective-permute-done | bytes 8224 | tf_op jit(solution)/shard_map/ppermute | solution.py:662
  38.7 1.8 %collective-permute-done.2.refs_2_ = f32[8,256]{1,0:T(8,128)S(1)} collective-permute-done((f32[8,256]{1,0:T(8,128)S(1)}, f32[8,256]{1,0:T(8,128)S(1)}, u32[]{:S(2)}, u32[]{:S(2)}) %collective-permute-start.2) | collective-permute-done | bytes 8224 | tf_op jit(solution)/shard_map/ppermute | solution.py:662
  40.4 0.6 %collective-permute-done.1.refs_1_ = f32[8,256]{1,0:T(8,128)S(1)} collective-permute-done((f32[8,256]{1,0:T(8,128)S(1)}, f32[8,256]{1,0:T(8,128)S(1)}, u32[]{:S(2)}, u32[]{:S(2)}) %collective-permute-start.1) | collective-permute-done | bytes 8224 | tf_op jit(solution)/shard_map/ppermute | solution.py:662
  41.0 0.0 all-to-all-done.1
  41.0 0.9 %unpack.1 = (bf16[256,512]{1,0:T(8,128)(2,1)}, f32[8,256]{1,0:T(8,128)}) custom-call(bf16[256,512]{1,0:T(8,128)(2,1)S(1)} %bitcast.5, bf16[256,256]{1,0:T(8,128)(2,1)S(1)} %get-tuple-element.18.order, f32[8,256]{1,0:T(8,128)S(1)} %pad_maximum_fusion.refs_0_, f32[8,256]{1,0:T(8,128)S(1)} %collective-permute-done.1.refs_1_, ...), custom_call_target="tpu_custom_call" | custom-call | tf_op jit(solution)/shard_map/unpack/pallas_call | solution.py:556
  (1 shorter events, 0.0 us)
Async XLA Ops:
  2.7 19.8 %copy-start = (f32[3,512]{1,0:T(4,128)S(1)}, f32[3,512]{1,0:T(4,128)}, u32[]{:S(2)}) copy-start(f32[3,512]{1,0:T(4,128)} %spectral_dirs.1) | copy-start | bytes 18436
  2.7 19.8 %all-to-all-start = ((bf16[32,4,1664]{2,1,0:T(4,128)(2,1)}), bf16[32,4,1664]{2,1,0:T(4,128)(2,1)S(1)}, u32[]{:S(2)}, u32[]{:S(2)}) async-start(bf16[32,4,1664]{2,1,0:T(4,128)(2,1)} %pack.1), calls=%async_computation | async-start | bytes 851968 | tf_op jit(solution)/shard_map/all_to_all | solution.py:617
  11.6 18.2 %copy-start.1 = (f32[3,2048]{1,0:T(4,128)S(1)}, f32[3,2048]{1,0:T(4,128)}, u32[]{:S(2)}) copy-start(f32[3,2048]{1,0:T(4,128)} %receiver_dirs.1) | copy-start | bytes 73732
  25.8 15.2 %all-to-all-start.1 = ((bf16[32,8,512]{2,1,0:T(8,128)(2,1)}), bf16[32,8,512]{2,1,0:T(8,128)(2,1)S(1)}, u32[]{:S(2)}, u32[]{:S(2)}) async-start(bf16[32,8,512]{2,1,0:T(8,128)(2,1)} %bitcast.2), calls=%async_computation.1 | async-start | bytes 524288 | tf_op jit(solution)/shard_map/all_to_all | solution.py:643
  32.9 1.2 %collective-permute-start = (f32[4,256]{1,0:T(4,128)S(1)}, f32[4,256]{1,0:T(4,128)S(1)}, u32[]{:S(2)}, u32[]{:S(2)}) collective-permute-start(f32[4,256]{1,0:T(4,128)S(1)} %get-tuple-element.23), channel_id=1, source_target_pairs={{0,4},{4,0},{8,12},{12,8},{16,20},{20,16},{24,28},{28,24},{1,5},{5... | collective-permute-start | bytes 12296 | tf_op jit(solution)/shard_map/ppermute | solution.py:662
  34.1 4.6 %collective-permute-start.3 = (f32[8,256]{1,0:T(8,128)S(1)}, f32[8,256]{1,0:T(8,128)S(1)}, u32[]{:S(2)}, u32[]{:S(2)}) collective-permute-start(f32[8,256]{1,0:T(8,128)S(1)} %pad_maximum_fusion.refs_0_), channel_id=1, source_target_pairs={{0,24},{4,28},{8,16},{12,20},{16,8},{20,12},{24,0},{28,4},{1,25},{... | collective-permute-start | bytes 24584 | tf_op jit(solution)/shard_map/ppermute | solution.py:662
  36.8 3.7 %collective-permute-start.2 = (f32[8,256]{1,0:T(8,128)S(1)}, f32[8,256]{1,0:T(8,128)S(1)}, u32[]{:S(2)}, u32[]{:S(2)}) collective-permute-start(f32[8,256]{1,0:T(8,128)S(1)} %pad_maximum_fusion.refs_0_), channel_id=1, source_target_pairs={{0,16},{4,20},{8,24},{12,28},{16,0},{20,4},{24,8},{28,12},{1,17},{... | collective-permute-start | bytes 24584 | tf_op jit(solution)/shard_map/ppermute | solution.py:662
  37.4 3.7 %collective-permute-start.1 = (f32[8,256]{1,0:T(8,128)S(1)}, f32[8,256]{1,0:T(8,128)S(1)}, u32[]{:S(2)}, u32[]{:S(2)}) collective-permute-start(f32[8,256]{1,0:T(8,128)S(1)} %pad_maximum_fusion.refs_0_), channel_id=1, source_target_pairs={{0,8},{4,12},{8,0},{12,4},{16,24},{20,28},{24,16},{28,20},{1,9},{5... | collective-permute-start | bytes 24584 | tf_op jit(solution)/shard_map/ppermute | solution.py:662
